TPU v7x, 32 devices: a whole 2x2x4 slice. The times are simulated.
32 devices in a mesh: pts: 32 (over z, y, x, core).
Axes of the slice: x: 2, y: 2, z: 4, core: 2. Of those that a mesh axis runs over, the one named last changes fastest.
Arguments:
- right_solved: float32 [64, 65536], P(None, 'pts'), may hold values from -6 to 6
- solved_basis_1: bfloat16 [128, 65536], P(None, 'pts'), may hold values from -0.5 to 0.5
- solved_basis_2: bfloat16 [128, 65536], P(None, 'pts'), may hold values from -0.5 to 0.5
- solved_basis_3: bfloat16 [128, 65536], P(None, 'pts'), may hold values from -0.5 to 0.5
- solved_basis_4: bfloat16 [128, 65536], P(None, 'pts'), may hold values from -0.5 to 0.5
- row_basis_1: bfloat16 [128, 65536], P(None, 'pts'), may hold values from -0.03125 to 0.03125
- row_basis_2: bfloat16 [128, 65536], P(None, 'pts'), may hold values from -0.046875 to 0.046875
- row_basis_3: bfloat16 [128, 65536], P(None, 'pts'), may hold values from -0.0625 to 0.0625
- row_basis_4: bfloat16 [128, 65536], P(None, 'pts'), may hold values from -0.09375 to 0.09375
- coupling_1: float32 [256, 256], P('pts'), may hold values from -0.375 to 0.375
- coupling_2: float32 [512, 256], P('pts'), may hold values from -0.375 to 0.375
- coupling_3: float32 [1024, 256], P('pts'), may hold values from -0.375 to 0.375
- coupling_4: float32 [2048, 256], P('pts'), may hold values from -0.375 to 0.375
Outputs:
- solution: float32 [64, 65536], P(None, 'pts')
All inputs are finite; a program needn't handle non-finite values.
Results may differ from a plain program's by a relative error of at most 0.0085.
Values may be sent and summed in bfloat16 or wider, within the bound.
No kernel may reach another device: no remote copies, remote signals or barrier semaphores. Data moves between devices by JAX's collectives and lax.ppermute only.
A program may use at most 64 MiB of HBM per device.

v0:
```python
import jax
import jax.numpy as jnp
from jax import lax
from jax.sharding import PartitionSpec as P


def from_partner(x, axis, bit):
    return lax.ppermute(x, axis, [(i, i ^ 1 << bit) for i in range(lax.axis_size(axis))])


def on_device(
    right_solved,
    solved_basis_1,
    solved_basis_2,
    solved_basis_3,
    solved_basis_4,
    row_basis_1,
    row_basis_2,
    row_basis_3,
    row_basis_4,
    coupling_1,
    coupling_2,
    coupling_3,
    coupling_4,
):
    solved_all = (solved_basis_1, solved_basis_2, solved_basis_3, solved_basis_4)
    basis_all = (row_basis_1, row_basis_2, row_basis_3, row_basis_4)
    coupling_all = (coupling_1, coupling_2, coupling_3, coupling_4)
    depth_bits = lax.axis_size("pts").bit_length() - 1
    my_index = lax.axis_index("pts")
    current = right_solved
    rank_width = solved_basis_1.shape[0]
    for level_num in (4, 3, 2, 1):
        solved = solved_all[level_num - 1]
        basis = basis_all[level_num - 1]
        coupling = coupling_all[level_num - 1]
        low_bit = depth_bits - level_num
        rounded = current.astype(jnp.bfloat16)
        projected = lax.dot_general(
            basis, rounded, (((1,), (1,)), ((), ())), preferred_element_type=jnp.float32
        )
        upper_bit = my_index >> low_bit & 1
        node_index = my_index >> low_bit + 1
        gathered = projected
        for bit_num in range(low_bit):
            gathered = gathered + from_partner(gathered, "pts", bit_num)
        partner = from_partner(gathered, "pts", low_bit)
        first_half = jnp.where(upper_bit == 1, partner, gathered)
        second_half = jnp.where(upper_bit == 1, gathered, partner)
        stacked = jnp.concatenate([first_half, second_half], axis=0)
        own_rows = jnp.dot(
            coupling, stacked, precision=lax.Precision.HIGHEST, preferred_element_type=jnp.float32
        ).astype(jnp.bfloat16)
        every_rows = lax.all_gather(own_rows, "pts", axis=0, tiled=True)
        block_rows = lax.dynamic_slice_in_dim(
            every_rows, node_index * 2 * rank_width, 2 * rank_width, 0
        )
        own_half = lax.dynamic_slice_in_dim(block_rows, upper_bit * rank_width, rank_width, 0)
        correction = lax.dot_general(
            own_half, solved, (((0,), (0,)), ((), ())), preferred_element_type=jnp.float32
        )
        current = current - correction
    return current


def solution(mesh):
    in_specs = (
        P(None, "pts"),
        P(None, "pts"),
        P(None, "pts"),
        P(None, "pts"),
        P(None, "pts"),
        P(None, "pts"),
        P(None, "pts"),
        P(None, "pts"),
        P(None, "pts"),
        P("pts", None),
        P("pts", None),
        P("pts", None),
        P("pts", None),
    )
    out_specs = P(None, "pts")
    return jax.shard_map(
        on_device, mesh=mesh, in_specs=in_specs, out_specs=out_specs, check_vma=False
    )
```

profile of v0, /device:TPU:0, one launch (start us, length us, event | category | flops | bytes accessed | tf_op | source)
XLA Modules:
  0.0 210.4 jit_solution(17300495716162911986)
XLA Ops:
  0.0 1.6 fusion.7
  1.6 0.5 collective-permute-start
  2.1 0.9 collective-permute-done
  3.0 2.8 %collective-permute-start.1 = (f32[128,64]{0,1:T(8,128)S(1)}, f32[128,64]{0,1:T(8,128)S(1)}, u32[]{:S(2)}, u32[]{:S(2)}) collective-permute-start(f32[128,64]{0,1:T(8,128)S(1)} %add.58), channel_id=1, source_target_pairs={{0,2},{1,3},{2,0},{3,1},{4,6},{5,7},{6,4},{7,5},{8,10},{9,11},{10,... | collective-permute-start | bytes 98312 | tf_op jit(solution)/shard_map/ppermute | solution.py:8
  5.8 1.9 collective-permute-done.1
  7.9 43.7 %all_gather.12 = bf16[2048,64]{1,0:T(8,128)(2,1)S(1)} all-gather(bf16[64,64]{1,0:T(8,128)(2,1)S(1)} %fusion), channel_id=1, replica_groups=mesh['pts'=32] {'pts'}, dimensions={0}, use_global_device_ids=true | all-gather | bytes 270336 | tf_op jit(solution)/shard_map/all_gather | solution.py:54
  51.9 0.8 copy-done.2
  52.7 0.3 convolution_bitcast_fusion.2
  53.0 0.4 collective-permute-start.2
  53.4 0.9 collective-permute-done.2
  54.3 3.9 %collective-permute-done.3 = f32[128,64]{0,1:T(8,128)S(1)} collective-permute-done((f32[128,64]{0,1:T(8,128)S(1)}, f32[128,64]{0,1:T(8,128)S(1)}, u32[]{:S(2)}, u32[]{:S(2)}) %collective-permute-start.3) | collective-permute-done | bytes 32800 | tf_op jit(solution)/shard_map/ppermute | solution.py:8
  58.3 3.9 %collective-permute-done.4 = f32[128,64]{0,1:T(8,128)S(1)} collective-permute-done((f32[128,64]{0,1:T(8,128)S(1)}, f32[128,64]{0,1:T(8,128)S(1)}, u32[]{:S(2)}, u32[]{:S(2)}) %collective-permute-start.4) | collective-permute-done | bytes 32800 | tf_op jit(solution)/shard_map/ppermute | solution.py:8
  62.4 37.0 %all_gather.13 = bf16[1024,64]{1,0:T(8,128)(2,1)S(1)} all-gather(bf16[32,64]{1,0:T(8,128)(2,1)S(1)} %fusion.1), channel_id=1, replica_groups=mesh['pts'=32] {'pts'}, dimensions={0}, use_global_device_ids=true | all-gather | bytes 135168 | tf_op jit(solution)/shard_map/all_gather | solution.py:54
  99.7 0.8 copy-done.4
  100.8 0.4 collective-permute-start.5
  101.2 0.9 collective-permute-done.5
  102.1 2.0 collective-permute-start.6
  104.0 1.9 collective-permute-done.6
  106.0 3.9 %collective-permute-done.7 = f32[128,64]{0,1:T(8,128)S(1)} collective-permute-done((f32[128,64]{0,1:T(8,128)S(1)}, f32[128,64]{0,1:T(8,128)S(1)}, u32[]{:S(2)}, u32[]{:S(2)}) %collective-permute-start.7) | collective-permute-done | bytes 32800 | tf_op jit(solution)/shard_map/ppermute | solution.py:8
  109.9 3.9 %collective-permute-done.8 = f32[128,64]{0,1:T(8,128)S(1)} collective-permute-done((f32[128,64]{0,1:T(8,128)S(1)}, f32[128,64]{0,1:T(8,128)S(1)}, u32[]{:S(2)}, u32[]{:S(2)}) %collective-permute-start.8) | collective-permute-done | bytes 32800 | tf_op jit(solution)/shard_map/ppermute | solution.py:8
  114.0 38.6 %all_gather.14 = bf16[512,64]{1,0:T(8,128)(2,1)S(1)} all-gather(bf16[16,64]{1,0:T(8,128)(2,1)S(1)} %fusion.2), channel_id=1, replica_groups=mesh['pts'=32] {'pts'}, dimensions={0}, use_global_device_ids=true | all-gather | bytes 67584 | tf_op jit(solution)/shard_map/all_gather | solution.py:54
  152.9 0.8 copy-done.6
  153.7 0.3 convolution_bitcast_fusion
  154.0 0.4 collective-permute-start.9
  154.4 0.9 collective-permute-done.9
  155.3 3.9 %collective-permute-done.10 = f32[128,64]{0,1:T(8,128)S(1)} collective-permute-done((f32[128,64]{0,1:T(8,128)S(1)}, f32[128,64]{0,1:T(8,128)S(1)}, u32[]{:S(2)}, u32[]{:S(2)}) %collective-permute-start.10) | collective-permute-done | bytes 32800 | tf_op jit(solution)/shard_map/ppermute | solution.py:8
  159.2 3.9 %collective-permute-done.11 = f32[128,64]{0,1:T(8,128)S(1)} collective-permute-done((f32[128,64]{0,1:T(8,128)S(1)}, f32[128,64]{0,1:T(8,128)S(1)}, u32[]{:S(2)}, u32[]{:S(2)}) %collective-permute-start.11) | collective-permute-done | bytes 32800 | tf_op jit(solution)/shard_map/ppermute | solution.py:8
  163.1 3.9 %collective-permute-done.12 = f32[128,64]{0,1:T(8,128)S(1)} collective-permute-done((f32[128,64]{0,1:T(8,128)S(1)}, f32[128,64]{0,1:T(8,128)S(1)}, u32[]{:S(2)}, u32[]{:S(2)}) %collective-permute-start.12) | collective-permute-done | bytes 32800 | tf_op jit(solution)/shard_map/ppermute | solution.py:8
  167.0 4.8 %collective-permute-done.13 = f32[128,64]{0,1:T(8,128)S(1)} collective-permute-done((f32[128,64]{0,1:T(8,128)S(1)}, f32[128,64]{0,1:T(8,128)S(1)}, u32[]{:S(2)}, u32[]{:S(2)}) %collective-permute-start.13) | collective-permute-done | bytes 32800 | tf_op jit(solution)/shard_map/ppermute | solution.py:8
  171.9 0.7 copy-done.11
  172.7 36.6 %all_gather.15 = bf16[256,64]{1,0:T(8,128)(2,1)S(1)} all-gather(bf16[8,64]{1,0:T(8,128)(2,1)S(1)} %fusion.3), channel_id=1, replica_groups=mesh['pts'=32] {'pts'}, dimensions={0}, use_global_device_ids=true | all-gather | bytes 33792 | tf_op jit(solution)/shard_map/all_gather | solution.py:54
  209.3 1.1 convolution_subtract_fusion
  (50 shorter events, 2.0 us)
Async XLA Ops:
  0.0 51.7 %copy-start = (bf16[128,2048]{1,0:T(8,128)(2,1)S(1)}, bf16[128,2048]{1,0:T(8,128)(2,1)}, u32[]{:S(2)}) copy-start(bf16[128,2048]{1,0:T(8,128)(2,1)} %param.17) | copy-start | bytes 1572868
  0.0 7.7 %copy-start.8 = (f32[64,256]{1,0:T(8,128)S(1)}, f32[64,256]{1,0:T(8,128)}, u32[]{:S(2)}) copy-start(f32[64,256]{1,0:T(8,128)} %param.25) | copy-start | bytes 196612
  1.6 50.1 %copy-start.1 = (f32[64,2048]{1,0:T(8,128)S(1)}, f32[64,2048]{1,0:T(8,128)}, u32[]{:S(2)}) copy-start(f32[64,2048]{1,0:T(8,128)} %param.13) | copy-start | bytes 1572868
  1.6 1.4 collective-permute-start
  3.0 4.7 %collective-permute-start.1 = (f32[128,64]{0,1:T(8,128)S(1)}, f32[128,64]{0,1:T(8,128)S(1)}, u32[]{:S(2)}, u32[]{:S(2)}) collective-permute-start(f32[128,64]{0,1:T(8,128)S(1)} %add.58), channel_id=1, source_target_pairs={{0,2},{1,3},{2,0},{3,1},{4,6},{5,7},{6,4},{7,5},{8,10},{9,11},{10,... | collective-permute-start | bytes 98312 | tf_op jit(solution)/shard_map/ppermute | solution.py:8
  51.7 1.0 copy-start.2
  52.7 9.5 %copy-start.9 = (f32[32,256]{1,0:T(8,128)S(1)}, f32[32,256]{1,0:T(8,128)}, u32[]{:S(2)}) copy-start(f32[32,256]{1,0:T(8,128)} %param.24) | copy-start | bytes 98308
  53.0 46.4 %copy-start.3 = (bf16[128,2048]{1,0:T(8,128)(2,1)S(1)}, bf16[128,2048]{1,0:T(8,128)(2,1)}, u32[]{:S(2)}) copy-start(bf16[128,2048]{1,0:T(8,128)(2,1)} %param.16) | copy-start | bytes 1572868
  53.0 1.3 collective-permute-start.2
  54.3 3.9 %collective-permute-start.3 = (f32[128,64]{0,1:T(8,128)S(1)}, f32[128,64]{0,1:T(8,128)S(1)}, u32[]{:S(2)}, u32[]{:S(2)}) collective-permute-start(f32[128,64]{0,1:T(8,128)S(1)} %add.61), channel_id=1, source_target_pairs={{0,2},{1,3},{2,0},{3,1},{4,6},{5,7},{6,4},{7,5},{8,10},{9,11},{10,... | collective-permute-start | bytes 98312 | tf_op jit(solution)/shard_map/ppermute | solution.py:8
  58.2 3.9 %collective-permute-start.4 = (f32[128,64]{0,1:T(8,128)S(1)}, f32[128,64]{0,1:T(8,128)S(1)}, u32[]{:S(2)}, u32[]{:S(2)}) collective-permute-start(f32[128,64]{0,1:T(8,128)S(1)} %add.62), channel_id=1, source_target_pairs={{0,4},{1,5},{2,6},{3,7},{4,0},{5,1},{6,2},{7,3},{8,12},{9,13},{10,... | collective-permute-start | bytes 98312 | tf_op jit(solution)/shard_map/ppermute | solution.py:8
  99.4 1.0 copy-start.4
  100.5 13.4 %copy-start.10 = (f32[16,256]{1,0:T(8,128)S(1)}, f32[16,256]{1,0:T(8,128)}, u32[]{:S(2)}) copy-start(f32[16,256]{1,0:T(8,128)} %param.23) | copy-start | bytes 49156
  100.8 51.9 %copy-start.5 = (bf16[128,2048]{1,0:T(8,128)(2,1)S(1)}, bf16[128,2048]{1,0:T(8,128)(2,1)}, u32[]{:S(2)}) copy-start(bf16[128,2048]{1,0:T(8,128)(2,1)} %param.15) | copy-start | bytes 1572868
  100.8 1.3 collective-permute-start.5
  102.1 3.9 %collective-permute-start.6 = (f32[128,64]{0,1:T(8,128)S(1)}, f32[128,64]{0,1:T(8,128)S(1)}, u32[]{:S(2)}, u32[]{:S(2)}) collective-permute-start(f32[128,64]{0,1:T(8,128)S(1)} %add.65), channel_id=1, source_target_pairs={{0,2},{1,3},{2,0},{3,1},{4,6},{5,7},{6,4},{7,5},{8,10},{9,11},{10,... | collective-permute-start | bytes 98312 | tf_op jit(solution)/shard_map/ppermute | solution.py:8
  106.0 3.9 %collective-permute-start.7 = (f32[128,64]{0,1:T(8,128)S(1)}, f32[128,64]{0,1:T(8,128)S(1)}, u32[]{:S(2)}, u32[]{:S(2)}) collective-permute-start(f32[128,64]{0,1:T(8,128)S(1)} %add.66), channel_id=1, source_target_pairs={{0,4},{1,5},{2,6},{3,7},{4,0},{5,1},{6,2},{7,3},{8,12},{9,13},{10,... | collective-permute-start | bytes 98312 | tf_op jit(solution)/shard_map/ppermute | solution.py:8
  109.9 3.9 %collective-permute-start.8 = (f32[128,64]{0,1:T(8,128)S(1)}, f32[128,64]{0,1:T(8,128)S(1)}, u32[]{:S(2)}, u32[]{:S(2)}) collective-permute-start(f32[128,64]{0,1:T(8,128)S(1)} %add.67), channel_id=1, source_target_pairs={{0,8},{1,9},{2,10},{3,11},{4,12},{5,13},{6,14},{7,15},{8,0},{9,1},... | collective-permute-start | bytes 98312 | tf_op jit(solution)/shard_map/ppermute | solution.py:8
  152.6 1.0 copy-start.6
  154.0 55.4 %copy-start.7 = (bf16[128,2048]{1,0:T(8,128)(2,1)S(1)}, bf16[128,2048]{1,0:T(8,128)(2,1)}, u32[]{:S(2)}) copy-start(bf16[128,2048]{1,0:T(8,128)(2,1)} %param.14) | copy-start | bytes 1572868
  154.0 1.3 collective-permute-start.9
  155.3 3.9 %collective-permute-start.10 = (f32[128,64]{0,1:T(8,128)S(1)}, f32[128,64]{0,1:T(8,128)S(1)}, u32[]{:S(2)}, u32[]{:S(2)}) collective-permute-start(f32[128,64]{0,1:T(8,128)S(1)} %add.70), channel_id=1, source_target_pairs={{0,2},{1,3},{2,0},{3,1},{4,6},{5,7},{6,4},{7,5},{8,10},{9,11},{10,... | collective-permute-start | bytes 98312 | tf_op jit(solution)/shard_map/ppermute | solution.py:8
  159.2 3.9 %collective-permute-start.11 = (f32[128,64]{0,1:T(8,128)S(1)}, f32[128,64]{0,1:T(8,128)S(1)}, u32[]{:S(2)}, u32[]{:S(2)}) collective-permute-start(f32[128,64]{0,1:T(8,128)S(1)} %add.71), channel_id=1, source_target_pairs={{0,4},{1,5},{2,6},{3,7},{4,0},{5,1},{6,2},{7,3},{8,12},{9,13},{10,... | collective-permute-start | bytes 98312 | tf_op jit(solution)/shard_map/ppermute | solution.py:8
  163.1 3.9 %collective-permute-start.12 = (f32[128,64]{0,1:T(8,128)S(1)}, f32[128,64]{0,1:T(8,128)S(1)}, u32[]{:S(2)}, u32[]{:S(2)}) collective-permute-start(f32[128,64]{0,1:T(8,128)S(1)} %add.72), channel_id=1, source_target_pairs={{0,8},{1,9},{2,10},{3,11},{4,12},{5,13},{6,14},{7,15},{8,0},{9,1},... | collective-permute-start | bytes 98312 | tf_op jit(solution)/shard_map/ppermute | solution.py:8
  167.0 4.8 %collective-permute-start.13 = (f32[128,64]{0,1:T(8,128)S(1)}, f32[128,64]{0,1:T(8,128)S(1)}, u32[]{:S(2)}, u32[]{:S(2)}) collective-permute-start(f32[128,64]{0,1:T(8,128)S(1)} %add.73), channel_id=1, source_target_pairs={{0,16},{1,17},{2,18},{3,19},{4,20},{5,21},{6,22},{7,23},{8,24},{9,... | collective-permute-start | bytes 98312 | tf_op jit(solution)/shard_map/ppermute | solution.py:8
  171.9 0.7 copy-start.11
where the time goes:
time: 211 us; the launch traced here: 210 us
  blocking collectives  156 us (74%)
  waiting for transfers between devices  39.4 us (19%)
  starting transfers between devices  6.63 us (3%)
  matrix products  5 us (2%)
  local copies, waits for them, and re-layouts  3.04 us (1%)
    all_gather x4, blocking collectives, on_device(): every_rows = lax.all_gather(own_rows, 'pts', axis=0, tiled=True)  156 us
    ppermute x14, waiting for transfers between devices, from_partner(): lax.ppermute(x, axis, [(i, i ^ 1 << bit) for i in range(lax.axis_size(axi...  39.4 us
    ppermute x14, starting transfers between devices, from_partner(): lax.ppermute(x, axis, [(i, i ^ 1 << bit) for i in range(lax.axis_size(axi...  6.63 us
  transfers between devices with their start and end apart: 14, of which 14 were waited for; matrix products, arithmetic and copies ran while one was open for 0% of the time, Pallas kernels for 0%

commit v1 on v0

v1 whole, which is shorter than its diff:
```python
import jax
import jax.numpy as jnp
from jax import lax
from jax.sharding import PartitionSpec as P

BF = jnp.bfloat16
F32 = jnp.float32
LEVELS = (4, 3, 2, 1)


def nn(a, b):
    return lax.dot_general(a, b, (((1,), (0,)), ((), ())), preferred_element_type=F32)


def nt(a, b):
    return lax.dot_general(a, b, (((1,), (1,)), ((), ())), preferred_element_type=F32)


def exchange(parts, bit):
    size = lax.axis_size("pts")
    sent = jnp.concatenate(parts, axis=0)
    got = lax.ppermute(sent, "pts", [(i, i ^ (1 << bit)) for i in range(size)])
    out, start = [], 0
    for part in parts:
        out.append(got[start : start + part.shape[0]])
        start += part.shape[0]
    return out


def on_device(right_solved, s1, s2, s3, s4, r1, r2, r3, r4, c1, c2, c3, c4):
    solved = {1: s1, 2: s2, 3: s3, 4: s4}
    basis = {1: r1, 2: r2, 3: r3, 4: r4}
    rank = s1.shape[0]
    size = lax.axis_size("pts")
    bits = size.bit_length() - 1
    me = lax.axis_index("pts")

    rounded = right_solved.astype(BF)
    proj = {l: nt(rounded, basis[l]) for l in LEVELS}
    gram = {(l, k): nt(solved[l], basis[k]).astype(BF) for l in LEVELS for k in LEVELS if k < l}
    coup = {
        l: (c[:, :rank].astype(BF), c[:, rank:].astype(BF))
        for l, c in ((1, c1), (2, c2), (3, c3), (4, c4))
    }

    current = right_solved
    for bit in range(bits):
        level = bits - bit
        upper = (me >> bit & 1) == 1
        live = [k for k in LEVELS if k <= level]
        pairs = [lk for lk in gram if lk[0] <= level]
        rows_of = [k for k in live if not (level == 1 and k == 1)]
        parts = [proj[k].astype(BF) for k in live]
        parts += [gram[lk] for lk in pairs]
        for k in rows_of:
            parts += list(coup[k])
        got = exchange(parts, bit)
        their_proj = dict(zip(live, got[: len(live)]))
        their_gram = dict(zip(pairs, got[len(live) : len(live) + len(pairs)]))
        rest = got[len(live) + len(pairs) :]
        for i, k in enumerate(rows_of):
            coup[k] = tuple(
                jnp.where(
                    upper,
                    jnp.concatenate([rest[2 * i + h], coup[k][h]], axis=0),
                    jnp.concatenate([coup[k][h], rest[2 * i + h]], axis=0),
                )
                for h in range(2)
            )
        if level in LEVELS:
            own, other = proj[level].astype(BF), their_proj[level]
            left = jnp.where(upper, other, own)
            right = jnp.where(upper, own, other)
            weights = (nt(left, coup[level][0]) + nt(right, coup[level][1])).astype(BF)
            if level == 1:
                mine = weights
            else:
                mine = jnp.where(upper, weights[:, rank:], weights[:, :rank])
                theirs = jnp.where(upper, weights[:, :rank], weights[:, rank:])
            for k in live[1:]:
                proj[k] = (
                    proj[k]
                    + their_proj[k].astype(F32)
                    - nn(mine, gram[level, k])
                    - nn(theirs, their_gram[level, k])
                )
            current = current - nn(mine, solved[level])
        else:
            for k in live:
                proj[k] = proj[k] + their_proj[k].astype(F32)
        for lk in pairs:
            if lk[0] < level:
                gram[lk] = (gram[lk].astype(F32) + their_gram[lk].astype(F32)).astype(BF)
    return current


def solution(mesh):
    wide, tall = P(None, "pts"), P("pts", None)
    return jax.shard_map(
        on_device, mesh=mesh, in_specs=(wide,) * 9 + (tall,) * 4, out_specs=wide, check_vma=False
    )
```

time: 211 us -> 57.6 us (0.27)
  blocking collectives: 156 us -> 0 us
  waiting for transfers between devices: 39.4 us -> 22 us
  other arithmetic: 0.08 us -> 12.6 us
  starting transfers between devices: 6.63 us -> 9.32 us
  matrix products: 5 us -> 7.66 us
  local copies, waits for them, and re-layouts: 3.04 us -> 5.29 us
    all_gather x4 -> x0, blocking collectives: 156 us -> none  [on_device(): every_rows = lax.all_gather(own_rows, 'pts', axis=0, tiled=True)]
    ppermute x14 -> x5, waiting for transfers between devices: 39.4 us -> 22 us  [exchange(): got = lax.ppermute(sent, 'pts', [(i, i ^ 1 << bit) for i in range(size)])]
    unnamed x0 -> x28, other arithmetic: none -> 10.2 us
    ppermute x14 -> x5, starting transfers between devices: 6.63 us -> 9.32 us  [exchange(): got = lax.ppermute(sent, 'pts', [(i, i ^ 1 << bit) for i in range(size)])]
    dot_general x12 -> x33, matrix products: 5 us -> 7.66 us  [the longest x17 4.13 us: nt(): lax.dot_general(a, b, (((1,), (1,)), ((), ())), preferred_element_type=F32)]
    unnamed x24 -> x29, local copies, waits for them, and re-layouts: 3.04 us -> 5.19 us
  transfers between devices with their start and end apart: 14 -> 5, of which waited for: 14 -> 5; matrix products, arithmetic and copies ran while one was open for 0% -> 1% of each run, Pallas kernels for 0% -> 0%
where the time goes in v1:
time: 57.6 us; the launch traced here: 57.2 us
  waiting for transfers between devices  22 us (38%)
  other arithmetic  12.6 us (22%)
  starting transfers between devices  9.32 us (16%)
  matrix products  7.66 us (13%)
  local copies, waits for them, and re-layouts  5.29 us (9%)
    ppermute x5, waiting for transfers between devices, exchange(): got = lax.ppermute(sent, 'pts', [(i, i ^ 1 << bit) for i in range(size)])  22 us
    unnamed x28, other arithmetic  10.2 us
    ppermute x5, starting transfers between devices, exchange(): got = lax.ppermute(sent, 'pts', [(i, i ^ 1 << bit) for i in range(size)])  9.32 us
    unnamed x29, local copies, waits for them, and re-layouts  5.19 us
    dot_general x17, matrix products, nt(): lax.dot_general(a, b, (((1,), (1,)), ((), ())), preferred_element_type=F32)  4.13 us
    dot_general x16, matrix products, nn(): lax.dot_general(a, b, (((1,), (0,)), ((), ())), preferred_element_type=F32)  3.53 us
    convert_element_type x1, other arithmetic, on_device(): rounded = right_solved.astype(BF)  1.16 us
  transfers between devices with their start and end apart: 5, of which 5 were waited for; matrix products, arithmetic and copies ran while one was open for 1% of the time, Pallas kernels for 0%

profile of v1, /device:TPU:0, one launch (start us, length us, event | category | flops | bytes accessed | tf_op | source)
XLA Modules:
  0.0 57.2 jit_solution(11016245020547733451)
XLA Ops:
  0.0 1.2 %convert_element_type.207 = bf16[64,2048]{1,0:T(8,128)(2,1)S(1)} convert(f32[64,2048]{1,0:T(8,128)} %param.13) | non-fusion elementwise | flops 131072 | bytes 786432 | tf_op jit(solution)/shard_map/convert_element_type | solution.py:38
  1.6 0.7 %copy-done.5 = bf16[128,2048]{1,0:T(8,128)(2,1)S(1)} copy-done((bf16[128,2048]{1,0:T(8,128)(2,1)S(1)}, bf16[128,2048]{1,0:T(8,128)(2,1)}, u32[]{:S(2)}) %copy-start.5) | copy-done | bytes 524312
  3.3 0.7 %copy-done.1 = bf16[128,2048]{1,0:T(8,128)(2,1)S(1)} copy-done((bf16[128,2048]{1,0:T(8,128)(2,1)S(1)}, bf16[128,2048]{1,0:T(8,128)(2,1)}, u32[]{:S(2)}) %copy-start.1) | copy-done | bytes 524312
  5.0 0.7 %copy-done.2 = bf16[128,2048]{1,0:T(8,128)(2,1)S(1)} copy-done((bf16[128,2048]{1,0:T(8,128)(2,1)S(1)}, bf16[128,2048]{1,0:T(8,128)(2,1)}, u32[]{:S(2)}) %copy-start.2) | copy-done | bytes 524312
  7.5 0.7 %copy-done.10 = f32[32,256]{1,0:T(8,128)S(1)} copy-done((f32[32,256]{1,0:T(8,128)S(1)}, f32[32,256]{1,0:T(8,128)}, u32[]{:S(2)}) %copy-start.10) | copy-done | bytes 32792
  8.2 0.7 %copy-done.11 = f32[16,256]{1,0:T(8,128)S(1)} copy-done((f32[16,256]{1,0:T(8,128)S(1)}, f32[16,256]{1,0:T(8,128)}, u32[]{:S(2)}) %copy-start.11) | copy-done | bytes 16408
  9.0 0.7 %copy-done.12 = f32[8,256]{1,0:T(8,128)S(1)} copy-done((f32[8,256]{1,0:T(8,128)S(1)}, f32[8,256]{1,0:T(8,128)}, u32[]{:S(2)}) %copy-start.12) | copy-done | bytes 8216
  10.2 1.2 %collective-permute-done = bf16[1264,128]{1,0:T(8,128)(2,1)S(1)} collective-permute-done((bf16[1264,128]{1,0:T(8,128)(2,1)S(1)}, bf16[1264,128]{1,0:T(8,128)(2,1)S(1)}, u32[]{:S(2)}, u32[]{:S(2)}) %collective-permute-start) | collective-permute-done | bytes 323616 | tf_op jit(solution)/shard_map/ppermute | solution.py:22
  11.4 0.6 %constant_dynamic-update-slice_fusion.35 = (bf16[1504,128]{1,0:T(8,128)(2,1)}, bf16[64,128]{1,0:T(8,128)(2,1)S(1)}) fusion(f32[64,128]{1,0:T(8,128)S(1)} %get-tuple-element.95, bf16[1264,128]{1,0:T(8,128)(2,1)S(1)} %collective-permute-done), kind=kLoop, calls=%fused_computation.53 | loop fusion | flops 24575 | bytes 81920
  12.0 0.6 %constant_dynamic-update-slice_fusion.34 = bf16[1504,128]{1,0:T(8,128)(2,1)} fusion(bf16[1504,128]{1,0:T(8,128)(2,1)} %get-tuple-element.49, f32[64,128]{1,0:T(8,128)S(1)} %get-tuple-element.97, bf16[1264,128]{1,0:T(8,128)(2,1)S(1)} %collective-permute-done), kind=kLoop, calls=%fused_computation.52 | loop fusion | flops 24576 | bytes 65536
  12.7 0.6 %constant_dynamic-update-slice_fusion.33 = bf16[1504,128]{1,0:T(8,128)(2,1)} fusion(bf16[1504,128]{1,0:T(8,128)(2,1)} %constant_dynamic-update-slice_fusion.34, f32[64,128]{1,0:T(8,128)S(1)} %get-tuple-element.99, bf16[1264,128]{1,0:T(8,128)(2,1)S(1)} %collective-permute-done), kind=kLoop, calls=%fused_computation.51 | loop fusion | flops 24576 | bytes 65536
  13.3 0.6 %fusion.135 = (bf16[64,128]{1,0:T(8,128)(2,1)S(1)}, bf16[64,128]{1,0:T(8,128)(2,1)S(1)}, bf16[1504,128]{1,0:T(8,128)(2,1)}) fusion(bf16[1264,128]{1,0:T(8,128)(2,1)S(1)} %collective-permute-done, bf16[1504,128]{1,0:T(8,128)(2,1)} %constant_dynamic-update-slice_fusion.33, f32[64,128]{1,0:T(8,128)S(1)} %get-tuple-element.101), kind=kLoop, calls=%fused_computation.238 | loop fusion | flops 24576 | bytes 131072 | tf_op jit(solution)/shard_map/slice | solution.py:25
  13.9 0.6 %constant_dynamic-update-slice_fusion.31 = bf16[1504,128]{1,0:T(8,128)(2,1)} fusion(bf16[1504,128]{1,0:T(8,128)(2,1)} %get-tuple-element.69, bf16[1264,128]{1,0:T(8,128)(2,1)S(1)} %collective-permute-done, bf16[128,128]{1,0:T(8,128)(2,1)S(1)} %get-tuple-element.103), kind=kLoop, calls=%fused_computation.49 | loop fusion | flops 65536 | bytes 98304
  14.5 0.6 %constant_dynamic-update-slice_fusion.30 = bf16[1504,128]{1,0:T(8,128)(2,1)} fusion(bf16[1504,128]{1,0:T(8,128)(2,1)} %constant_dynamic-update-slice_fusion.31, bf16[1264,128]{1,0:T(8,128)(2,1)S(1)} %collective-permute-done, bf16[128,128]{1,0:T(8,128)(2,1)S(1)} %get-tuple-element.105), kind=kLoop, calls=%fused_computation.48 | loop fusion | flops 65536 | bytes 98304
  15.1 0.6 %constant_dynamic-update-slice_fusion.29 = bf16[1504,128]{1,0:T(8,128)(2,1)} fusion(bf16[1504,128]{1,0:T(8,128)(2,1)} %constant_dynamic-update-slice_fusion.30, bf16[1264,128]{1,0:T(8,128)(2,1)S(1)} %collective-permute-done, bf16[128,128]{1,0:T(8,128)(2,1)S(1)} %get-tuple-element.107), kind=kLoop, calls=%fused_computation.47 | loop fusion | flops 65536 | bytes 98304
  15.8 0.6 %constant_dynamic-update-slice_fusion.28 = bf16[1504,128]{1,0:T(8,128)(2,1)} fusion(bf16[1504,128]{1,0:T(8,128)(2,1)} %constant_dynamic-update-slice_fusion.29, bf16[1264,128]{1,0:T(8,128)(2,1)S(1)} %collective-permute-done, bf16[128,128]{1,0:T(8,128)(2,1)S(1)} %get-tuple-element.109), kind=kLoop, calls=%fused_computation.46 | loop fusion | flops 65536 | bytes 98304
  16.4 0.6 %constant_dynamic-update-slice_fusion.27 = bf16[1504,128]{1,0:T(8,128)(2,1)} fusion(bf16[1504,128]{1,0:T(8,128)(2,1)} %constant_dynamic-update-slice_fusion.28, bf16[1264,128]{1,0:T(8,128)(2,1)S(1)} %collective-permute-done, bf16[128,128]{1,0:T(8,128)(2,1)S(1)} %get-tuple-element.111), kind=kLoop, calls=%fused_computation.45 | loop fusion | flops 65536 | bytes 98304
  17.0 0.6 %constant_dynamic-update-slice_fusion.26 = bf16[1504,128]{1,0:T(8,128)(2,1)} fusion(bf16[1504,128]{1,0:T(8,128)(2,1)} %constant_dynamic-update-slice_fusion.27, bf16[1264,128]{1,0:T(8,128)(2,1)S(1)} %collective-permute-done, bf16[128,128]{1,0:T(8,128)(2,1)S(1)} %get-tuple-element.113), kind=kLoop, calls=%fused_computation.44 | loop fusion | flops 65536 | bytes 98304
  17.6 0.6 %constant_dynamic-update-slice_fusion.25 = (bf16[1504,128]{1,0:T(8,128)(2,1)}, bf16[128,128]{1,0:T(8,128)(2,1)S(1)}) fusion(bf16[1504,128]{1,0:T(8,128)(2,1)} %constant_dynamic-update-slice_fusion.26, bf16[64,128]{1,0:T(8,128)(2,1)S(1)} %get-tuple-element.68, bf16[64,128]{1,0:T(8,128)(2,1)S(1)} %get-tuple-element.84, pred[]{:T(512)S(6)} %eq.16), kind=kLoop, calls=%fused_computation.43 | loop fusion | flops 147456 | bytes 98305
  18.3 0.6 %constant_dynamic-update-slice_fusion.24 = (bf16[1504,128]{1,0:T(8,128)(2,1)}, bf16[128,128]{1,0:T(8,128)(2,1)S(1)}) fusion(bf16[1504,128]{1,0:T(8,128)(2,1)} %get-tuple-element.47, bf16[64,128]{1,0:T(8,128)(2,1)S(1)} %get-tuple-element.67, bf16[64,128]{1,0:T(8,128)(2,1)S(1)} %get-tuple-element.82, pred[]{:T(512)S(6)} %eq.16), kind=kLoop, calls=%fused_computation.42 | loop fusion | flops 147456 | bytes 98305
  18.9 0.6 %constant_dynamic-update-slice_fusion.23 = (bf16[1504,128]{1,0:T(8,128)(2,1)}, bf16[64,128]{1,0:T(8,128)(2,1)S(1)}) fusion(bf16[1504,128]{1,0:T(8,128)(2,1)} %get-tuple-element.45, bf16[32,128]{1,0:T(8,128)(2,1)S(1)} %get-tuple-element.66, bf16[32,128]{1,0:T(8,128)(2,1)S(1)} %get-tuple-element.87, pred[]{:T(512)S(6)} %eq.16), kind=kLoop, calls=%fused_computation.41 | loop fusion | flops 73728 | bytes 49153
  19.5 0.6 %constant_dynamic-update-slice_fusion.22 = (bf16[1504,128]{1,0:T(8,128)(2,1)}, bf16[64,128]{1,0:T(8,128)(2,1)S(1)}) fusion(bf16[1504,128]{1,0:T(8,128)(2,1)} %get-tuple-element.43, bf16[32,128]{1,0:T(8,128)(2,1)S(1)} %get-tuple-element.65, bf16[32,128]{1,0:T(8,128)(2,1)S(1)} %get-tuple-element.85, pred[]{:T(512)S(6)} %eq.16), kind=kLoop, calls=%fused_computation.40 | loop fusion | flops 73728 | bytes 49153
  20.1 0.6 %constant_dynamic-update-slice_fusion.21 = (bf16[1504,128]{1,0:T(8,128)(2,1)}, bf16[32,128]{1,0:T(8,128)(2,1)S(1)}) fusion(bf16[1504,128]{1,0:T(8,128)(2,1)} %get-tuple-element.41, bf16[16,128]{1,0:T(8,128)(2,1)S(1)} %get-tuple-element.64, bf16[16,128]{1,0:T(8,128)(2,1)S(1)} %get-tuple-element.90, pred[]{:T(512)S(6)} %eq.16), kind=kLoop, calls=%fused_computation.39 | loop fusion | flops 36864 | bytes 24577
  22.5 2.9 %collective-permute-start.1 = (bf16[1504,128]{1,0:T(8,128)(2,1)}, bf16[1504,128]{1,0:T(8,128)(2,1)S(1)}, u32[]{:S(2)}, u32[]{:S(2)}) collective-permute-start(bf16[1504,128]{1,0:T(8,128)(2,1)} %get-tuple-element.33), channel_id=1, source_target_pairs={{0,2},{1,3},{2,0},{3,1},{4,6},{5,7},{6,4},{7,5},{8,10},{9,11},{10,... | collective-permute-start | bytes 1155080 | tf_op jit(solution)/shard_map/ppermute | solution.py:22
  25.4 9.4 %collective-permute-done.1 = bf16[1504,128]{1,0:T(8,128)(2,1)S(1)} collective-permute-done((bf16[1504,128]{1,0:T(8,128)(2,1)}, bf16[1504,128]{1,0:T(8,128)(2,1)S(1)}, u32[]{:S(2)}, u32[]{:S(2)}) %collective-permute-start.1) | collective-permute-done | bytes 385056 | tf_op jit(solution)/shard_map/ppermute | solution.py:22
  36.3 1.8 %collective-permute-start.2 = (bf16[1024,128]{1,0:T(8,128)(2,1)S(1)}, bf16[1024,128]{1,0:T(8,128)(2,1)S(1)}, u32[]{:S(2)}, u32[]{:S(2)}) collective-permute-start(bf16[1024,128]{1,0:T(8,128)(2,1)S(1)} %get-tuple-element.13), channel_id=1, source_target_pairs={{0,4},{1,5},{2,6},{3,7},{4,0},{5,1},{6,2},{7,3},{8,12},{9,13},{10,... | collective-permute-start | bytes 786440 | tf_op jit(solution)/shard_map/ppermute | solution.py:22
  38.4 5.8 %collective-permute-done.2 = bf16[1024,128]{1,0:T(8,128)(2,1)S(1)} collective-permute-done((bf16[1024,128]{1,0:T(8,128)(2,1)S(1)}, bf16[1024,128]{1,0:T(8,128)(2,1)S(1)}, u32[]{:S(2)}, u32[]{:S(2)}) %collective-permute-start.2) | collective-permute-done | bytes 262176 | tf_op jit(solution)/shard_map/ppermute | solution.py:22
  45.2 1.6 %collective-permute-start.3 = (bf16[640,128]{1,0:T(8,128)(2,1)S(1)}, bf16[640,128]{1,0:T(8,128)(2,1)S(1)}, u32[]{:S(2)}, u32[]{:S(2)}) collective-permute-start(bf16[640,128]{1,0:T(8,128)(2,1)S(1)} %get-tuple-element.5), channel_id=1, source_target_pairs={{0,8},{1,9},{2,10},{3,11},{4,12},{5,13},{6,14},{7,15},{8,0},{9,1},... | collective-permute-start | bytes 491528 | tf_op jit(solution)/shard_map/ppermute | solution.py:22
  47.1 3.6 %collective-permute-done.3 = bf16[640,128]{1,0:T(8,128)(2,1)S(1)} collective-permute-done((bf16[640,128]{1,0:T(8,128)(2,1)S(1)}, bf16[640,128]{1,0:T(8,128)(2,1)S(1)}, u32[]{:S(2)}, u32[]{:S(2)}) %collective-permute-start.3) | collective-permute-done | bytes 163872 | tf_op jit(solution)/shard_map/ppermute | solution.py:22
  51.2 2.5 %collective-permute-start.4 = (bf16[64,128]{1,0:T(8,128)(2,1)S(1)}, bf16[64,128]{1,0:T(8,128)(2,1)S(1)}, u32[]{:S(2)}, u32[]{:S(2)}) collective-permute-start(bf16[64,128]{1,0:T(8,128)(2,1)S(1)} %subtract_convert_fusion), channel_id=1, source_target_pairs={{0,16},{1,17},{2,18},{3,19},{4,20},{5,21},{6,22},{7,23},{8,24},{9,... | collective-permute-start | bytes 49160 | tf_op jit(solution)/shard_map/ppermute | solution.py:22
  54.0 1.9 %collective-permute-done.4 = bf16[64,128]{1,0:T(8,128)(2,1)S(1)} collective-permute-done((bf16[64,128]{1,0:T(8,128)(2,1)S(1)}, bf16[64,128]{1,0:T(8,128)(2,1)S(1)}, u32[]{:S(2)}, u32[]{:S(2)}) %collective-permute-start.4) | collective-permute-done | bytes 16416 | tf_op jit(solution)/shard_map/ppermute | solution.py:22
  56.0 1.2 %convolution_subtract_fusion = f32[64,2048]{1,0:T(8,128)} fusion(f32[64,2048]{1,0:T(8,128)S(1)} %convolution_subtract_fusion.1, bf16[128,2048]{1,0:T(8,128)(2,1)S(1)} %copy-done.7, f32[64,128]{1,0:T(8,128)S(1)} %fusion.65, bf16[64,128]{1,0:T(8,128)(2,1)S(1)} %get-tuple-element.8, bf16[64,128]{1,0:T(8,128)(2,1)S(1)} %get-tuple-element.76, pred[]{:T(512)S(6)} %eq.18, ...), kind=kOutput, calls=%fused_computation | convolution fusion | flops 35954688 | bytes 1671170 | tf_op jit(solution)/shard_map/dot_general | solution.py:12
  (95 shorter events, 10.2 us)
Async XLA Ops:
  0.0 3.0 %copy-start = (bf16[128,2048]{1,0:T(8,128)(2,1)S(1)}, bf16[128,2048]{1,0:T(8,128)(2,1)}, u32[]{:S(2)}) copy-start(bf16[128,2048]{1,0:T(8,128)(2,1)} %param.18) | copy-start | bytes 1572868
  0.0 1.3 %copy-start.8 = (bf16[128,2048]{1,0:T(8,128)(2,1)S(1)}, bf16[128,2048]{1,0:T(8,128)(2,1)}, u32[]{:S(2)}) copy-start(bf16[128,2048]{1,0:T(8,128)(2,1)} %param.21) | copy-start | bytes 1572868
  1.3 1.0 %copy-start.5 = (bf16[128,2048]{1,0:T(8,128)(2,1)S(1)}, bf16[128,2048]{1,0:T(8,128)(2,1)}, u32[]{:S(2)}) copy-start(bf16[128,2048]{1,0:T(8,128)(2,1)} %param.20) | copy-start | bytes 1572868
  1.6 1.1 %copy-start.3 = (bf16[128,2048]{1,0:T(8,128)(2,1)S(1)}, bf16[128,2048]{1,0:T(8,128)(2,1)}, u32[]{:S(2)}) copy-start(bf16[128,2048]{1,0:T(8,128)(2,1)} %param.19) | copy-start | bytes 1572868
  3.0 1.0 %copy-start.1 = (bf16[128,2048]{1,0:T(8,128)(2,1)S(1)}, bf16[128,2048]{1,0:T(8,128)(2,1)}, u32[]{:S(2)}) copy-start(bf16[128,2048]{1,0:T(8,128)(2,1)} %param.17) | copy-start | bytes 1572868
  4.6 1.0 %copy-start.2 = (bf16[128,2048]{1,0:T(8,128)(2,1)S(1)}, bf16[128,2048]{1,0:T(8,128)(2,1)}, u32[]{:S(2)}) copy-start(bf16[128,2048]{1,0:T(8,128)(2,1)} %param.16) | copy-start | bytes 1572868
  6.0 0.8 %copy-start.9 = (f32[64,256]{1,0:T(8,128)S(1)}, f32[64,256]{1,0:T(8,128)}, u32[]{:S(2)}) copy-start(f32[64,256]{1,0:T(8,128)} %param.25) | copy-start | bytes 196612
  6.0 1.1 %copy-start.6 = (bf16[128,2048]{1,0:T(8,128)(2,1)S(1)}, bf16[128,2048]{1,0:T(8,128)(2,1)}, u32[]{:S(2)}) copy-start(bf16[128,2048]{1,0:T(8,128)(2,1)} %param.15) | copy-start | bytes 1572868
  7.4 0.8 %copy-start.10 = (f32[32,256]{1,0:T(8,128)S(1)}, f32[32,256]{1,0:T(8,128)}, u32[]{:S(2)}) copy-start(f32[32,256]{1,0:T(8,128)} %param.24) | copy-start | bytes 98308
  8.2 0.7 %copy-start.11 = (f32[16,256]{1,0:T(8,128)S(1)}, f32[16,256]{1,0:T(8,128)}, u32[]{:S(2)}) copy-start(f32[16,256]{1,0:T(8,128)} %param.23) | copy-start | bytes 49156
  8.9 0.7 %copy-start.12 = (f32[8,256]{1,0:T(8,128)S(1)}, f32[8,256]{1,0:T(8,128)}, u32[]{:S(2)}) copy-start(f32[8,256]{1,0:T(8,128)} %param.22) | copy-start | bytes 24580
  9.7 1.8 %collective-permute-start = (bf16[1264,128]{1,0:T(8,128)(2,1)S(1)}, bf16[1264,128]{1,0:T(8,128)(2,1)S(1)}, u32[]{:S(2)}, u32[]{:S(2)}) collective-permute-start(bf16[1264,128]{1,0:T(8,128)(2,1)S(1)} %constant_dynamic-update-slice_fusion), channel_id=1, source_target_pairs={{0,1},{1,0},{2,3},{3,2},{4,5},{5,4},{6,7},{7,6},{8,9},{9,8},{10,11... | collective-permute-start | bytes 970760 | tf_op jit(solution)/shard_map/ppermute | solution.py:22
  22.5 12.3 %collective-permute-start.1 = (bf16[1504,128]{1,0:T(8,128)(2,1)}, bf16[1504,128]{1,0:T(8,128)(2,1)S(1)}, u32[]{:S(2)}, u32[]{:S(2)}) collective-permute-start(bf16[1504,128]{1,0:T(8,128)(2,1)} %get-tuple-element.33), channel_id=1, source_target_pairs={{0,2},{1,3},{2,0},{3,1},{4,6},{5,7},{6,4},{7,5},{8,10},{9,11},{10,... | collective-permute-start | bytes 1155080 | tf_op jit(solution)/shard_map/ppermute | solution.py:22
  35.9 2.3 %copy-start.4 = (f32[64,2048]{1,0:T(8,128)S(1)}, f32[64,2048]{1,0:T(8,128)}, u32[]{:S(2)}) copy-start(f32[64,2048]{1,0:T(8,128)} %param.13) | copy-start | bytes 1572868
  36.3 7.9 %collective-permute-start.2 = (bf16[1024,128]{1,0:T(8,128)(2,1)S(1)}, bf16[1024,128]{1,0:T(8,128)(2,1)S(1)}, u32[]{:S(2)}, u32[]{:S(2)}) collective-permute-start(bf16[1024,128]{1,0:T(8,128)(2,1)S(1)} %get-tuple-element.13), channel_id=1, source_target_pairs={{0,4},{1,5},{2,6},{3,7},{4,0},{5,1},{6,2},{7,3},{8,12},{9,13},{10,... | collective-permute-start | bytes 786440 | tf_op jit(solution)/shard_map/ppermute | solution.py:22
  45.2 5.4 %collective-permute-start.3 = (bf16[640,128]{1,0:T(8,128)(2,1)S(1)}, bf16[640,128]{1,0:T(8,128)(2,1)S(1)}, u32[]{:S(2)}, u32[]{:S(2)}) collective-permute-start(bf16[640,128]{1,0:T(8,128)(2,1)S(1)} %get-tuple-element.5), channel_id=1, source_target_pairs={{0,8},{1,9},{2,10},{3,11},{4,12},{5,13},{6,14},{7,15},{8,0},{9,1},... | collective-permute-start | bytes 491528 | tf_op jit(solution)/shard_map/ppermute | solution.py:22
  51.2 4.8 %copy-start.7 = (bf16[128,2048]{1,0:T(8,128)(2,1)S(1)}, bf16[128,2048]{1,0:T(8,128)(2,1)}, u32[]{:S(2)}) copy-start(bf16[128,2048]{1,0:T(8,128)(2,1)} %param.14) | copy-start | bytes 1572868
  51.2 4.6 %collective-permute-start.4 = (bf16[64,128]{1,0:T(8,128)(2,1)S(1)}, bf16[64,128]{1,0:T(8,128)(2,1)S(1)}, u32[]{:S(2)}, u32[]{:S(2)}) collective-permute-start(bf16[64,128]{1,0:T(8,128)(2,1)S(1)} %subtract_convert_fusion), channel_id=1, source_target_pairs={{0,16},{1,17},{2,18},{3,19},{4,20},{5,21},{6,22},{7,23},{8,24},{9,... | collective-permute-start | bytes 49160 | tf_op jit(solution)/shard_map/ppermute | solution.py:22

commit v2 on v1

v2 whole, which is shorter than its diff:
```python
import jax
import jax.numpy as jnp
from jax import lax
from jax.experimental import pallas as pl
from jax.experimental.pallas import tpu as pltpu
from jax.sharding import PartitionSpec as P

BF = jnp.bfloat16
F32 = jnp.float32
LEVELS = (4, 3, 2, 1)
PAIRS = tuple((l, k) for l in LEVELS for k in LEVELS if k < l)
VMEM = pl.BlockSpec(memory_space=pltpu.VMEM)
HBM = pl.BlockSpec(memory_space=pltpu.HBM)


def nn(a, b):
    return lax.dot_general(a, b, (((1,), (0,)), ((), ())), preferred_element_type=F32)


def nt(a, b):
    return lax.dot_general(a, b, (((1,), (1,)), ((), ())), preferred_element_type=F32)


def layout(level, width, rank, rows):
    sizes = {("p", k): width for k in LEVELS if k <= level}
    sizes.update({("g", l, k): rank for l, k in PAIRS if l <= level})
    if level > 1:
        sizes.update({("c", k): 2 * rows[k] for k in LEVELS if k <= level})
    out, start = {}, 0
    for key, size in sizes.items():
        out[key] = (start, start + size)
        start += size
    return out, start


def swap(x, bit):
    size = lax.axis_size("pts")
    return lax.ppermute(x, "pts", [(i, i ^ (1 << bit)) for i in range(size)])


def first_kernel(spans, rank, with_coupling, x_hbm, *refs):
    names = ("r1", "r2", "s4", "s3", "r3", "s2", "r4")
    b_hbm = dict(zip(names, refs[:7]))
    c_refs = dict(zip(LEVELS, refs[7:11])) if with_coupling else {}
    refs = refs[7 + len(c_refs) :]
    out, x_v, b_v = refs[0], refs[1], refs[2]
    sems = refs[3]
    copies = {"x": pltpu.make_async_copy(x_hbm, x_v, sems.at[0])}
    b = {}
    for i, name in enumerate(names):
        b[name] = b_v.at[i]
        copies[name] = pltpu.make_async_copy(b_hbm[name], b[name], sems.at[i + 1])
    for copy in copies.values():
        copy.start()

    def put(key, value):
        out[spans[key][0] : spans[key][1]] = value.astype(BF)

    for k, ref in c_refs.items():
        c = ref[...]
        put(("c", k), jnp.concatenate([c[:, :rank], c[:, rank:]], axis=0))

    copies["x"].wait()
    copies["r1"].wait()
    copies["r2"].wait()
    x = x_v[...].astype(BF)
    low = jnp.concatenate([b["r1"][...], b["r2"][...]], axis=0)
    got = nt(x, low)
    put(("p", 1), got[:, :rank])
    put(("p", 2), got[:, rank:])
    for l, name in ((4, "s4"), (3, "s3")):
        copies[name].wait()
        got = nt(b[name][...], low)
        put(("g", l, 1), got[:, :rank])
        put(("g", l, 2), got[:, rank:])
    copies["r3"].wait()
    put(("g", 4, 3), nt(b["s4"][...], b["r3"][...]))
    copies["s2"].wait()
    put(("g", 2, 1), nt(b["s2"][...], b["r1"][...]))
    copies["r4"].wait()
    got = nt(x, jnp.concatenate([b["r3"][...], b["r4"][...]], axis=0))
    put(("p", 3), got[:, :rank])
    put(("p", 4), got[:, rank:])


def interleave(own, other, upper):
    half = own.shape[0] // 2
    own, other = own.astype(F32), other.astype(F32)
    first = jnp.where(upper, other, own)
    second = jnp.where(upper, own, other)
    return jnp.concatenate([first[:half], second[:half], first[half:], second[half:]], axis=0).astype(BF)


def merge_kernel(bit, spans, then, own, got, out):
    upper = (lax.axis_index("pts") >> bit & 1) == 1
    for key, (lo, hi) in spans.items():
        a, z = own[lo:hi], got[lo:hi]
        if key[0] == "c":
            out[then[key][0] : then[key][1]] = interleave(a, z, upper)
        else:
            out[then[key][0] : then[key][1]] = (a.astype(F32) + z.astype(F32)).astype(BF)


def level_kernel(level, bit, spans, then, rank, own, got, *refs):
    upper = (lax.axis_index("pts") >> bit & 1) == 1
    if level == 1:
        last, weights = refs
    else:
        out, weights = refs[0], refs[1]

    def both(key):
        lo, hi = spans[key]
        return own[lo:hi], got[lo:hi]

    a, z = both(("p", level))
    stacked = jnp.concatenate([jnp.where(upper, z, a), jnp.where(upper, a, z)], axis=1)
    if level == 1:
        c = last[...]
        weights[...] = nt(stacked, jnp.concatenate([c[:rank], c[rank:]], axis=1)).astype(BF)
        return
    a, z = both(("c", level))
    rows = jnp.concatenate(
        [
            jnp.concatenate([a[:rank], a[rank:]], axis=1),
            jnp.concatenate([z[:rank], z[rank:]], axis=1),
        ],
        axis=0,
    )
    w = nt(stacked, rows).astype(BF)
    weights[...] = w[:, :rank]
    below = [k for k in LEVELS if k < level]
    gram = jnp.concatenate([jnp.concatenate(both(("g", level, k)), axis=0) for k in below], axis=1)
    change = nn(w, gram)
    for i, k in enumerate(below):
        a, z = both(("p", k))
        lo, hi = then[("p", k)]
        out[lo:hi] = (a.astype(F32) + z.astype(F32) - change[:, i * rank : (i + 1) * rank]).astype(BF)
    for key in spans:
        if key[0] == "g" and key[1] < level:
            a, z = both(key)
            out[then[key][0] : then[key][1]] = (a.astype(F32) + z.astype(F32)).astype(BF)
        if key[0] == "c" and key[1] < level:
            a, z = both(key)
            rows = interleave(a, z, upper)
            if level == 2:
                refs[2][...] = rows
            else:
                out[then[key][0] : then[key][1]] = rows


def on_device(right_solved, s1, s2, s3, s4, r1, r2, r3, r4, c1, c2, c3, c4):
    solved = {1: s1, 2: s2, 3: s3, 4: s4}
    coupling = {1: c1, 2: c2, 3: c3, 4: c4}
    rank, points = s1.shape
    width = right_solved.shape[0]
    bits = lax.axis_size("pts").bit_length() - 1

    rows = {k: coupling[k].shape[0] for k in LEVELS}
    in_kernel = all(rows[k] % 8 == 0 for k in LEVELS)
    spans, total = layout(4, width, rank, rows)
    inner = total if in_kernel else spans[("c", 4)][0]
    operands = [right_solved, r1, r2, s4, s3, r3, s2, r4]
    if in_kernel:
        operands += [coupling[k] for k in LEVELS]
    operands = [pltpu.with_memory_space_constraint(x, pltpu.HBM) for x in operands]
    buf = pl.pallas_call(
        lambda *refs: first_kernel(spans, rank, in_kernel, *refs),
        out_shape=jax.ShapeDtypeStruct((inner, rank), BF),
        in_specs=[HBM] * 8 + [VMEM] * (len(operands) - 8),
        out_specs=VMEM,
        scratch_shapes=[
            pltpu.VMEM((width, points), F32),
            pltpu.VMEM((7, rank, points), BF),
            pltpu.SemaphoreType.DMA((8,)),
        ],
        compiler_params=pltpu.CompilerParams(vmem_limit_bytes=24 * 2**20),
        name="products",
    )(*operands)

    bit = 0
    if not in_kernel:
        parts = {k: jnp.stack([c[:, :rank], c[:, rank:]]).astype(BF) for k, c in coupling.items()}
        while bits - bit > 4:
            got = swap(buf, bit)
            buf = (buf.astype(F32) + got.astype(F32)).astype(BF)
            upper = (lax.axis_index("pts") >> bit & 1) == 1
            for k in LEVELS:
                got = swap(parts[k], bit)
                first, second = jnp.where(upper, got, parts[k]), jnp.where(upper, parts[k], got)
                parts[k] = jnp.concatenate([first, second], axis=1)
            bit += 1
        rows = {k: parts[k].shape[1] for k in LEVELS}
        buf = jnp.concatenate([buf] + [parts[k].reshape(2 * rows[k], rank) for k in LEVELS], axis=0)
        spans, total = layout(4, width, rank, rows)

    current, last = right_solved, None
    while bit < bits:
        level = bits - bit
        got = swap(buf, bit)
        rows = {k: 2 * rows[k] for k in LEVELS}
        operands, more = [buf, got], []
        if level > 4:
            then, total = layout(4, width, rank, rows)
            kernel = lambda *refs, b=bit, s=spans, t=then: merge_kernel(b, s, t, *refs)
        else:
            then, total = layout(level - 1, width, rank, rows)
            kernel = lambda *refs, l=level, b=bit, s=spans, t=then: level_kernel(l, b, s, t, rank, *refs)
            more = [jax.ShapeDtypeStruct((width, rank), BF)]
        if level == 2:
            more.append(jax.ShapeDtypeStruct((2 * rank, rank), BF))
        if level == 1:
            operands.append(last)
            shapes = more
        else:
            shapes = [jax.ShapeDtypeStruct((total, rank), BF)] + more
        outs = pl.pallas_call(
            kernel,
            out_shape=shapes,
            in_specs=[VMEM] * len(operands),
            out_specs=[VMEM] * len(shapes),
            compiler_params=pltpu.CompilerParams(vmem_limit_bytes=24 * 2**20),
            name="stage",
        )(*operands)
        if level == 2:
            last = outs[2]
        if level <= 4:
            current = current - nn(outs[0 if level == 1 else 1], solved[level])
        buf, spans = outs[0], then
        bit += 1
    return current


def solution(mesh):
    wide, tall = P(None, "pts"), P("pts", None)
    return jax.shard_map(
        on_device, mesh=mesh, in_specs=(wide,) * 9 + (tall,) * 4, out_specs=wide, check_vma=False
    )
```

time: 57.6 us -> 41.3 us (0.72)
  other arithmetic: 12.6 us -> 0 us
  Pallas kernels: 0 us -> 6.89 us
  matrix products: 7.66 us -> 1.67 us
  local copies, waits for them, and re-layouts: 5.29 us -> 1 us
    unnamed x28 -> x0, other arithmetic: 10.2 us -> none
    pallas_call x0 -> x6, Pallas kernels: none -> 6.89 us  [the longest x1 5.72 us: on_device(): pl.pallas_call(lambda *refs: first_kernel(spans, rank, in_kernel, *refs),...]
    unnamed x29 -> x10, local copies, waits for them, and re-layouts: 5.19 us -> 1 us
    dot_general x17 -> x0, matrix products: 4.13 us -> none  [nt(): lax.dot_general(a, b, (((1,), (1,)), ((), ())), preferred_element_type=F32)]
    dot_general x16 -> x4, matrix products: 3.53 us -> 1.67 us  [nn(): lax.dot_general(a, b, (((1,), (0,)), ((), ())), preferred_element_type=F32)]
    convert_element_type x1 -> x0, other arithmetic: 1.16 us -> none  [on_device(): rounded = right_solved.astype(BF)]
    concatenate x3 -> x0, other arithmetic: 0.63 us -> none  [exchange(): sent = jnp.concatenate(parts, axis=0)]
    slice x1 -> x0, other arithmetic: 0.62 us -> none  [exchange(): out.append(got[start:start + part.shape[0]])]
where the time goes in v2:
time: 41.3 us; the launch traced here: 41.1 us
  waiting for transfers between devices  22 us (53%)
  starting transfers between devices  9.44 us (23%)
  Pallas kernels  6.89 us (17%)
  matrix products  1.67 us (4%)
  local copies, waits for them, and re-layouts  1 us (2%)
    ppermute x5, waiting for transfers between devices, swap(): return lax.ppermute(x, 'pts', [(i, i ^ 1 << bit) for i in range(size)])  22 us
    ppermute x5, starting transfers between devices, swap(): return lax.ppermute(x, 'pts', [(i, i ^ 1 << bit) for i in range(size)])  9.44 us
    pallas_call x1, Pallas kernels, on_device(): pl.pallas_call(lambda *refs: first_kernel(spans, rank, in_kernel, *refs),...  5.72 us
    dot_general x4, matrix products, nn(): lax.dot_general(a, b, (((1,), (0,)), ((), ())), preferred_element_type=F32)  1.67 us
    pallas_call x5, Pallas kernels, on_device(): pl.pallas_call(kernel, out_shape=shapes, in_specs=[VMEM] * len(operands),...  1.17 us
    unnamed x10, local copies, waits for them, and re-layouts  1 us
  transfers between devices with their start and end apart: 5, of which 5 were waited for; matrix products, arithmetic and copies ran while one was open for 1% of the time, Pallas kernels for 0%

profile of v2, /device:TPU:0, one launch (start us, length us, event | category | flops | bytes accessed | tf_op | source)
XLA Modules:
  0.0 41.1 jit_solution(4509034793395448097)
XLA Ops:
  0.0 0.0 copy-start
  0.0 5.7 %products.1.refs_0_ = bf16[1264,128]{1,0:T(8,128)(2,1)S(1)} custom-call(f32[64,2048]{1,0:T(8,128)} %refs_0_.1, bf16[128,2048]{1,0:T(8,128)(2,1)} %refs_1_.1, bf16[128,2048]{1,0:T(8,128)(2,1)} %refs_2_.1, bf16[128,2048]{1,0:T(8,128)(2,1)} %refs_3_.1, bf16[128,2048]{1,0:T(8,128)(2,1)} %refs_4_.1, bf16[128,2048]{1,0:T(8,128)(2,1)} %refs_5_.1, ...), custom_call_target="tpu_custom_call" | custom-call | tf_op jit(solution)/shard_map/products/pallas_call | solution.py:166
  5.7 0.5 %collective-permute-start = (bf16[1264,128]{1,0:T(8,128)(2,1)S(1)}, bf16[1264,128]{1,0:T(8,128)(2,1)S(1)}, u32[]{:S(2)}, u32[]{:S(2)}) collective-permute-start(bf16[1264,128]{1,0:T(8,128)(2,1)S(1)} %products.1.refs_0_), channel_id=1, source_target_pairs={{0,1},{1,0},{2,3},{3,2},{4,5},{5,4},{6,7},{7,6},{8,9},{9,8},{10,11... | collective-permute-start | bytes 970760 | tf_op jit(solution)/shard_map/ppermute | solution.py:38
  6.2 1.2 %collective-permute-done.refs_1_ = bf16[1264,128]{1,0:T(8,128)(2,1)S(1)} collective-permute-done((bf16[1264,128]{1,0:T(8,128)(2,1)S(1)}, bf16[1264,128]{1,0:T(8,128)(2,1)S(1)}, u32[]{:S(2)}, u32[]{:S(2)}) %collective-permute-start) | collective-permute-done | bytes 323616 | tf_op jit(solution)/shard_map/ppermute | solution.py:38
  7.5 0.1 stage.5.refs_0_
  7.6 0.0 copy-start.1
  7.6 2.9 %collective-permute-start.1 = (bf16[1504,128]{1,0:T(8,128)(2,1)S(1)}, bf16[1504,128]{1,0:T(8,128)(2,1)S(1)}, u32[]{:S(2)}, u32[]{:S(2)}) collective-permute-start(bf16[1504,128]{1,0:T(8,128)(2,1)S(1)} %stage.5.refs_0_), channel_id=1, source_target_pairs={{0,2},{1,3},{2,0},{3,1},{4,6},{5,7},{6,4},{7,5},{8,10},{9,11},{10,... | collective-permute-start | bytes 1155080 | tf_op jit(solution)/shard_map/ppermute | solution.py:38
  10.5 9.2 %collective-permute-done.1.refs_1_ = bf16[1504,128]{1,0:T(8,128)(2,1)S(1)} collective-permute-done((bf16[1504,128]{1,0:T(8,128)(2,1)S(1)}, bf16[1504,128]{1,0:T(8,128)(2,1)S(1)}, u32[]{:S(2)}, u32[]{:S(2)}) %collective-permute-start.1) | collective-permute-done | bytes 385056 | tf_op jit(solution)/shard_map/ppermute | solution.py:38
  19.8 0.3 stage.6
  20.1 1.8 %collective-permute-start.2 = (bf16[1024,128]{1,0:T(8,128)(2,1)S(1)}, bf16[1024,128]{1,0:T(8,128)(2,1)S(1)}, u32[]{:S(2)}, u32[]{:S(2)}) collective-permute-start(bf16[1024,128]{1,0:T(8,128)(2,1)S(1)} %get-tuple-element.13.refs_0_), channel_id=1, source_target_pairs={{0,4},{1,5},{2,6},{3,7},{4,0},{5,1},{6,2},{7,3},{8,12},{9,13},{10,... | collective-permute-start | bytes 786440 | tf_op jit(solution)/shard_map/ppermute | solution.py:38
  21.9 6.1 %collective-permute-done.2.refs_1_ = bf16[1024,128]{1,0:T(8,128)(2,1)S(1)} collective-permute-done((bf16[1024,128]{1,0:T(8,128)(2,1)S(1)}, bf16[1024,128]{1,0:T(8,128)(2,1)S(1)}, u32[]{:S(2)}, u32[]{:S(2)}) %collective-permute-start.2) | collective-permute-done | bytes 262176 | tf_op jit(solution)/shard_map/ppermute | solution.py:38
  28.0 0.3 stage.7
  28.3 1.6 %collective-permute-start.3 = (bf16[640,128]{1,0:T(8,128)(2,1)S(1)}, bf16[640,128]{1,0:T(8,128)(2,1)S(1)}, u32[]{:S(2)}, u32[]{:S(2)}) collective-permute-start(bf16[640,128]{1,0:T(8,128)(2,1)S(1)} %get-tuple-element.15.refs_0_), channel_id=1, source_target_pairs={{0,8},{1,9},{2,10},{3,11},{4,12},{5,13},{6,14},{7,15},{8,0},{9,1},... | collective-permute-start | bytes 491528 | tf_op jit(solution)/shard_map/ppermute | solution.py:38
  29.9 0.0 copy-done.1
  29.9 0.0 copy-start.2
  29.9 0.2 fusion.3
  30.1 3.6 %collective-permute-done.3.refs_1_ = bf16[640,128]{1,0:T(8,128)(2,1)S(1)} collective-permute-done((bf16[640,128]{1,0:T(8,128)(2,1)S(1)}, bf16[640,128]{1,0:T(8,128)(2,1)S(1)}, u32[]{:S(2)}, u32[]{:S(2)}) %collective-permute-start.3) | collective-permute-done | bytes 163872 | tf_op jit(solution)/shard_map/ppermute | solution.py:38
  33.7 0.3 stage.8
  34.0 2.6 %collective-permute-start.4 = (bf16[64,128]{1,0:T(8,128)(2,1)S(1)}, bf16[64,128]{1,0:T(8,128)(2,1)S(1)}, u32[]{:S(2)}, u32[]{:S(2)}) collective-permute-start(bf16[64,128]{1,0:T(8,128)(2,1)S(1)} %get-tuple-element.17.refs_0_), channel_id=1, source_target_pairs={{0,16},{1,17},{2,18},{3,19},{4,20},{5,21},{6,22},{7,23},{8,24},{9,... | collective-permute-start | bytes 49160 | tf_op jit(solution)/shard_map/ppermute | solution.py:38
  36.6 0.0 copy-done.2
  36.6 0.2 fusion.4
  36.8 1.9 %collective-permute-done.4.refs_1_ = bf16[64,128]{1,0:T(8,128)(2,1)S(1)} collective-permute-done((bf16[64,128]{1,0:T(8,128)(2,1)S(1)}, bf16[64,128]{1,0:T(8,128)(2,1)S(1)}, u32[]{:S(2)}, u32[]{:S(2)}) %collective-permute-start.4) | collective-permute-done | bytes 16416 | tf_op jit(solution)/shard_map/ppermute | solution.py:38
  38.7 0.1 stage.9
  38.9 0.0 copy-done
  38.9 0.0 copy-start.3
  38.9 0.0 copy-start.4
  38.9 0.2 fusion.5
  39.1 0.8 %copy-done.3 = f32[64,2048]{1,0:T(8,128)S(1)} copy-done((f32[64,2048]{1,0:T(8,128)S(1)}, f32[64,2048]{1,0:T(8,128)}, u32[]{:S(2)}) %copy-start.3) | copy-done | bytes 524312
  39.9 0.2 copy-done.4
  40.1 1.0 %fusion.2 = f32[64,2048]{1,0:T(8,128)} fusion(f32[64,2048]{1,0:T(8,128)S(1)} %fusion.5, f32[64,2048]{1,0:T(8,128)S(1)} %fusion.4, f32[64,2048]{1,0:T(8,128)S(1)} %fusion.3, f32[64,2048]{1,0:T(8,128)S(1)} %copy-done.3, bf16[64,128]{1,0:T(8,128)(2,1)S(1)} %get-tuple-element.12, bf16[128,2048]{1,0:T(8,128)(2,1)S(1)} %copy-done.4), kind=kOutput, calls=%fused_computation.3 | convolution fusion | flops 34078720 | bytes 3162112 | tf_op jit(solution)/shard_map/dot_general | solution.py:17
Async XLA Ops:
  0.0 38.9 %copy-start = (bf16[128,2048]{1,0:T(8,128)(2,1)S(1)}, bf16[128,2048]{1,0:T(8,128)(2,1)}, u32[]{:S(2)}) copy-start(bf16[128,2048]{1,0:T(8,128)(2,1)} %param.14) | copy-start | bytes 1572868
  5.7 1.8 %collective-permute-start = (bf16[1264,128]{1,0:T(8,128)(2,1)S(1)}, bf16[1264,128]{1,0:T(8,128)(2,1)S(1)}, u32[]{:S(2)}, u32[]{:S(2)}) collective-permute-start(bf16[1264,128]{1,0:T(8,128)(2,1)S(1)} %products.1.refs_0_), channel_id=1, source_target_pairs={{0,1},{1,0},{2,3},{3,2},{4,5},{5,4},{6,7},{7,6},{8,9},{9,8},{10,11... | collective-permute-start | bytes 970760 | tf_op jit(solution)/shard_map/ppermute | solution.py:38
  7.6 22.3 %copy-start.1 = (bf16[128,2048]{1,0:T(8,128)(2,1)S(1)}, bf16[128,2048]{1,0:T(8,128)(2,1)}, u32[]{:S(2)}) copy-start(bf16[128,2048]{1,0:T(8,128)(2,1)} %refs_4_.1) | copy-start | bytes 1572868
  7.6 12.2 %collective-permute-start.1 = (bf16[1504,128]{1,0:T(8,128)(2,1)S(1)}, bf16[1504,128]{1,0:T(8,128)(2,1)S(1)}, u32[]{:S(2)}, u32[]{:S(2)}) collective-permute-start(bf16[1504,128]{1,0:T(8,128)(2,1)S(1)} %stage.5.refs_0_), channel_id=1, source_target_pairs={{0,2},{1,3},{2,0},{3,1},{4,6},{5,7},{6,4},{7,5},{8,10},{9,11},{10,... | collective-permute-start | bytes 1155080 | tf_op jit(solution)/shard_map/ppermute | solution.py:38
  20.1 7.9 %collective-permute-start.2 = (bf16[1024,128]{1,0:T(8,128)(2,1)S(1)}, bf16[1024,128]{1,0:T(8,128)(2,1)S(1)}, u32[]{:S(2)}, u32[]{:S(2)}) collective-permute-start(bf16[1024,128]{1,0:T(8,128)(2,1)S(1)} %get-tuple-element.13.refs_0_), channel_id=1, source_target_pairs={{0,4},{1,5},{2,6},{3,7},{4,0},{5,1},{6,2},{7,3},{8,12},{9,13},{10,... | collective-permute-start | bytes 786440 | tf_op jit(solution)/shard_map/ppermute | solution.py:38
  28.3 5.4 %collective-permute-start.3 = (bf16[640,128]{1,0:T(8,128)(2,1)S(1)}, bf16[640,128]{1,0:T(8,128)(2,1)S(1)}, u32[]{:S(2)}, u32[]{:S(2)}) collective-permute-start(bf16[640,128]{1,0:T(8,128)(2,1)S(1)} %get-tuple-element.15.refs_0_), channel_id=1, source_target_pairs={{0,8},{1,9},{2,10},{3,11},{4,12},{5,13},{6,14},{7,15},{8,0},{9,1},... | collective-permute-start | bytes 491528 | tf_op jit(solution)/shard_map/ppermute | solution.py:38
  29.9 6.7 %copy-start.2 = (bf16[128,2048]{1,0:T(8,128)(2,1)S(1)}, bf16[128,2048]{1,0:T(8,128)(2,1)}, u32[]{:S(2)}) copy-start(bf16[128,2048]{1,0:T(8,128)(2,1)} %refs_6_.1) | copy-start | bytes 1572868
  34.0 4.7 %collective-permute-start.4 = (bf16[64,128]{1,0:T(8,128)(2,1)S(1)}, bf16[64,128]{1,0:T(8,128)(2,1)S(1)}, u32[]{:S(2)}, u32[]{:S(2)}) collective-permute-start(bf16[64,128]{1,0:T(8,128)(2,1)S(1)} %get-tuple-element.17.refs_0_), channel_id=1, source_target_pairs={{0,16},{1,17},{2,18},{3,19},{4,20},{5,21},{6,22},{7,23},{8,24},{9,... | collective-permute-start | bytes 49160 | tf_op jit(solution)/shard_map/ppermute | solution.py:38
  38.9 1.1 %copy-start.3 = (f32[64,2048]{1,0:T(8,128)S(1)}, f32[64,2048]{1,0:T(8,128)}, u32[]{:S(2)}) copy-start(f32[64,2048]{1,0:T(8,128)} %refs_0_.1) | copy-start | bytes 1572868
  38.9 1.2 %copy-start.4 = (bf16[128,2048]{1,0:T(8,128)(2,1)S(1)}, bf16[128,2048]{1,0:T(8,128)(2,1)}, u32[]{:S(2)}) copy-start(bf16[128,2048]{1,0:T(8,128)(2,1)} %refs_3_.1) | copy-start | bytes 1572868

commit v3 on v2

--- a/solution.py
+++ b/solution.py
@@ -11,6 +11,8 @@
 PAIRS = tuple((l, k) for l in LEVELS for k in LEVELS if k < l)
 VMEM = pl.BlockSpec(memory_space=pltpu.VMEM)
 HBM = pl.BlockSpec(memory_space=pltpu.HBM)
+CHUNKS_IN = 2
+CHUNKS_OUT = 4
 
 
 def nn(a, b):
@@ -38,49 +40,64 @@
     return lax.ppermute(x, "pts", [(i, i ^ (1 << bit)) for i in range(size)])
 
 
-def first_kernel(spans, rank, with_coupling, x_hbm, *refs):
-    names = ("r1", "r2", "s4", "s3", "r3", "s2", "r4")
-    b_hbm = dict(zip(names, refs[:7]))
-    c_refs = dict(zip(LEVELS, refs[7:11])) if with_coupling else {}
-    refs = refs[7 + len(c_refs) :]
-    out, x_v, b_v = refs[0], refs[1], refs[2]
-    sems = refs[3]
-    copies = {"x": pltpu.make_async_copy(x_hbm, x_v, sems.at[0])}
-    b = {}
-    for i, name in enumerate(names):
-        b[name] = b_v.at[i]
-        copies[name] = pltpu.make_async_copy(b_hbm[name], b[name], sems.at[i + 1])
-    for copy in copies.values():
+def first_kernel(spans, rank, width, chunks, with_coupling, x_hbm, *refs):
+    b_hbm = dict(zip(("r1", "r2", "s4", "s3", "s2", "r3", "r4"), refs[:7]))
+    c_hbm = dict(zip(LEVELS, refs[7:11])) if with_coupling else {}
+    refs = refs[7 + len(c_hbm) :]
+    out, x_v, left_v, right_v, acc_lo, acc_hi, acc_2, sems, c_sem = refs[:9]
+    c_v = dict(zip(LEVELS, refs[9:]))
+    points = x_v.shape[1]
+    cut = points // chunks
+    place = {"s4": (left_v, width), "s3": (left_v, width + rank), "s2": (left_v, width + 2 * rank)}
+    place.update({name: (right_v, i * rank) for i, name in enumerate(("r1", "r2", "r3", "r4"))})
+
+    def piece(j, i, name):
+        cols = pl.ds(j * cut, cut)
+        if name == "x":
+            return pltpu.make_async_copy(x_hbm.at[:, cols], x_v.at[:, cols], sems.at[j, i])
+        ref, row = place[name]
+        return pltpu.make_async_copy(b_hbm[name].at[:, cols], ref.at[pl.ds(row, rank), cols], sems.at[j, i])
+
+    copies = [[piece(j, i, n) for i, n in enumerate(("x", *b_hbm))] for j in range(chunks)]
+    c_copies = [pltpu.make_async_copy(c_hbm[k], c_v[k], c_sem.at[i]) for i, k in enumerate(c_hbm)]
+    for copy in copies[0] + c_copies:
         copy.start()
+    for group in copies[1:]:
+        for copy in group:
+            copy.start()
 
     def put(key, value):
         out[spans[key][0] : spans[key][1]] = value.astype(BF)
 
-    for k, ref in c_refs.items():
+    for copy in c_copies:
+        copy.wait()
+    for k, ref in c_v.items():
         c = ref[...]
         put(("c", k), jnp.concatenate([c[:, :rank], c[:, rank:]], axis=0))
 
-    copies["x"].wait()
-    copies["r1"].wait()
-    copies["r2"].wait()
-    x = x_v[...].astype(BF)
-    low = jnp.concatenate([b["r1"][...], b["r2"][...]], axis=0)
-    got = nt(x, low)
-    put(("p", 1), got[:, :rank])
-    put(("p", 2), got[:, rank:])
-    for l, name in ((4, "s4"), (3, "s3")):
-        copies[name].wait()
-        got = nt(b[name][...], low)
-        put(("g", l, 1), got[:, :rank])
-        put(("g", l, 2), got[:, rank:])
-    copies["r3"].wait()
-    put(("g", 4, 3), nt(b["s4"][...], b["r3"][...]))
-    copies["s2"].wait()
-    put(("g", 2, 1), nt(b["s2"][...], b["r1"][...]))
-    copies["r4"].wait()
-    got = nt(x, jnp.concatenate([b["r3"][...], b["r4"][...]], axis=0))
-    put(("p", 3), got[:, :rank])
-    put(("p", 4), got[:, rank:])
+    def total(j, ref, value):
+        if j > 0:
+            value = ref[...] + value
+        if j + 1 < chunks:
+            ref[...] = value
+        return value
+
+    for j in range(chunks):
+        for copy in copies[j]:
+            copy.wait()
+        cols = slice(j * cut, (j + 1) * cut)
+        left_v[:width, cols] = x_v[:, cols].astype(BF)
+        lo = total(j, acc_lo, nt(left_v[: width + 2 * rank, cols], right_v[: 2 * rank, cols]))
+        hi = total(j, acc_hi, nt(left_v[: width + rank, cols], right_v[2 * rank :, cols]))
+        two = total(j, acc_2, nt(left_v[width + 2 * rank :, cols], right_v[:rank, cols]))
+    for i in range(2):
+        side = slice(i * rank, (i + 1) * rank)
+        put(("p", 1 + i), lo[:width, side])
+        put(("p", 3 + i), hi[:width, side])
+        put(("g", 4, 1 + i), lo[width : width + rank, side])
+        put(("g", 3, 1 + i), lo[width + rank :, side])
+    put(("g", 4, 3), hi[width:, :rank])
+    put(("g", 2, 1), two)
 
 
 def interleave(own, other, upper):
@@ -103,10 +120,7 @@
 
 def level_kernel(level, bit, spans, then, rank, own, got, *refs):
     upper = (lax.axis_index("pts") >> bit & 1) == 1
-    if level == 1:
-        last, weights = refs
-    else:
-        out, weights = refs[0], refs[1]
+    out, weights = refs[0], refs[1]
 
     def both(key):
         lo, hi = spans[key]
@@ -114,10 +128,6 @@
 
     a, z = both(("p", level))
     stacked = jnp.concatenate([jnp.where(upper, z, a), jnp.where(upper, a, z)], axis=1)
-    if level == 1:
-        c = last[...]
-        weights[...] = nt(stacked, jnp.concatenate([c[:rank], c[rank:]], axis=1)).astype(BF)
-        return
     a, z = both(("c", level))
     rows = jnp.concatenate(
         [
@@ -148,32 +158,80 @@
                 out[then[key][0] : then[key][1]] = rows
 
 
+def early_kernel(x_hbm, s4, s3, s2, s1, w4, w3, rest, s2_out, s1_out, s_v, sems):
+    rank = s4.shape[0]
+    pairs = ((x_hbm, rest), (s4, s_v.at[:rank]), (s3, s_v.at[rank:]), (s2, s2_out), (s1, s1_out))
+    copies = [pltpu.make_async_copy(a, z, sems.at[i]) for i, (a, z) in enumerate(pairs)]
+    for copy in copies:
+        copy.start()
+    for copy in copies[:3]:
+        copy.wait()
+    rest[...] -= nn(jnp.concatenate([w4[...], w3[...]], axis=1), s_v[...])
+    for copy in copies[3:]:
+        copy.wait()
+
+
+def middle_kernel(rest, s2, w2, out):
+    out[...] = rest[...] - nn(w2[...], s2[...])
+
+
+def last_kernel(bit, chunks, own, got, coupling, rest, s1, out_hbm, out_v, sems):
+    upper = (lax.axis_index("pts") >> bit & 1) == 1
+    rank = coupling.shape[0] // 2
+    a, z, c = own[...], got[...], coupling[...]
+    stacked = jnp.concatenate([jnp.where(upper, z, a), jnp.where(upper, a, z)], axis=1)
+    weights = nt(stacked, jnp.concatenate([c[:rank], c[rank:]], axis=1)).astype(BF)
+    cut = rest.shape[1] // chunks
+    copies = []
+    for j in range(chunks):
+        cols = slice(j * cut, (j + 1) * cut)
+        out_v[:, cols] = rest[:, cols] - nn(weights, s1[:, cols])
+        span = pl.ds(j * cut, cut)
+        copies.append(pltpu.make_async_copy(out_v.at[:, span], out_hbm.at[:, span], sems.at[j]))
+        copies[-1].start()
+    for copy in copies:
+        copy.wait()
+
+
 def on_device(right_solved, s1, s2, s3, s4, r1, r2, r3, r4, c1, c2, c3, c4):
-    solved = {1: s1, 2: s2, 3: s3, 4: s4}
     coupling = {1: c1, 2: c2, 3: c3, 4: c4}
     rank, points = s1.shape
     width = right_solved.shape[0]
     bits = lax.axis_size("pts").bit_length() - 1
+    params = pltpu.CompilerParams(vmem_limit_bytes=24 * 2**20)
+
+    def stay(x):
+        return pltpu.with_memory_space_constraint(x, pltpu.HBM)
+
+    def cost(flops, moved):
+        return pl.CostEstimate(flops=flops, bytes_accessed=moved, transcendentals=0)
 
     rows = {k: coupling[k].shape[0] for k in LEVELS}
     in_kernel = all(rows[k] % 8 == 0 for k in LEVELS)
     spans, total = layout(4, width, rank, rows)
     inner = total if in_kernel else spans[("c", 4)][0]
-    operands = [right_solved, r1, r2, s4, s3, r3, s2, r4]
+    operands = [right_solved, r1, r2, s4, s3, s2, r3, r4]
     if in_kernel:
         operands += [coupling[k] for k in LEVELS]
-    operands = [pltpu.with_memory_space_constraint(x, pltpu.HBM) for x in operands]
+    operands = [stay(x) for x in operands]
+    chunks = CHUNKS_IN
     buf = pl.pallas_call(
-        lambda *refs: first_kernel(spans, rank, in_kernel, *refs),
+        lambda *refs: first_kernel(spans, rank, width, chunks, in_kernel, *refs),
         out_shape=jax.ShapeDtypeStruct((inner, rank), BF),
-        in_specs=[HBM] * 8 + [VMEM] * (len(operands) - 8),
+        in_specs=[HBM] * len(operands),
         out_specs=VMEM,
         scratch_shapes=[
             pltpu.VMEM((width, points), F32),
-            pltpu.VMEM((7, rank, points), BF),
-            pltpu.SemaphoreType.DMA((8,)),
-        ],
-        compiler_params=pltpu.CompilerParams(vmem_limit_bytes=24 * 2**20),
+            pltpu.VMEM((width + 3 * rank, points), BF),
+            pltpu.VMEM((4 * rank, points), BF),
+            pltpu.VMEM((width + 2 * rank, 2 * rank), F32),
+            pltpu.VMEM((width + rank, 2 * rank), F32),
+            pltpu.VMEM((rank, rank), F32),
+            pltpu.SemaphoreType.DMA((chunks, 8)),
+            pltpu.SemaphoreType.DMA((4,)),
+        ]
+        + ([pltpu.VMEM(coupling[k].shape, F32) for k in LEVELS] if in_kernel else []),
+        compiler_params=params,
         name="products",
     )(*operands)
 
@@ -193,41 +251,67 @@
         buf = jnp.concatenate([buf] + [parts[k].reshape(2 * rows[k], rank) for k in LEVELS], axis=0)
         spans, total = layout(4, width, rank, rows)
 
-    current, last = right_solved, None
-    while bit < bits:
+    weights = {}
+    while bits - bit > 1:
         level = bits - bit
         got = swap(buf, bit)
         rows = {k: 2 * rows[k] for k in LEVELS}
-        operands, more = [buf, got], []
         if level > 4:
             then, total = layout(4, width, rank, rows)
             kernel = lambda *refs, b=bit, s=spans, t=then: merge_kernel(b, s, t, *refs)
         else:
             then, total = layout(level - 1, width, rank, rows)
             kernel = lambda *refs, l=level, b=bit, s=spans, t=then: level_kernel(l, b, s, t, rank, *refs)
-            more = [jax.ShapeDtypeStruct((width, rank), BF)]
+        shapes = [jax.ShapeDtypeStruct((total, rank), BF)]
+        if level <= 4:
+            shapes.append(jax.ShapeDtypeStruct((width, rank), BF))
         if level == 2:
-            more.append(jax.ShapeDtypeStruct((2 * rank, rank), BF))
-        if level == 1:
-            operands.append(last)
-            shapes = more
-        else:
-            shapes = [jax.ShapeDtypeStruct((total, rank), BF)] + more
+            shapes.append(jax.ShapeDtypeStruct((2 * rank, rank), BF))
         outs = pl.pallas_call(
             kernel,
             out_shape=shapes,
-            in_specs=[VMEM] * len(operands),
+            in_specs=[VMEM] * 2,
             out_specs=[VMEM] * len(shapes),
-            compiler_params=pltpu.CompilerParams(vmem_limit_bytes=24 * 2**20),
+            compiler_params=params,
             name="stage",
-        )(*operands)
+        )(buf, got)
+        if level <= 4:
+            weights[level] = outs[1]
+        if level == 3:
+            wide = (width, points)
+            rest, s2_v, s1_v = pl.pallas_call(
+                early_kernel,
+                out_shape=[jax.ShapeDtypeStruct(wide, F32)] + [jax.ShapeDtypeStruct((rank, points), BF)] * 2,
+                in_specs=[HBM] * 5 + [VMEM] * 2,
+                out_specs=[VMEM] * 3,
+                scratch_shapes=[pltpu.VMEM((2 * rank, points), BF), pltpu.SemaphoreType.DMA((5,))],
+                compiler_params=params,
+                cost_estimate=cost(4 * width * rank * points, 6 * width * points + 8 * rank * points),
+                name="early",
+            )(*[stay(x) for x in (right_solved, s4, s3, s2, s1)], weights[4], weights[3])
         if level == 2:
-            last = outs[2]
-        if level <= 4:
-            current = current - nn(outs[0 if level == 1 else 1], solved[level])
+            rest = pl.pallas_call(
+                middle_kernel,
+                out_shape=jax.ShapeDtypeStruct(wide, F32),
+                in_specs=[VMEM] * 3,
+                out_specs=VMEM,
+                compiler_params=params,
+                cost_estimate=cost(2 * width * rank * points, 8 * width * points),
+                name="middle",
+            )(rest, s2_v, weights[2])
         buf, spans = outs[0], then
         bit += 1
-    return current
+    got = swap(buf, bit)
+    chunks = CHUNKS_OUT
+    return pl.pallas_call(
+        lambda *refs: last_kernel(bit, chunks, *refs),
+        out_shape=jax.ShapeDtypeStruct(wide, F32),
+        in_specs=[VMEM] * 5,
+        out_specs=HBM,
+        scratch_shapes=[pltpu.VMEM(wide, F32), pltpu.SemaphoreType.DMA((chunks,))],
+        compiler_params=params,
+        name="last",
+    )(buf, got, outs[2], rest, s1_v)
 
 
 def solution(mesh):

time: 41.3 us -> 37.6 us (0.910)
  matrix products: 1.67 us -> 0 us
  waiting for transfers between devices: 22 us -> 20.5 us
  local copies, waits for them, and re-layouts: 1 us -> 0 us
  Pallas kernels: 6.89 us -> 7.38 us
    dot_general x4 -> x0, matrix products: 1.67 us -> none  [nn(): lax.dot_general(a, b, (((1,), (0,)), ((), ())), preferred_element_type=F32)]
    ppermute x5, waiting for transfers between devices: 22 us -> 20.5 us  [swap(): return lax.ppermute(x, 'pts', [(i, i ^ 1 << bit) for i in range(size)])]
    unnamed x10 -> x0, local copies, waits for them, and re-layouts: 1 us -> none
    pallas_call x6 -> x8, Pallas kernels: 6.89 us -> 7.38 us  [the longest x1 3.29 us: on_device(): pl.pallas_call(lambda *refs: first_kernel(spans, rank, width, chunks, in_...]
  transfers between devices with their start and end apart: 5 -> 5, of which waited for: 5 -> 5; matrix products, arithmetic and copies ran while one was open for 1% -> 0% of each run, Pallas kernels for 0% -> 5%
where the time goes in v3:
time: 37.6 us; the launch traced here: 37.4 us
  waiting for transfers between devices  20.5 us (55%)
  starting transfers between devices  9.44 us (25%)
  Pallas kernels  7.38 us (20%)
    ppermute x5, waiting for transfers between devices, swap(): return lax.ppermute(x, 'pts', [(i, i ^ 1 << bit) for i in range(size)])  20.5 us
    ppermute x5, starting transfers between devices, swap(): return lax.ppermute(x, 'pts', [(i, i ^ 1 << bit) for i in range(size)])  9.44 us
    pallas_call x1, Pallas kernels, on_device(): pl.pallas_call(lambda *refs: first_kernel(spans, rank, width, chunks, in_...  3.29 us
    pallas_call x1, Pallas kernels, on_device(): pl.pallas_call(early_kernel, out_shape=[jax.ShapeDtypeStruct(wide, F32)]...  1.71 us
    pallas_call x1, Pallas kernels, on_device(): pl.pallas_call(lambda *refs: last_kernel(bit, chunks, *refs), out_shape=j...  1.12 us
    pallas_call x4, Pallas kernels, on_device(): pl.pallas_call(kernel, out_shape=shapes, in_specs=[VMEM] * 2, out_specs=[...  1.03 us
  transfers between devices with their start and end apart: 5, of which 5 were waited for; matrix products, arithmetic and copies ran while one was open for 0% of the time, Pallas kernels for 5%

profile of v3, /device:TPU:0, one launch (start us, length us, event | category | flops | bytes accessed | tf_op | source)
XLA Modules:
  0.0 37.4 jit_solution(14146766638123918646)
XLA Ops:
  0.0 3.3 %products.1.refs_0_ = bf16[1264,128]{1,0:T(8,128)(2,1)S(1)} custom-call(f32[64,2048]{1,0:T(8,128)} %x_hbm.1, bf16[128,2048]{1,0:T(8,128)(2,1)} %refs_1_.1, bf16[128,2048]{1,0:T(8,128)(2,1)} %refs_2_.1, bf16[128,2048]{1,0:T(8,128)(2,1)} %s4_.1, bf16[128,2048]{1,0:T(8,128)(2,1)} %s3.1, bf16[128,2048]{1,0:T(8,128)(2,1)} %s2_.1, bf16[128,2048]{1,0:T(8,128)(2,1)} %refs_6_.1, ...), custom_call_target="tpu_custom_call" | custom-call | tf_op jit(solution)/shard_map/products/pallas_call | solution.py:218
  3.3 0.5 %collective-permute-start = (bf16[1264,128]{1,0:T(8,128)(2,1)S(1)}, bf16[1264,128]{1,0:T(8,128)(2,1)S(1)}, u32[]{:S(2)}, u32[]{:S(2)}) collective-permute-start(bf16[1264,128]{1,0:T(8,128)(2,1)S(1)} %products.1.refs_0_), channel_id=1, source_target_pairs={{0,1},{1,0},{2,3},{3,2},{4,5},{5,4},{6,7},{7,6},{8,9},{9,8},{10,11... | collective-permute-start | bytes 970760 | tf_op jit(solution)/shard_map/ppermute | solution.py:40
  3.8 1.2 %collective-permute-done.refs_1_ = bf16[1264,128]{1,0:T(8,128)(2,1)S(1)} collective-permute-done((bf16[1264,128]{1,0:T(8,128)(2,1)S(1)}, bf16[1264,128]{1,0:T(8,128)(2,1)S(1)}, u32[]{:S(2)}, u32[]{:S(2)}) %collective-permute-start) | collective-permute-done | bytes 323616 | tf_op jit(solution)/shard_map/ppermute | solution.py:40
  5.1 0.1 stage.4.refs_0_
  5.2 2.9 %collective-permute-start.1 = (bf16[1504,128]{1,0:T(8,128)(2,1)S(1)}, bf16[1504,128]{1,0:T(8,128)(2,1)S(1)}, u32[]{:S(2)}, u32[]{:S(2)}) collective-permute-start(bf16[1504,128]{1,0:T(8,128)(2,1)S(1)} %stage.4.refs_0_), channel_id=1, source_target_pairs={{0,2},{1,3},{2,0},{3,1},{4,6},{5,7},{6,4},{7,5},{8,10},{9,11},{10,... | collective-permute-start | bytes 1155080 | tf_op jit(solution)/shard_map/ppermute | solution.py:40
  8.1 9.2 %collective-permute-done.1.refs_1_ = bf16[1504,128]{1,0:T(8,128)(2,1)S(1)} collective-permute-done((bf16[1504,128]{1,0:T(8,128)(2,1)S(1)}, bf16[1504,128]{1,0:T(8,128)(2,1)S(1)}, u32[]{:S(2)}, u32[]{:S(2)}) %collective-permute-start.1) | collective-permute-done | bytes 385056 | tf_op jit(solution)/shard_map/ppermute | solution.py:40
  17.3 0.3 stage.5
  17.7 1.8 %collective-permute-start.2 = (bf16[1024,128]{1,0:T(8,128)(2,1)S(1)}, bf16[1024,128]{1,0:T(8,128)(2,1)S(1)}, u32[]{:S(2)}, u32[]{:S(2)}) collective-permute-start(bf16[1024,128]{1,0:T(8,128)(2,1)S(1)} %get-tuple-element.15.refs_0_), channel_id=1, source_target_pairs={{0,4},{1,5},{2,6},{3,7},{4,0},{5,1},{6,2},{7,3},{8,12},{9,13},{10,... | collective-permute-start | bytes 786440 | tf_op jit(solution)/shard_map/ppermute | solution.py:40
  19.5 6.1 %collective-permute-done.2.refs_1_ = bf16[1024,128]{1,0:T(8,128)(2,1)S(1)} collective-permute-done((bf16[1024,128]{1,0:T(8,128)(2,1)S(1)}, bf16[1024,128]{1,0:T(8,128)(2,1)S(1)}, u32[]{:S(2)}, u32[]{:S(2)}) %collective-permute-start.2) | collective-permute-done | bytes 262176 | tf_op jit(solution)/shard_map/ppermute | solution.py:40
  25.6 0.3 stage.6
  25.9 1.6 %collective-permute-start.3 = (bf16[640,128]{1,0:T(8,128)(2,1)S(1)}, bf16[640,128]{1,0:T(8,128)(2,1)S(1)}, u32[]{:S(2)}, u32[]{:S(2)}) collective-permute-start(bf16[640,128]{1,0:T(8,128)(2,1)S(1)} %get-tuple-element.16.refs_0_), channel_id=1, source_target_pairs={{0,8},{1,9},{2,10},{3,11},{4,12},{5,13},{6,14},{7,15},{8,0},{9,1},... | collective-permute-start | bytes 491528 | tf_op jit(solution)/shard_map/ppermute | solution.py:40
  27.5 3.8 %collective-permute-done.3.refs_1_ = bf16[640,128]{1,0:T(8,128)(2,1)S(1)} collective-permute-done((bf16[640,128]{1,0:T(8,128)(2,1)S(1)}, bf16[640,128]{1,0:T(8,128)(2,1)S(1)}, u32[]{:S(2)}, u32[]{:S(2)}) %collective-permute-start.3) | collective-permute-done | bytes 163872 | tf_op jit(solution)/shard_map/ppermute | solution.py:40
  31.3 0.3 stage.7
  31.6 2.6 %collective-permute-start.4 = (bf16[64,128]{1,0:T(8,128)(2,1)S(1)}, bf16[64,128]{1,0:T(8,128)(2,1)S(1)}, u32[]{:S(2)}, u32[]{:S(2)}) collective-permute-start(bf16[64,128]{1,0:T(8,128)(2,1)S(1)} %get-tuple-element.17.refs_0_), channel_id=1, source_target_pairs={{0,16},{1,17},{2,18},{3,19},{4,20},{5,21},{6,22},{7,23},{8,24},{9,... | collective-permute-start | bytes 49160 | tf_op jit(solution)/shard_map/ppermute | solution.py:40
  34.2 1.7 %early.1 = (f32[64,2048]{1,0:T(8,128)S(1)}, bf16[128,2048]{1,0:T(8,128)(2,1)S(1)}, bf16[128,2048]{1,0:T(8,128)(2,1)S(1)}) custom-call(f32[64,2048]{1,0:T(8,128)} %x_hbm.1, bf16[128,2048]{1,0:T(8,128)(2,1)} %s4_.1, bf16[128,2048]{1,0:T(8,128)(2,1)} %s3.1, bf16[128,2048]{1,0:T(8,128)(2,1)} %s2_.1, bf16[128,2048]{1,0:T(8,128)(2,1)} %s1_.1, ...), custom_call_target="tpu_custom_call" | custom-call | flops 67108864 | bytes 2883584 | tf_op jit(solution)/shard_map/early/pallas_call | solution.py:282
  35.9 0.2 middle.1.refs_3_
  36.1 0.2 collective-permute-done.4.refs_1_
  36.3 1.1 %last.1 = f32[64,2048]{1,0:T(8,128)} custom-call(bf16[64,128]{1,0:T(8,128)(2,1)S(1)} %get-tuple-element.17.refs_0_, bf16[64,128]{1,0:T(8,128)(2,1)S(1)} %collective-permute-done.4.refs_1_, bf16[256,128]{1,0:T(8,128)(2,1)S(1)} %get-tuple-element.18.refs_2_, f32[64,2048]{1,0:T(8,128)S(1)} %middle.1.refs_3_, bf16[128,2048]{1,0:T(8,128)(2,1)S(1)} %get-tuple-element.24.refs_4_), custom_call_target="tpu_custom_call" | custom-call | tf_op jit(solution)/shard_map/last/pallas_call | solution.py:306
Async XLA Ops:
  3.3 1.8 %collective-permute-start = (bf16[1264,128]{1,0:T(8,128)(2,1)S(1)}, bf16[1264,128]{1,0:T(8,128)(2,1)S(1)}, u32[]{:S(2)}, u32[]{:S(2)}) collective-permute-start(bf16[1264,128]{1,0:T(8,128)(2,1)S(1)} %products.1.refs_0_), channel_id=1, source_target_pairs={{0,1},{1,0},{2,3},{3,2},{4,5},{5,4},{6,7},{7,6},{8,9},{9,8},{10,11... | collective-permute-start | bytes 970760 | tf_op jit(solution)/shard_map/ppermute | solution.py:40
  5.2 12.2 %collective-permute-start.1 = (bf16[1504,128]{1,0:T(8,128)(2,1)S(1)}, bf16[1504,128]{1,0:T(8,128)(2,1)S(1)}, u32[]{:S(2)}, u32[]{:S(2)}) collective-permute-start(bf16[1504,128]{1,0:T(8,128)(2,1)S(1)} %stage.4.refs_0_), channel_id=1, source_target_pairs={{0,2},{1,3},{2,0},{3,1},{4,6},{5,7},{6,4},{7,5},{8,10},{9,11},{10,... | collective-permute-start | bytes 1155080 | tf_op jit(solution)/shard_map/ppermute | solution.py:40
  17.7 7.9 %collective-permute-start.2 = (bf16[1024,128]{1,0:T(8,128)(2,1)S(1)}, bf16[1024,128]{1,0:T(8,128)(2,1)S(1)}, u32[]{:S(2)}, u32[]{:S(2)}) collective-permute-start(bf16[1024,128]{1,0:T(8,128)(2,1)S(1)} %get-tuple-element.15.refs_0_), channel_id=1, source_target_pairs={{0,4},{1,5},{2,6},{3,7},{4,0},{5,1},{6,2},{7,3},{8,12},{9,13},{10,... | collective-permute-start | bytes 786440 | tf_op jit(solution)/shard_map/ppermute | solution.py:40
  25.9 5.4 %collective-permute-start.3 = (bf16[640,128]{1,0:T(8,128)(2,1)S(1)}, bf16[640,128]{1,0:T(8,128)(2,1)S(1)}, u32[]{:S(2)}, u32[]{:S(2)}) collective-permute-start(bf16[640,128]{1,0:T(8,128)(2,1)S(1)} %get-tuple-element.16.refs_0_), channel_id=1, source_target_pairs={{0,8},{1,9},{2,10},{3,11},{4,12},{5,13},{6,14},{7,15},{8,0},{9,1},... | collective-permute-start | bytes 491528 | tf_op jit(solution)/shard_map/ppermute | solution.py:40
  31.6 4.7 %collective-permute-start.4 = (bf16[64,128]{1,0:T(8,128)(2,1)S(1)}, bf16[64,128]{1,0:T(8,128)(2,1)S(1)}, u32[]{:S(2)}, u32[]{:S(2)}) collective-permute-start(bf16[64,128]{1,0:T(8,128)(2,1)S(1)} %get-tuple-element.17.refs_0_), channel_id=1, source_target_pairs={{0,16},{1,17},{2,18},{3,19},{4,20},{5,21},{6,22},{7,23},{8,24},{9,... | collective-permute-start | bytes 49160 | tf_op jit(solution)/shard_map/ppermute | solution.py:40

commit v4 on v3

v4 whole, which is shorter than its diff:
```python
import functools

import jax
import jax.numpy as jnp
from jax import lax
from jax.experimental import pallas as pl
from jax.experimental.pallas import tpu as pltpu
from jax.sharding import PartitionSpec as P

BF = jnp.bfloat16
F32 = jnp.float32
LEVELS = (4, 3, 2, 1)
VMEM = pl.BlockSpec(memory_space=pltpu.VMEM)
HBM = pl.BlockSpec(memory_space=pltpu.HBM)
CHUNKS_IN = 2
CHUNKS_OUT = 4


def nn(a, b):
    return lax.dot_general(a, b, (((1,), (0,)), ((), ())), preferred_element_type=F32)


def nt(a, b):
    return lax.dot_general(a, b, (((1,), (1,)), ((), ())), preferred_element_type=F32)


def spread(sizes):
    out, start = {}, 0
    for key, size in sizes.items():
        out[key] = (start, start + size)
        start += size
    return out, start


class Plan:
    def __init__(self, width, rank, rows):
        w, r = width, rank

        def start(scale):
            first = {("p", k): w for k in LEVELS}
            first.update({("g", 4, k): r for k in (3, 2, 1)})
            first.update({("c", k): 2 * scale * rows[k] for k in (4, 3)})
            second = {("g", l, k): r for l, k in ((3, 2), (3, 1), (2, 1))}
            second.update({("c", k): 2 * scale * rows[k] for k in (2, 1)})
            return spread(first), spread(second)

        self.device = start(1)
        self.child = start(2)
        self.after_4 = (
            spread({("p", 3): w, ("p", 2): w, ("p", 1): w, ("c", 3): 8 * rows[3]}),
            spread(
                {
                    **{("own", 3, k): r for k in (2, 1)},
                    **{("sib", 3, k): r for k in (2, 1)},
                    ("g", 2, 1): r,
                    **{("c", k, y): 4 * rows[k] for k in (2, 1) for y in (0, 1)},
                }
            ),
        )
        self.before_3 = (
            spread(
                {
                    **{(side, k): w for k in (3, 2, 1) for side in ("own", "sib")},
                    "w4": w,
                    ("own", "c"): 8 * rows[3],
                    ("sib", "c"): 8 * rows[3],
                }
            ),
            spread(
                {
                    **{("own", 3, k): r for k in (2, 1)},
                    **{("sib", 3, k): r for k in (2, 1)},
                    ("g", 2, 1): r,
                    **{("c", k): 16 * rows[k] for k in (2, 1)},
                }
            ),
        )
        self.after_3 = spread(
            {("p", 2): w, ("p", 1): w, ("g", 2, 1): r, **{("c", k): 16 * rows[k] for k in (2, 1)}}
        )

    @staticmethod
    def total(pair):
        return max(pair[0][1], pair[1][1])


def swap(x, even, odd):
    size = lax.axis_size("pts")
    return lax.ppermute(x, "pts", [(i, i ^ (1 << (odd if i & 1 else even))) for i in range(size)])


def index_bit(bit):
    return lax.axis_index("pts") >> bit & 1


def by_role(first, second):
    role = index_bit(0)
    pl.when(role == 0)(first)
    pl.when(role == 1)(second)


def first_kernel(spans, rank, width, chunks, in_kernel, x_hbm, *refs):
    b_hbm = dict(zip(("r1", "r2", "s4", "s3", "s2", "r3", "r4"), refs[:7]))
    c_hbm = dict(zip(LEVELS, refs[7:11])) if in_kernel else {}
    refs = refs[7 + len(c_hbm) :]
    keep, send, x_v, left_v, right_v, acc_lo, acc_hi, acc_2, sems, c_sem = refs[:10]
    c_v = dict(zip(LEVELS, refs[10:]))
    points = x_v.shape[1]
    cut = points // chunks
    place = {"s4": (left_v, width), "s3": (left_v, width + rank), "s2": (left_v, width + 2 * rank)}
    place.update({name: (right_v, i * rank) for i, name in enumerate(("r1", "r2", "r3", "r4"))})

    def piece(j, i, name):
        cols = pl.ds(j * cut, cut)
        if name == "x":
            return pltpu.make_async_copy(x_hbm.at[:, cols], x_v.at[:, cols], sems.at[j, i])
        ref, row = place[name]
        return pltpu.make_async_copy(b_hbm[name].at[:, cols], ref.at[pl.ds(row, rank), cols], sems.at[j, i])

    copies = [[piece(j, i, n) for i, n in enumerate(("x", *b_hbm))] for j in range(chunks)]
    c_copies = [pltpu.make_async_copy(c_hbm[k], c_v[k], c_sem.at[i]) for i, k in enumerate(c_hbm)]
    for copy in copies[0] + c_copies:
        copy.start()
    for group in copies[1:]:
        for copy in group:
            copy.start()

    def add(j, ref, value):
        ref[...] = value if j == 0 else ref[...] + value

    for j in range(chunks):
        for copy in copies[j]:
            copy.wait()
        cols = slice(j * cut, (j + 1) * cut)
        left_v[:width, cols] = x_v[:, cols].astype(BF)
        add(j, acc_lo, nt(left_v[: width + 2 * rank, cols], right_v[: 2 * rank, cols]))
        add(j, acc_hi, nt(left_v[: width + rank, cols], right_v[2 * rank :, cols]))
        add(j, acc_2, nt(left_v[width + 2 * rank :, cols], right_v[:rank, cols]))
    for copy in c_copies:
        copy.wait()

    def write(role_0, role_1):
        def put(key, value):
            for out, table in zip((role_0, role_1), spans):
                if key in table:
                    out[table[key][0] : table[key][1]] = value.astype(BF)

        for i in range(2):
            side = slice(i * rank, (i + 1) * rank)
            put(("p", 1 + i), acc_lo[:width, side])
            put(("p", 3 + i), acc_hi[:width, side])
            put(("g", 4, 1 + i), acc_lo[width : width + rank, side])
            put(("g", 3, 1 + i), acc_lo[width + rank :, side])
        put(("g", 4, 3), acc_hi[width:, :rank])
        put(("g", 2, 1), acc_2[...])
        for k, ref in c_v.items():
            c = ref[...]
            put(("c", k), jnp.concatenate([c[:, :rank], c[:, rank:]], axis=0))

    by_role(lambda: write(keep, send), lambda: write(send, keep))


def interleave(first, second):
    half = first.shape[0] // 2
    if half % 16:
        first, second = first.astype(F32), second.astype(F32)
    parts = [first[:half], second[:half], first[half:], second[half:]]
    return jnp.concatenate(parts, axis=0).astype(BF)


def ordered(own, other, upper):
    return jnp.where(upper, other, own), jnp.where(upper, own, other)


def plus(a, z):
    return (a.astype(F32) + z.astype(F32)).astype(BF)


def merge_kernel(plan, keep, got, out):
    def merge(role):
        for key, (lo, hi) in plan.device[role][0].items():
            a, z = keep[lo:hi], got[lo:hi]
            if key[0] == "c":
                value = interleave(z, a) if role else interleave(a, z)
            else:
                value = plus(a, z)
            lo, hi = plan.child[role][0][key]
            out[lo:hi] = value

    by_role(lambda: merge(0), lambda: merge(1))


def solve(stacked, own_rows, sib_rows, rank):
    sides = [jnp.concatenate([c[:rank], c[rank:]], axis=1) for c in (own_rows, sib_rows)]
    return nt(stacked, jnp.concatenate(sides, axis=0)).astype(BF)


def effect(weights, own_gram, sib_gram):
    gram = [jnp.concatenate([a, z], axis=0) for a, z in zip(own_gram, sib_gram)]
    return nn(weights, jnp.concatenate(gram, axis=1))


def kernel_4(plan, bits, rank, own, got, out, w4):
    def first():
        spans, then = plan.child[0][0], plan.after_4[0][0]

        def both(key):
            lo, hi = spans[key]
            return own[lo:hi], got[lo:hi]

        upper = index_bit(bits - 4) == 1
        stacked = jnp.concatenate(ordered(*both(("p", 4)), upper), axis=1)
        w = solve(stacked, *both(("c", 4)), rank)
        w4[...] = w[:, :rank]
        below = (3, 2, 1)
        pairs = [both(("g", 4, k)) for k in below]
        change = effect(w, [p[0] for p in pairs], [p[1] for p in pairs])
        for i, k in enumerate(below):
            a, z = both(("p", k))
            lo, hi = then[("p", k)]
            out[lo:hi] = (a.astype(F32) + z.astype(F32) - change[:, i * rank : (i + 1) * rank]).astype(BF)
        lo, hi = then[("c", 3)]
        out[lo:hi] = interleave(*ordered(*both(("c", 3)), upper))

    def second():
        spans, then = plan.child[1][0], plan.after_4[1][0]
        upper = index_bit(bits - 3) == 1

        def put(key, value):
            out[then[key][0] : then[key][1]] = value

        for key, (lo, hi) in spans.items():
            a, z = own[lo:hi], got[lo:hi]
            if key[0] == "c":
                for y, value in enumerate(ordered(a, z, upper)):
                    put(("c", key[1], y), value)
            elif key[1] == 3:
                put(("own", *key[1:]), a)
                put(("sib", *key[1:]), z)
            else:
                put(key, plus(a, z))
        w4[...] = jnp.zeros_like(w4)

    by_role(first, second)


def gather_kernel(plan, bits, own, got, w4, out):
    def first():
        spans, then = plan.after_4[0][0], plan.before_3[0][0]
        for key, (lo, hi) in spans.items():
            for side, ref in (("own", own), ("sib", got)):
                to = then[(side, "c" if key[0] == "c" else key[1])]
                out[to[0] : to[1]] = ref[lo:hi]
        out[then["w4"][0] : then["w4"][1]] = w4[...]

    def second():
        spans, then = plan.after_4[1][0], plan.before_3[1][0]
        upper = index_bit(bits - 4) == 1
        for key, (lo, hi) in spans.items():
            if key[0] != "c":
                to = then[key]
                out[to[0] : to[1]] = plus(own[lo:hi], got[lo:hi])
        for k in (2, 1):
            rows = []
            for y in (0, 1):
                lo, hi = spans[("c", k, y)]
                rows.append(interleave(*ordered(own[lo:hi], got[lo:hi], upper)))
            to = then[("c", k)]
            out[to[0] : to[1]] = interleave(*rows)

    by_role(first, second)


def kernel_3(plan, bits, rank, own, got, out, w4, w3):
    def run(a_ref, b_ref):
        a_spans, b_spans, then = plan.before_3[0][0], plan.before_3[1][0], plan.after_3[0]

        def a(key):
            return a_ref[a_spans[key][0] : a_spans[key][1]]

        def b(key):
            return b_ref[b_spans[key][0] : b_spans[key][1]]

        def put(key, value):
            out[then[key][0] : then[key][1]] = value

        upper = index_bit(bits - 3) == 1
        stacked = jnp.concatenate(ordered(a(("own", 3)), a(("sib", 3)), upper), axis=1)
        w = solve(stacked, a(("own", "c")), a(("sib", "c")), rank)
        w3[...] = w[:, :rank]
        w4[...] = a("w4")
        below = (2, 1)
        change = effect(w, [b(("own", 3, k)) for k in below], [b(("sib", 3, k)) for k in below])
        for i, k in enumerate(below):
            total = a(("own", k)).astype(F32) + a(("sib", k)).astype(F32)
            put(("p", k), (total - change[:, i * rank : (i + 1) * rank]).astype(BF))
        for key in (("g", 2, 1), ("c", 2), ("c", 1)):
            put(key, b(key))

    by_role(lambda: run(own, got), lambda: run(got, own))


def kernel_2(plan, bits, rank, own, got, out, w2, last):
    spans = plan.after_3[0]

    def both(key):
        lo, hi = spans[key]
        return own[lo:hi], got[lo:hi]

    upper = index_bit(bits - 2) == 1
    w = solve(jnp.concatenate(ordered(*both(("p", 2)), upper), axis=1), *both(("c", 2)), rank)
    w2[...] = w[:, :rank]
    a, z = both(("p", 1))
    gram = both(("g", 2, 1))
    out[...] = (a.astype(F32) + z.astype(F32) - effect(w, gram[:1], gram[1:])).astype(BF)
    last[...] = interleave(*ordered(*both(("c", 1)), upper))


def early_kernel(x_hbm, s4, s3, s2, s1, w4, w3, rest, s2_out, s1_out, s_v, sems):
    rank = s4.shape[0]
    pairs = ((x_hbm, rest), (s4, s_v.at[:rank]), (s3, s_v.at[rank:]), (s2, s2_out), (s1, s1_out))
    copies = [pltpu.make_async_copy(a, z, sems.at[i]) for i, (a, z) in enumerate(pairs)]
    for copy in copies:
        copy.start()
    for copy in copies[:3]:
        copy.wait()
    rest[...] -= nn(jnp.concatenate([w4[...], w3[...]], axis=1), s_v[...])
    for copy in copies[3:]:
        copy.wait()


def middle_kernel(rest, s2, w2, out):
    out[...] = rest[...] - nn(w2[...], s2[...])


def last_kernel(bits, chunks, own, got, coupling, rest, s1, out_hbm, out_v, sems):
    upper = index_bit(bits - 1) == 1
    rank = coupling.shape[0] // 2
    a, z, c = own[...], got[...], coupling[...]
    stacked = jnp.concatenate(ordered(a, z, upper), axis=1)
    weights = nt(stacked, jnp.concatenate([c[:rank], c[rank:]], axis=1)).astype(BF)
    cut = rest.shape[1] // chunks
    copies = []
    for j in range(chunks):
        cols = slice(j * cut, (j + 1) * cut)
        out_v[:, cols] = rest[:, cols] - nn(weights, s1[:, cols])
        span = pl.ds(j * cut, cut)
        copies.append(pltpu.make_async_copy(out_v.at[:, span], out_hbm.at[:, span], sems.at[j]))
        copies[-1].start()
    for copy in copies:
        copy.wait()


def on_device(right_solved, s1, s2, s3, s4, r1, r2, r3, r4, c1, c2, c3, c4):
    coupling = {1: c1, 2: c2, 3: c3, 4: c4}
    rank, points = s1.shape
    width = right_solved.shape[0]
    bits = lax.axis_size("pts").bit_length() - 1
    params = pltpu.CompilerParams(vmem_limit_bytes=24 * 2**20)

    def stay(x):
        return pltpu.with_memory_space_constraint(x, pltpu.HBM)

    def cost(flops, moved):
        return pl.CostEstimate(flops=flops, bytes_accessed=moved, transcendentals=0)

    def vmem_call(kernel, operands, shapes, name, **more):
        return pl.pallas_call(
            kernel,
            out_shape=shapes,
            in_specs=[VMEM] * len(operands),
            out_specs=[VMEM] * len(shapes),
            compiler_params=params,
            name=name,
            **more,
        )(*operands)

    def buffer(size):
        return jax.ShapeDtypeStruct((size, rank), BF)

    child_bits = bits - 4
    rows = {k: coupling[k].shape[0] for k in LEVELS}
    in_kernel = child_bits == 1 and all(rows[k] % 8 == 0 for k in LEVELS)
    if not in_kernel:
        rows = {k: rows[k] << child_bits - 1 for k in LEVELS}
    plan = Plan(width, rank, rows)
    device = plan.device
    if not in_kernel:
        device = tuple(spread({k: z - a for k, (a, z) in t.items() if k[0] != "c"}) for t, _ in device)
    operands = [right_solved, r1, r2, s4, s3, s2, r3, r4]
    if in_kernel:
        operands += [coupling[k] for k in LEVELS]
    chunks = CHUNKS_IN
    keep, send = pl.pallas_call(
        lambda *refs: first_kernel([t for t, _ in device], rank, width, chunks, in_kernel, *refs),
        out_shape=[buffer(Plan.total(device))] * 2,
        in_specs=[HBM] * len(operands),
        out_specs=[VMEM] * 2,
        scratch_shapes=[
            pltpu.VMEM((width, points), F32),
            pltpu.VMEM((width + 3 * rank, points), BF),
            pltpu.VMEM((4 * rank, points), BF),
            pltpu.VMEM((width + 2 * rank, 2 * rank), F32),
            pltpu.VMEM((width + rank, 2 * rank), F32),
            pltpu.VMEM((rank, rank), F32),
            pltpu.SemaphoreType.DMA((chunks, 8)),
            pltpu.SemaphoreType.DMA((4,)),
        ]
        + ([pltpu.VMEM(coupling[k].shape, F32) for k in LEVELS] if in_kernel else []),
        compiler_params=params,
        name="products",
    )(*[stay(x) for x in operands])

    size = Plan.total(plan.child)
    if in_kernel:
        got = swap(send, 0, 0)
        (buf,) = vmem_call(functools.partial(merge_kernel, plan), (keep, got), [buffer(size)], "merge")
    else:
        both = jnp.stack([keep, send])
        parts = {k: jnp.stack([c[:, :rank], c[:, rank:]]).astype(BF) for k, c in coupling.items()}
        both = plus(both, swap(both[::-1], 0, 0))
        both = jnp.where(index_bit(0) == 1, both[::-1], both)
        for bit in range(child_bits):
            if bit:
                both = plus(both, swap(both, bit, bit))
            upper = index_bit(bit) == 1
            for k in LEVELS:
                got = swap(parts[k], bit, bit)
                parts[k] = jnp.concatenate(ordered(parts[k], got, upper), axis=1)
        shares = []
        for role in (0, 1):
            share = [both[role, : device[role][1]]]
            share += [parts[k].reshape(-1, rank) for k in ((4, 3), (2, 1))[role]]
            share = jnp.concatenate(share, axis=0)
            shares.append(jnp.pad(share, ((0, size - share.shape[0]), (0, 0))))
        buf = jnp.where(index_bit(0) == 1, shares[1], shares[0])

    weight = jax.ShapeDtypeStruct((width, rank), BF)
    got = swap(buf, bits - 4, bits - 3)
    shapes = [buffer(Plan.total(plan.after_4)), weight]
    buf, w4 = vmem_call(functools.partial(kernel_4, plan, bits, rank), (buf, got), shapes, "level_4")
    got = swap(buf, bits - 3, bits - 4)
    shapes = [buffer(Plan.total(plan.before_3))]
    (buf,) = vmem_call(functools.partial(gather_kernel, plan, bits), (buf, got, w4), shapes, "gather")
    got = swap(buf, 0, 0)
    shapes = [buffer(plan.after_3[1]), weight, weight]
    buf, w4, w3 = vmem_call(functools.partial(kernel_3, plan, bits, rank), (buf, got), shapes, "level_3")

    wide = jax.ShapeDtypeStruct((width, points), F32)
    rest, s2_v, s1_v = pl.pallas_call(
        early_kernel,
        out_shape=[wide] + [jax.ShapeDtypeStruct((rank, points), BF)] * 2,
        in_specs=[HBM] * 5 + [VMEM] * 2,
        out_specs=[VMEM] * 3,
        scratch_shapes=[pltpu.VMEM((2 * rank, points), BF), pltpu.SemaphoreType.DMA((5,))],
        compiler_params=params,
        cost_estimate=cost(4 * width * rank * points, 6 * width * points + 8 * rank * points),
        name="early",
    )(*[stay(x) for x in (right_solved, s4, s3, s2, s1)], w4, w3)

    got = swap(buf, bits - 2, bits - 2)
    shapes = [buffer(width), weight, buffer(2 * rank)]
    buf, w2, last = vmem_call(functools.partial(kernel_2, plan, bits, rank), (buf, got), shapes, "level_2")
    (rest,) = vmem_call(
        middle_kernel,
        (rest, s2_v, w2),
        [wide],
        "middle",
        cost_estimate=cost(2 * width * rank * points, 8 * width * points),
    )
    got = swap(buf, bits - 1, bits - 1)
    chunks = CHUNKS_OUT
    return pl.pallas_call(
        functools.partial(last_kernel, bits, chunks),
        out_shape=wide,
        in_specs=[VMEM] * 5,
        out_specs=HBM,
        scratch_shapes=[pltpu.VMEM(wide.shape, F32), pltpu.SemaphoreType.DMA((chunks,))],
        compiler_params=params,
        name="last",
    )(buf, got, last, rest, s1_v)


def solution(mesh):
    wide, tall = P(None, "pts"), P("pts", None)
    return jax.shard_map(
        on_device, mesh=mesh, in_specs=(wide,) * 9 + (tall,) * 4, out_specs=wide, check_vma=False
    )
```

time: 37.6 us -> 33.2 us (0.88)
  waiting for transfers between devices: 20.5 us -> 15.3 us
  starting transfers between devices: 9.44 us -> 10.6 us
    ppermute x5 -> x6, waiting for transfers between devices: 20.5 us -> 15.3 us  [swap(): lax.ppermute(x, 'pts', [(i, i ^ 1 << (odd if i & 1 else even)) for i in r...]
    ppermute x5 -> x6, starting transfers between devices: 9.44 us -> 10.6 us  [swap(): lax.ppermute(x, 'pts', [(i, i ^ 1 << (odd if i & 1 else even)) for i in r...]
    pallas_call x8 -> x9, Pallas kernels: 7.38 us -> 7.06 us  [the longest x1 2.98 us: on_device(): pl.pallas_call(lambda *refs: first_kernel([t for t, _ in device], rank, w...]
  transfers between devices with their start and end apart: 5 -> 6, of which waited for: 5 -> 5; matrix products, arithmetic and copies ran while one was open for 0% -> 0% of each run, Pallas kernels for 5% -> 6%
where the time goes in v4:
time: 33.2 us; the launch traced here: 33 us
  waiting for transfers between devices  15.3 us (46%)
  starting transfers between devices  10.6 us (32%)
  Pallas kernels  7.06 us (21%)
    ppermute x6, waiting for transfers between devices, swap(): lax.ppermute(x, 'pts', [(i, i ^ 1 << (odd if i & 1 else even)) for i in r...  15.3 us
    ppermute x6, starting transfers between devices, swap(): lax.ppermute(x, 'pts', [(i, i ^ 1 << (odd if i & 1 else even)) for i in r...  10.6 us
    pallas_call x1, Pallas kernels, on_device(): pl.pallas_call(lambda *refs: first_kernel([t for t, _ in device], rank, w...  2.98 us
    pallas_call x1, Pallas kernels, on_device(): pl.pallas_call(early_kernel, out_shape=[wide] + [jax.ShapeDtypeStruct((ra...  1.71 us
    pallas_call x6, Pallas kernels, vmem_call(): pl.pallas_call(kernel, out_shape=shapes, in_specs=[VMEM] * len(operands),...  1.23 us
    pallas_call x1, Pallas kernels, on_device(): pl.pallas_call(functools.partial(last_kernel, bits, chunks), out_shape=wi...  1.13 us
  transfers between devices with their start and end apart: 6, of which 5 were waited for; matrix products, arithmetic and copies ran while one was open for 0% of the time, Pallas kernels for 6%

profile of v4, /device:TPU:0, one launch (start us, length us, event | category | flops | bytes accessed | tf_op | source)
XLA Modules:
  0.0 33.0 jit_solution(10754747631465601980)
XLA Ops:
  0.0 3.0 %products.1 = (bf16[832,128]{1,0:T(8,128)(2,1)S(1)}, bf16[832,128]{1,0:T(8,128)(2,1)S(1)}) custom-call(f32[64,2048]{1,0:T(8,128)} %x_hbm.1, bf16[128,2048]{1,0:T(8,128)(2,1)} %refs_1_.1, bf16[128,2048]{1,0:T(8,128)(2,1)} %refs_2_.1, bf16[128,2048]{1,0:T(8,128)(2,1)} %s4_.1, bf16[128,2048]{1,0:T(8,128)(2,1)} %s3.1, bf16[128,2048]{1,0:T(8,128)(2,1)} %s2_.1, ...), custom_call_target="tpu_custom_call" | custom-call | tf_op jit(solution)/shard_map/products/pallas_call | solution.py:394
  3.0 0.5 %collective-permute-start = (bf16[832,128]{1,0:T(8,128)(2,1)S(1)}, bf16[832,128]{1,0:T(8,128)(2,1)S(1)}, u32[]{:S(2)}, u32[]{:S(2)}) collective-permute-start(bf16[832,128]{1,0:T(8,128)(2,1)S(1)} %get-tuple-element.19), channel_id=1, source_target_pairs={{0,1},{1,0},{2,3},{3,2},{4,5},{5,4},{6,7},{7,6},{8,9},{9,8},{10,11... | collective-permute-start | bytes 638984 | tf_op jit(solution)/shard_map/ppermute | solution.py:89
  3.5 1.1 %collective-permute-done.got = bf16[832,128]{1,0:T(8,128)(2,1)S(1)} collective-permute-done((bf16[832,128]{1,0:T(8,128)(2,1)S(1)}, bf16[832,128]{1,0:T(8,128)(2,1)S(1)}, u32[]{:S(2)}, u32[]{:S(2)}) %collective-permute-start) | collective-permute-done | bytes 213024 | tf_op jit(solution)/shard_map/ppermute | solution.py:89
  4.6 2.9 %collective-permute-start.1 = (bf16[1024,128]{1,0:T(8,128)(2,1)S(1)}, bf16[1024,128]{1,0:T(8,128)(2,1)S(1)}, u32[]{:S(2)}, u32[]{:S(2)}) collective-permute-start(bf16[1024,128]{1,0:T(8,128)(2,1)S(1)} %merge.1.own), channel_id=1, source_target_pairs={{0,2},{1,5},{2,0},{3,7},{4,6},{5,1},{6,4},{7,3},{8,10},{9,13},{10,... | collective-permute-start | bytes 786440 | tf_op jit(solution)/shard_map/ppermute | solution.py:89
  7.6 4.4 %collective-permute-done.1.got = bf16[1024,128]{1,0:T(8,128)(2,1)S(1)} collective-permute-done((bf16[1024,128]{1,0:T(8,128)(2,1)S(1)}, bf16[1024,128]{1,0:T(8,128)(2,1)S(1)}, u32[]{:S(2)}, u32[]{:S(2)}) %collective-permute-start.1) | collective-permute-done | bytes 262176 | tf_op jit(solution)/shard_map/ppermute | solution.py:89
  11.9 0.3 %level_4.1 = (bf16[832,128]{1,0:T(8,128)(2,1)S(1)}, bf16[64,128]{1,0:T(8,128)(2,1)S(1)}) custom-call(bf16[1024,128]{1,0:T(8,128)(2,1)S(1)} %merge.1.own, bf16[1024,128]{1,0:T(8,128)(2,1)S(1)} %collective-permute-done.1.got), custom_call_target="tpu_custom_call" | custom-call | tf_op jit(solution)/shard_map/level_4/pallas_call | solution.py:368
  12.3 2.1 %collective-permute-start.2 = (bf16[832,128]{1,0:T(8,128)(2,1)S(1)}, bf16[832,128]{1,0:T(8,128)(2,1)S(1)}, u32[]{:S(2)}, u32[]{:S(2)}) collective-permute-start(bf16[832,128]{1,0:T(8,128)(2,1)S(1)} %get-tuple-element.20.own), channel_id=1, source_target_pairs={{0,4},{1,3},{2,6},{3,1},{4,0},{5,7},{6,2},{7,5},{8,12},{9,11},{10,... | collective-permute-start | bytes 638984 | tf_op jit(solution)/shard_map/ppermute | solution.py:89
  14.4 3.8 %collective-permute-done.2.got = bf16[832,128]{1,0:T(8,128)(2,1)S(1)} collective-permute-done((bf16[832,128]{1,0:T(8,128)(2,1)S(1)}, bf16[832,128]{1,0:T(8,128)(2,1)S(1)}, u32[]{:S(2)}, u32[]{:S(2)}) %collective-permute-start.2) | collective-permute-done | bytes 213024 | tf_op jit(solution)/shard_map/ppermute | solution.py:89
  18.2 0.1 collective-permute-start.3
  18.3 1.5 %collective-permute-done.3.got = bf16[1024,128]{1,0:T(8,128)(2,1)S(1)} collective-permute-done((bf16[1024,128]{1,0:T(8,128)(2,1)S(1)}, bf16[1024,128]{1,0:T(8,128)(2,1)S(1)}, u32[]{:S(2)}, u32[]{:S(2)}) %collective-permute-start.3) | collective-permute-done | bytes 262176 | tf_op jit(solution)/shard_map/ppermute | solution.py:89
  19.8 0.3 level_3.1
  20.2 2.1 %collective-permute-start.4 = (bf16[640,128]{1,0:T(8,128)(2,1)S(1)}, bf16[640,128]{1,0:T(8,128)(2,1)S(1)}, u32[]{:S(2)}, u32[]{:S(2)}) collective-permute-start(bf16[640,128]{1,0:T(8,128)(2,1)S(1)} %get-tuple-element.22.own), channel_id=1, source_target_pairs={{0,8},{1,9},{2,10},{3,11},{4,12},{5,13},{6,14},{7,15},{8,0},{9,1},... | collective-permute-start | bytes 491528 | tf_op jit(solution)/shard_map/ppermute | solution.py:89
  22.3 4.5 %collective-permute-done.4.got = bf16[640,128]{1,0:T(8,128)(2,1)S(1)} collective-permute-done((bf16[640,128]{1,0:T(8,128)(2,1)S(1)}, bf16[640,128]{1,0:T(8,128)(2,1)S(1)}, u32[]{:S(2)}, u32[]{:S(2)}) %collective-permute-start.4) | collective-permute-done | bytes 163872 | tf_op jit(solution)/shard_map/ppermute | solution.py:89
  26.8 0.3 level_2.1
  27.1 2.8 %collective-permute-start.5 = (bf16[64,128]{1,0:T(8,128)(2,1)S(1)}, bf16[64,128]{1,0:T(8,128)(2,1)S(1)}, u32[]{:S(2)}, u32[]{:S(2)}) collective-permute-start(bf16[64,128]{1,0:T(8,128)(2,1)S(1)} %get-tuple-element.23.own), channel_id=1, source_target_pairs={{0,16},{1,17},{2,18},{3,19},{4,20},{5,21},{6,22},{7,23},{8,24},{9,... | collective-permute-start | bytes 49160 | tf_op jit(solution)/shard_map/ppermute | solution.py:89
  29.9 1.7 %early.1 = (f32[64,2048]{1,0:T(8,128)S(1)}, bf16[128,2048]{1,0:T(8,128)(2,1)S(1)}, bf16[128,2048]{1,0:T(8,128)(2,1)S(1)}) custom-call(f32[64,2048]{1,0:T(8,128)} %x_hbm.1, bf16[128,2048]{1,0:T(8,128)(2,1)} %s4_.1, bf16[128,2048]{1,0:T(8,128)(2,1)} %s3.1, bf16[128,2048]{1,0:T(8,128)(2,1)} %s2_.1, bf16[128,2048]{1,0:T(8,128)(2,1)} %s1_.1, ...), custom_call_target="tpu_custom_call" | custom-call | flops 67108864 | bytes 2883584 | tf_op jit(solution)/shard_map/early/pallas_call | solution.py:450
  31.7 0.2 middle.1.rest
  31.9 0.0 collective-permute-done.5.got
  31.9 1.1 %last.1 = f32[64,2048]{1,0:T(8,128)} custom-call(bf16[64,128]{1,0:T(8,128)(2,1)S(1)} %get-tuple-element.23.own, bf16[64,128]{1,0:T(8,128)(2,1)S(1)} %collective-permute-done.5.got, bf16[256,128]{1,0:T(8,128)(2,1)S(1)} %get-tuple-element.24.coupling, f32[64,2048]{1,0:T(8,128)S(1)} %middle.1.rest, bf16[128,2048]{1,0:T(8,128)(2,1)S(1)} %get-tuple-element.30.s1), custom_call_target="tpu_custom_call" | custom-call | tf_op jit(solution)/shard_map/last/pallas_call | solution.py:473
  (2 shorter events, 0.1 us)
Async XLA Ops:
  3.0 1.6 %collective-permute-start = (bf16[832,128]{1,0:T(8,128)(2,1)S(1)}, bf16[832,128]{1,0:T(8,128)(2,1)S(1)}, u32[]{:S(2)}, u32[]{:S(2)}) collective-permute-start(bf16[832,128]{1,0:T(8,128)(2,1)S(1)} %get-tuple-element.19), channel_id=1, source_target_pairs={{0,1},{1,0},{2,3},{3,2},{4,5},{5,4},{6,7},{7,6},{8,9},{9,8},{10,11... | collective-permute-start | bytes 638984 | tf_op jit(solution)/shard_map/ppermute | solution.py:89
  4.6 7.3 %collective-permute-start.1 = (bf16[1024,128]{1,0:T(8,128)(2,1)S(1)}, bf16[1024,128]{1,0:T(8,128)(2,1)S(1)}, u32[]{:S(2)}, u32[]{:S(2)}) collective-permute-start(bf16[1024,128]{1,0:T(8,128)(2,1)S(1)} %merge.1.own), channel_id=1, source_target_pairs={{0,2},{1,5},{2,0},{3,7},{4,6},{5,1},{6,4},{7,3},{8,10},{9,13},{10,... | collective-permute-start | bytes 786440 | tf_op jit(solution)/shard_map/ppermute | solution.py:89
  12.3 5.9 %collective-permute-start.2 = (bf16[832,128]{1,0:T(8,128)(2,1)S(1)}, bf16[832,128]{1,0:T(8,128)(2,1)S(1)}, u32[]{:S(2)}, u32[]{:S(2)}) collective-permute-start(bf16[832,128]{1,0:T(8,128)(2,1)S(1)} %get-tuple-element.20.own), channel_id=1, source_target_pairs={{0,4},{1,3},{2,6},{3,1},{4,0},{5,7},{6,2},{7,5},{8,12},{9,11},{10,... | collective-permute-start | bytes 638984 | tf_op jit(solution)/shard_map/ppermute | solution.py:89
  18.2 1.6 %collective-permute-start.3 = (bf16[1024,128]{1,0:T(8,128)(2,1)S(1)}, bf16[1024,128]{1,0:T(8,128)(2,1)S(1)}, u32[]{:S(2)}, u32[]{:S(2)}) collective-permute-start(bf16[1024,128]{1,0:T(8,128)(2,1)S(1)} %gather.1.own), channel_id=1, source_target_pairs={{0,1},{1,0},{2,3},{3,2},{4,5},{5,4},{6,7},{7,6},{8,9},{9,8},{10,11... | collective-permute-start | bytes 786440 | tf_op jit(solution)/shard_map/ppermute | solution.py:89
  20.2 6.6 %collective-permute-start.4 = (bf16[640,128]{1,0:T(8,128)(2,1)S(1)}, bf16[640,128]{1,0:T(8,128)(2,1)S(1)}, u32[]{:S(2)}, u32[]{:S(2)}) collective-permute-start(bf16[640,128]{1,0:T(8,128)(2,1)S(1)} %get-tuple-element.22.own), channel_id=1, source_target_pairs={{0,8},{1,9},{2,10},{3,11},{4,12},{5,13},{6,14},{7,15},{8,0},{9,1},... | collective-permute-start | bytes 491528 | tf_op jit(solution)/shard_map/ppermute | solution.py:89
  27.1 4.8 %collective-permute-start.5 = (bf16[64,128]{1,0:T(8,128)(2,1)S(1)}, bf16[64,128]{1,0:T(8,128)(2,1)S(1)}, u32[]{:S(2)}, u32[]{:S(2)}) collective-permute-start(bf16[64,128]{1,0:T(8,128)(2,1)S(1)} %get-tuple-element.23.own), channel_id=1, source_target_pairs={{0,16},{1,17},{2,18},{3,19},{4,20},{5,21},{6,22},{7,23},{8,24},{9,... | collective-permute-start | bytes 49160 | tf_op jit(solution)/shard_map/ppermute | solution.py:89

commit v5 on v4

--- a/solution.py
+++ b/solution.py
@@ -22,6 +22,10 @@
 
 def nt(a, b):
     return lax.dot_general(a, b, (((1,), (1,)), ((), ())), preferred_element_type=F32)
+
+
+def tn(a, b):
+    return lax.dot_general(a, b, (((0,), (0,)), ((), ())), preferred_element_type=F32)
 
 
 def spread(sizes):
@@ -75,9 +79,7 @@
                 }
             ),
         )
-        self.after_3 = spread(
-            {("p", 2): w, ("p", 1): w, ("g", 2, 1): r, **{("c", k): 16 * rows[k] for k in (2, 1)}}
-        )
+        self.after_3 = spread({("p", 2): w, ("p", 1): w, "h": 2 * r, ("c", 1): 16 * rows[1]})
 
     @staticmethod
     def total(pair):
@@ -198,6 +200,10 @@
 def effect(weights, own_gram, sib_gram):
     gram = [jnp.concatenate([a, z], axis=0) for a, z in zip(own_gram, sib_gram)]
     return nn(weights, jnp.concatenate(gram, axis=1))
+
+
+def transfer(rows, gram, rank):
+    return jnp.concatenate([tn(rows[:rank], gram), tn(rows[rank:], gram)], axis=0)
 
 
 def kernel_4(plan, bits, rank, own, got, out, w4):
@@ -271,7 +277,7 @@
     by_role(first, second)
 
 
-def kernel_3(plan, bits, rank, own, got, out, w4, w3):
+def kernel_3(plan, bits, rank, own, got, out, w4, w3, c2):
     def run(a_ref, b_ref):
         a_spans, b_spans, then = plan.before_3[0][0], plan.before_3[1][0], plan.after_3[0]
 
@@ -294,13 +300,15 @@
         for i, k in enumerate(below):
             total = a(("own", k)).astype(F32) + a(("sib", k)).astype(F32)
             put(("p", k), (total - change[:, i * rank : (i + 1) * rank]).astype(BF))
-        for key in (("g", 2, 1), ("c", 2), ("c", 1)):
-            put(key, b(key))
+        put("h", transfer(b(("c", 2)), b(("g", 2, 1)), rank).astype(BF))
+        put(("c", 1), b(("c", 1)))
+        c2[...] = b(("c", 2))
 
     by_role(lambda: run(own, got), lambda: run(got, own))
 
 
-def kernel_2(plan, bits, rank, own, got, out, w2, last):
+def kernel_2(plan, bits, own, got, early, out, stacked_out, last):
+    del early
     spans = plan.after_3[0]
 
     def both(key):
@@ -308,11 +316,10 @@
         return own[lo:hi], got[lo:hi]
 
     upper = index_bit(bits - 2) == 1
-    w = solve(jnp.concatenate(ordered(*both(("p", 2)), upper), axis=1), *both(("c", 2)), rank)
-    w2[...] = w[:, :rank]
+    stacked = jnp.concatenate(ordered(*both(("p", 2)), upper), axis=1)
+    stacked_out[...] = stacked
     a, z = both(("p", 1))
-    gram = both(("g", 2, 1))
-    out[...] = (a.astype(F32) + z.astype(F32) - effect(w, gram[:1], gram[1:])).astype(BF)
+    out[...] = (a.astype(F32) + z.astype(F32) - nn(stacked, plus(*both("h")))).astype(BF)
     last[...] = interleave(*ordered(*both(("c", 1)), upper))
 
 
@@ -329,8 +336,10 @@
         copy.wait()
 
 
-def middle_kernel(rest, s2, w2, out):
-    out[...] = rest[...] - nn(w2[...], s2[...])
+def middle_kernel(rest, s2, stacked, rows, out):
+    rank = s2.shape[0]
+    weights = nt(stacked[...], jnp.concatenate([rows[:rank], rows[rank:]], axis=1)).astype(BF)
+    out[...] = rest[...] - nn(weights, s2[...])
 
 
 def last_kernel(bits, chunks, own, got, coupling, rest, s1, out_hbm, out_v, sems):
@@ -443,8 +452,8 @@
     shapes = [buffer(Plan.total(plan.before_3))]
     (buf,) = vmem_call(functools.partial(gather_kernel, plan, bits), (buf, got, w4), shapes, "gather")
     got = swap(buf, 0, 0)
-    shapes = [buffer(plan.after_3[1]), weight, weight]
-    buf, w4, w3 = vmem_call(functools.partial(kernel_3, plan, bits, rank), (buf, got), shapes, "level_3")
+    shapes = [buffer(plan.after_3[1]), weight, weight, buffer(2 * rank)]
+    buf, w4, w3, c2_v = vmem_call(functools.partial(kernel_3, plan, bits, rank), (buf, got), shapes, "level_3")
 
     wide = jax.ShapeDtypeStruct((width, points), F32)
     rest, s2_v, s1_v = pl.pallas_call(
@@ -459,11 +468,11 @@
     )(*[stay(x) for x in (right_solved, s4, s3, s2, s1)], w4, w3)
 
     got = swap(buf, bits - 2, bits - 2)
-    shapes = [buffer(width), weight, buffer(2 * rank)]
-    buf, w2, last = vmem_call(functools.partial(kernel_2, plan, bits, rank), (buf, got), shapes, "level_2")
+    shapes = [buffer(width), jax.ShapeDtypeStruct((width, 2 * rank), BF), buffer(2 * rank)]
+    buf, stacked, last = vmem_call(functools.partial(kernel_2, plan, bits), (buf, got, s1_v), shapes, "level_2")
     (rest,) = vmem_call(
         middle_kernel,
-        (rest, s2_v, w2),
+        (rest, s2_v, stacked, c2_v),
         [wide],
         "middle",
         cost_estimate=cost(2 * width * rank * points, 8 * width * points),

time: 33.2 us -> 32.2 us (0.970)
  waiting for transfers between devices: 15.3 us -> 14.4 us
    ppermute x6, waiting for transfers between devices: 15.3 us -> 14.4 us  [swap(): lax.ppermute(x, 'pts', [(i, i ^ 1 << (odd if i & 1 else even)) for i in r...]
  transfers between devices with their start and end apart: 6 -> 6, of which waited for: 5 -> 6; matrix products, arithmetic and copies ran while one was open for 0% -> 0% of each run, Pallas kernels for 6% -> 6%
where the time goes in v5:
time: 32.2 us; the launch traced here: 32.1 us
  waiting for transfers between devices  14.4 us (45%)
  starting transfers between devices  10.6 us (33%)
  Pallas kernels  7.08 us (22%)
    ppermute x6, waiting for transfers between devices, swap(): lax.ppermute(x, 'pts', [(i, i ^ 1 << (odd if i & 1 else even)) for i in r...  14.4 us
    ppermute x6, starting transfers between devices, swap(): lax.ppermute(x, 'pts', [(i, i ^ 1 << (odd if i & 1 else even)) for i in r...  10.6 us
    pallas_call x1, Pallas kernels, on_device(): pl.pallas_call(lambda *refs: first_kernel([t for t, _ in device], rank, w...  2.98 us
    pallas_call x1, Pallas kernels, on_device(): pl.pallas_call(early_kernel, out_shape=[wide] + [jax.ShapeDtypeStruct((ra...  1.71 us
    pallas_call x6, Pallas kernels, vmem_call(): pl.pallas_call(kernel, out_shape=shapes, in_specs=[VMEM] * len(operands),...  1.26 us
    pallas_call x1, Pallas kernels, on_device(): pl.pallas_call(functools.partial(last_kernel, bits, chunks), out_shape=wi...  1.12 us
  transfers between devices with their start and end apart: 6, of which 6 were waited for; matrix products, arithmetic and copies ran while one was open for 0% of the time, Pallas kernels for 6%

profile of v5, /device:TPU:0, one launch (start us, length us, event | category | flops | bytes accessed | tf_op | source)
XLA Modules:
  0.0 32.1 jit_solution(16079751133650487814)
XLA Ops:
  0.0 3.0 %products.1 = (bf16[832,128]{1,0:T(8,128)(2,1)S(1)}, bf16[832,128]{1,0:T(8,128)(2,1)S(1)}) custom-call(f32[64,2048]{1,0:T(8,128)} %x_hbm.1, bf16[128,2048]{1,0:T(8,128)(2,1)} %refs_1_.1, bf16[128,2048]{1,0:T(8,128)(2,1)} %refs_2_.1, bf16[128,2048]{1,0:T(8,128)(2,1)} %s4_.1, bf16[128,2048]{1,0:T(8,128)(2,1)} %s3.1, bf16[128,2048]{1,0:T(8,128)(2,1)} %s2_.1, ...), custom_call_target="tpu_custom_call" | custom-call | tf_op jit(solution)/shard_map/products/pallas_call | solution.py:403
  3.0 0.5 %collective-permute-start = (bf16[832,128]{1,0:T(8,128)(2,1)S(1)}, bf16[832,128]{1,0:T(8,128)(2,1)S(1)}, u32[]{:S(2)}, u32[]{:S(2)}) collective-permute-start(bf16[832,128]{1,0:T(8,128)(2,1)S(1)} %get-tuple-element.20), channel_id=1, source_target_pairs={{0,1},{1,0},{2,3},{3,2},{4,5},{5,4},{6,7},{7,6},{8,9},{9,8},{10,11... | collective-permute-start | bytes 638984 | tf_op jit(solution)/shard_map/ppermute | solution.py:91
  3.5 1.1 %collective-permute-done.got = bf16[832,128]{1,0:T(8,128)(2,1)S(1)} collective-permute-done((bf16[832,128]{1,0:T(8,128)(2,1)S(1)}, bf16[832,128]{1,0:T(8,128)(2,1)S(1)}, u32[]{:S(2)}, u32[]{:S(2)}) %collective-permute-start) | collective-permute-done | bytes 213024 | tf_op jit(solution)/shard_map/ppermute | solution.py:91
  4.6 2.9 %collective-permute-start.1 = (bf16[1024,128]{1,0:T(8,128)(2,1)S(1)}, bf16[1024,128]{1,0:T(8,128)(2,1)S(1)}, u32[]{:S(2)}, u32[]{:S(2)}) collective-permute-start(bf16[1024,128]{1,0:T(8,128)(2,1)S(1)} %merge.1.own), channel_id=1, source_target_pairs={{0,2},{1,5},{2,0},{3,7},{4,6},{5,1},{6,4},{7,3},{8,10},{9,13},{10,... | collective-permute-start | bytes 786440 | tf_op jit(solution)/shard_map/ppermute | solution.py:91
  7.6 4.4 %collective-permute-done.1.got = bf16[1024,128]{1,0:T(8,128)(2,1)S(1)} collective-permute-done((bf16[1024,128]{1,0:T(8,128)(2,1)S(1)}, bf16[1024,128]{1,0:T(8,128)(2,1)S(1)}, u32[]{:S(2)}, u32[]{:S(2)}) %collective-permute-start.1) | collective-permute-done | bytes 262176 | tf_op jit(solution)/shard_map/ppermute | solution.py:91
  11.9 0.3 %level_4.1 = (bf16[832,128]{1,0:T(8,128)(2,1)S(1)}, bf16[64,128]{1,0:T(8,128)(2,1)S(1)}) custom-call(bf16[1024,128]{1,0:T(8,128)(2,1)S(1)} %merge.1.own, bf16[1024,128]{1,0:T(8,128)(2,1)S(1)} %collective-permute-done.1.got), custom_call_target="tpu_custom_call" | custom-call | tf_op jit(solution)/shard_map/level_4/pallas_call | solution.py:377
  12.3 2.1 %collective-permute-start.2 = (bf16[832,128]{1,0:T(8,128)(2,1)S(1)}, bf16[832,128]{1,0:T(8,128)(2,1)S(1)}, u32[]{:S(2)}, u32[]{:S(2)}) collective-permute-start(bf16[832,128]{1,0:T(8,128)(2,1)S(1)} %get-tuple-element.21.own), channel_id=1, source_target_pairs={{0,4},{1,3},{2,6},{3,1},{4,0},{5,7},{6,2},{7,5},{8,12},{9,11},{10,... | collective-permute-start | bytes 638984 | tf_op jit(solution)/shard_map/ppermute | solution.py:91
  14.4 3.8 %collective-permute-done.2.got = bf16[832,128]{1,0:T(8,128)(2,1)S(1)} collective-permute-done((bf16[832,128]{1,0:T(8,128)(2,1)S(1)}, bf16[832,128]{1,0:T(8,128)(2,1)S(1)}, u32[]{:S(2)}, u32[]{:S(2)}) %collective-permute-start.2) | collective-permute-done | bytes 213024 | tf_op jit(solution)/shard_map/ppermute | solution.py:91
  18.2 0.1 collective-permute-start.3
  18.3 1.5 %collective-permute-done.3.got = bf16[1024,128]{1,0:T(8,128)(2,1)S(1)} collective-permute-done((bf16[1024,128]{1,0:T(8,128)(2,1)S(1)}, bf16[1024,128]{1,0:T(8,128)(2,1)S(1)}, u32[]{:S(2)}, u32[]{:S(2)}) %collective-permute-start.3) | collective-permute-done | bytes 262176 | tf_op jit(solution)/shard_map/ppermute | solution.py:91
  19.8 0.4 %level_3.1 = (bf16[512,128]{1,0:T(8,128)(2,1)S(1)}, bf16[64,128]{1,0:T(8,128)(2,1)S(1)}, bf16[64,128]{1,0:T(8,128)(2,1)S(1)}, bf16[256,128]{1,0:T(8,128)(2,1)S(1)}) custom-call(bf16[1024,128]{1,0:T(8,128)(2,1)S(1)} %gather.1.own, bf16[1024,128]{1,0:T(8,128)(2,1)S(1)} %collective-permute-done.3.got), custom_call_target="tpu_custom_call" | custom-call | tf_op jit(solution)/shard_map/level_3/pallas_call | solution.py:377
  20.2 2.1 %collective-permute-start.4 = (bf16[512,128]{1,0:T(8,128)(2,1)S(1)}, bf16[512,128]{1,0:T(8,128)(2,1)S(1)}, u32[]{:S(2)}, u32[]{:S(2)}) collective-permute-start(bf16[512,128]{1,0:T(8,128)(2,1)S(1)} %get-tuple-element.23.own), channel_id=1, source_target_pairs={{0,8},{1,9},{2,10},{3,11},{4,12},{5,13},{6,14},{7,15},{8,0},{9,1},... | collective-permute-start | bytes 393224 | tf_op jit(solution)/shard_map/ppermute | solution.py:91
  22.3 1.7 %early.1 = (f32[64,2048]{1,0:T(8,128)S(1)}, bf16[128,2048]{1,0:T(8,128)(2,1)S(1)}, bf16[128,2048]{1,0:T(8,128)(2,1)S(1)}) custom-call(f32[64,2048]{1,0:T(8,128)} %x_hbm.1, bf16[128,2048]{1,0:T(8,128)(2,1)} %s4_.1, bf16[128,2048]{1,0:T(8,128)(2,1)} %s3.1, bf16[128,2048]{1,0:T(8,128)(2,1)} %s2_.1, bf16[128,2048]{1,0:T(8,128)(2,1)} %s1_.1, ...), custom_call_target="tpu_custom_call" | custom-call | flops 67108864 | bytes 2883584 | tf_op jit(solution)/shard_map/early/pallas_call | solution.py:459
  24.1 2.1 %collective-permute-done.4.got = bf16[512,128]{1,0:T(8,128)(2,1)S(1)} collective-permute-done((bf16[512,128]{1,0:T(8,128)(2,1)S(1)}, bf16[512,128]{1,0:T(8,128)(2,1)S(1)}, u32[]{:S(2)}, u32[]{:S(2)}) %collective-permute-start.4) | collective-permute-done | bytes 131104 | tf_op jit(solution)/shard_map/ppermute | solution.py:91
  26.1 0.2 level_2.1
  26.3 2.8 %collective-permute-start.5 = (bf16[64,128]{1,0:T(8,128)(2,1)S(1)}, bf16[64,128]{1,0:T(8,128)(2,1)S(1)}, u32[]{:S(2)}, u32[]{:S(2)}) collective-permute-start(bf16[64,128]{1,0:T(8,128)(2,1)S(1)} %get-tuple-element.27.own), channel_id=1, source_target_pairs={{0,16},{1,17},{2,18},{3,19},{4,20},{5,21},{6,22},{7,23},{8,24},{9,... | collective-permute-start | bytes 49160 | tf_op jit(solution)/shard_map/ppermute | solution.py:91
  29.1 0.4 %middle.1.rest = f32[64,2048]{1,0:T(8,128)S(1)} custom-call(f32[64,2048]{1,0:T(8,128)S(1)} %get-tuple-element.29.rest, bf16[128,2048]{1,0:T(8,128)(2,1)S(1)} %get-tuple-element.30.s2, bf16[64,256]{1,0:T(8,128)(2,1)S(1)} %get-tuple-element.31.stacked, bf16[256,128]{1,0:T(8,128)(2,1)S(1)} %get-tuple-element.32.rows), custom_call_target="tpu_custom_call" | custom-call | flops 33554432 | bytes 1048576 | tf_op jit(solution)/shard_map/middle/pallas_call | solution.py:377
  29.4 1.5 %collective-permute-done.5.got = bf16[64,128]{1,0:T(8,128)(2,1)S(1)} collective-permute-done((bf16[64,128]{1,0:T(8,128)(2,1)S(1)}, bf16[64,128]{1,0:T(8,128)(2,1)S(1)}, u32[]{:S(2)}, u32[]{:S(2)}) %collective-permute-start.5) | collective-permute-done | bytes 16416 | tf_op jit(solution)/shard_map/ppermute | solution.py:91
  31.0 1.1 %last.1 = f32[64,2048]{1,0:T(8,128)} custom-call(bf16[64,128]{1,0:T(8,128)(2,1)S(1)} %get-tuple-element.27.own, bf16[64,128]{1,0:T(8,128)(2,1)S(1)} %collective-permute-done.5.got, bf16[256,128]{1,0:T(8,128)(2,1)S(1)} %get-tuple-element.28.coupling, f32[64,2048]{1,0:T(8,128)S(1)} %middle.1.rest, bf16[128,2048]{1,0:T(8,128)(2,1)S(1)} %get-tuple-element.26.early.s1), custom_call_target="tpu_custom_call" | custom-call | tf_op jit(solution)/shard_map/last/pallas_call | solution.py:482
  (2 shorter events, 0.1 us)
Async XLA Ops:
  3.0 1.6 %collective-permute-start = (bf16[832,128]{1,0:T(8,128)(2,1)S(1)}, bf16[832,128]{1,0:T(8,128)(2,1)S(1)}, u32[]{:S(2)}, u32[]{:S(2)}) collective-permute-start(bf16[832,128]{1,0:T(8,128)(2,1)S(1)} %get-tuple-element.20), channel_id=1, source_target_pairs={{0,1},{1,0},{2,3},{3,2},{4,5},{5,4},{6,7},{7,6},{8,9},{9,8},{10,11... | collective-permute-start | bytes 638984 | tf_op jit(solution)/shard_map/ppermute | solution.py:91
  4.6 7.3 %collective-permute-start.1 = (bf16[1024,128]{1,0:T(8,128)(2,1)S(1)}, bf16[1024,128]{1,0:T(8,128)(2,1)S(1)}, u32[]{:S(2)}, u32[]{:S(2)}) collective-permute-start(bf16[1024,128]{1,0:T(8,128)(2,1)S(1)} %merge.1.own), channel_id=1, source_target_pairs={{0,2},{1,5},{2,0},{3,7},{4,6},{5,1},{6,4},{7,3},{8,10},{9,13},{10,... | collective-permute-start | bytes 786440 | tf_op jit(solution)/shard_map/ppermute | solution.py:91
  12.3 5.9 %collective-permute-start.2 = (bf16[832,128]{1,0:T(8,128)(2,1)S(1)}, bf16[832,128]{1,0:T(8,128)(2,1)S(1)}, u32[]{:S(2)}, u32[]{:S(2)}) collective-permute-start(bf16[832,128]{1,0:T(8,128)(2,1)S(1)} %get-tuple-element.21.own), channel_id=1, source_target_pairs={{0,4},{1,3},{2,6},{3,1},{4,0},{5,7},{6,2},{7,5},{8,12},{9,11},{10,... | collective-permute-start | bytes 638984 | tf_op jit(solution)/shard_map/ppermute | solution.py:91
  18.2 1.6 %collective-permute-start.3 = (bf16[1024,128]{1,0:T(8,128)(2,1)S(1)}, bf16[1024,128]{1,0:T(8,128)(2,1)S(1)}, u32[]{:S(2)}, u32[]{:S(2)}) collective-permute-start(bf16[1024,128]{1,0:T(8,128)(2,1)S(1)} %gather.1.own), channel_id=1, source_target_pairs={{0,1},{1,0},{2,3},{3,2},{4,5},{5,4},{6,7},{7,6},{8,9},{9,8},{10,11... | collective-permute-start | bytes 786440 | tf_op jit(solution)/shard_map/ppermute | solution.py:91
  20.2 5.9 %collective-permute-start.4 = (bf16[512,128]{1,0:T(8,128)(2,1)S(1)}, bf16[512,128]{1,0:T(8,128)(2,1)S(1)}, u32[]{:S(2)}, u32[]{:S(2)}) collective-permute-start(bf16[512,128]{1,0:T(8,128)(2,1)S(1)} %get-tuple-element.23.own), channel_id=1, source_target_pairs={{0,8},{1,9},{2,10},{3,11},{4,12},{5,13},{6,14},{7,15},{8,0},{9,1},... | collective-permute-start | bytes 393224 | tf_op jit(solution)/shard_map/ppermute | solution.py:91
  26.3 4.7 %collective-permute-start.5 = (bf16[64,128]{1,0:T(8,128)(2,1)S(1)}, bf16[64,128]{1,0:T(8,128)(2,1)S(1)}, u32[]{:S(2)}, u32[]{:S(2)}) collective-permute-start(bf16[64,128]{1,0:T(8,128)(2,1)S(1)} %get-tuple-element.27.own), channel_id=1, source_target_pairs={{0,16},{1,17},{2,18},{3,19},{4,20},{5,21},{6,22},{7,23},{8,24},{9,... | collective-permute-start | bytes 49160 | tf_op jit(solution)/shard_map/ppermute | solution.py:91

commit v6 on v5

--- a/solution.py
+++ b/solution.py
@@ -10,9 +10,11 @@
 BF = jnp.bfloat16
 F32 = jnp.float32
 LEVELS = (4, 3, 2, 1)
+SHARES = ((4, 3, 1), (2,))
 VMEM = pl.BlockSpec(memory_space=pltpu.VMEM)
 HBM = pl.BlockSpec(memory_space=pltpu.HBM)
 CHUNKS_IN = 2
+PAD = 16
 CHUNKS_OUT = 4
 
 
@@ -43,21 +45,21 @@
         def start(scale):
             first = {("p", k): w for k in LEVELS}
             first.update({("g", 4, k): r for k in (3, 2, 1)})
-            first.update({("c", k): 2 * scale * rows[k] for k in (4, 3)})
+            first.update({("c", k): 2 * scale * rows[k] for k in SHARES[0]})
             second = {("g", l, k): r for l, k in ((3, 2), (3, 1), (2, 1))}
-            second.update({("c", k): 2 * scale * rows[k] for k in (2, 1)})
+            second.update({("c", k): 2 * scale * rows[k] for k in SHARES[1]})
             return spread(first), spread(second)
 
         self.device = start(1)
         self.child = start(2)
         self.after_4 = (
-            spread({("p", 3): w, ("p", 2): w, ("p", 1): w, ("c", 3): 8 * rows[3]}),
+            spread({("p", 3): w, ("p", 2): w, ("p", 1): w, ("c", 3): 8 * rows[3], ("c", 1): 8 * rows[1]}),
             spread(
                 {
                     **{("own", 3, k): r for k in (2, 1)},
                     **{("sib", 3, k): r for k in (2, 1)},
                     ("g", 2, 1): r,
-                    **{("c", k, y): 4 * rows[k] for k in (2, 1) for y in (0, 1)},
+                    **{("c", 2, y): 4 * rows[2] for y in (0, 1)},
                 }
             ),
         )
@@ -74,12 +76,11 @@
                 {
                     **{("own", 3, k): r for k in (2, 1)},
                     **{("sib", 3, k): r for k in (2, 1)},
-                    ("g", 2, 1): r,
-                    **{("c", k): 16 * rows[k] for k in (2, 1)},
+                    ("c", 2): 16 * rows[2],
                 }
             ),
         )
-        self.after_3 = spread({("p", 2): w, ("p", 1): w, "h": 2 * r, ("c", 1): 16 * rows[1]})
+        self.after_3 = spread({("p", 2): w, ("p", 1): w, "spare": PAD})
 
     @staticmethod
     def total(pair):
@@ -206,7 +207,9 @@
     return jnp.concatenate([tn(rows[:rank], gram), tn(rows[rank:], gram)], axis=0)
 
 
-def kernel_4(plan, bits, rank, own, got, out, w4):
+def kernel_4(plan, bits, rank, own, got, after, out, w4):
+    del after
+
     def first():
         spans, then = plan.child[0][0], plan.after_4[0][0]
 
@@ -225,8 +228,9 @@
             a, z = both(("p", k))
             lo, hi = then[("p", k)]
             out[lo:hi] = (a.astype(F32) + z.astype(F32) - change[:, i * rank : (i + 1) * rank]).astype(BF)
-        lo, hi = then[("c", 3)]
-        out[lo:hi] = interleave(*ordered(*both(("c", 3)), upper))
+        for k in (3, 1):
+            lo, hi = then[("c", k)]
+            out[lo:hi] = interleave(*ordered(*both(("c", k)), upper))
 
     def second():
         spans, then = plan.child[1][0], plan.after_4[1][0]
@@ -250,34 +254,75 @@
     by_role(first, second)
 
 
-def gather_kernel(plan, bits, own, got, w4, out):
+def gather_kernel(plan, bits, own, got, w4, out, gram):
     def first():
         spans, then = plan.after_4[0][0], plan.before_3[0][0]
         for key, (lo, hi) in spans.items():
-            for side, ref in (("own", own), ("sib", got)):
-                to = then[(side, "c" if key[0] == "c" else key[1])]
-                out[to[0] : to[1]] = ref[lo:hi]
+            if key != ("c", 1):
+                for side, ref in (("own", own), ("sib", got)):
+                    to = then[(side, "c" if key[0] == "c" else key[1])]
+                    out[to[0] : to[1]] = ref[lo:hi]
         out[then["w4"][0] : then["w4"][1]] = w4[...]
+        lo, hi = spans[("c", 1)]
+        gram[...] = interleave(*ordered(own[lo:hi], got[lo:hi], index_bit(bits - 3) == 1))
 
     def second():
         spans, then = plan.after_4[1][0], plan.before_3[1][0]
         upper = index_bit(bits - 4) == 1
         for key, (lo, hi) in spans.items():
             if key[0] != "c":
-                to = then[key]
-                out[to[0] : to[1]] = plus(own[lo:hi], got[lo:hi])
-        for k in (2, 1):
-            rows = []
-            for y in (0, 1):
-                lo, hi = spans[("c", k, y)]
-                rows.append(interleave(*ordered(own[lo:hi], got[lo:hi], upper)))
-            to = then[("c", k)]
-            out[to[0] : to[1]] = interleave(*rows)
+                value = plus(own[lo:hi], got[lo:hi])
+                if key in then:
+                    out[then[key][0] : then[key][1]] = value
+                else:
+                    gram[...] = value
+        rows = []
+        for y in (0, 1):
+            lo, hi = spans[("c", 2, y)]
+            rows.append(interleave(*ordered(own[lo:hi], got[lo:hi], upper)))
+        to = then[("c", 2)]
+        out[to[0] : to[1]] = interleave(*rows)
 
     by_role(first, second)
 
 
-def kernel_3(plan, bits, rank, own, got, out, w4, w3, c2):
+def early_z_kernel(plan, rank, own, gram, out):
+    def first():
+        out[:rank] = gram[...]
+        out[rank:] = jnp.zeros_like(gram)
+
+    def second():
+        lo, hi = plan.before_3[1][0][("c", 2)]
+        out[...] = transfer(own[lo:hi], gram[...], rank).astype(BF)
+
+    by_role(first, second)
+
+
+def meet_z_kernel(bits, rank, own, got, after, *outs):
+    del after
+    upper = index_bit(bits - 2) == 1
+
+    def put(value):
+        for out, rows in zip(outs, (value[:rank], value[rank:])):
+            out[...] = rows
+
+    def first():
+        put(interleave(*ordered(own[:rank], got[:rank], upper)))
+
+    def second():
+        put(plus(own[...], got[...]))
+
+    by_role(first, second)
+
+
+def shared(mine, other, role):
+    own, theirs = [jnp.concatenate([ref[...] for ref in refs], axis=0) for refs in (mine, other)]
+    return jnp.where(index_bit(0) == role, own, theirs)
+
+
+def kernel_3(plan, bits, rank, own, got, after, out, w4, w3, c2):
+    del after
+
     def run(a_ref, b_ref):
         a_spans, b_spans, then = plan.before_3[0][0], plan.before_3[1][0], plan.after_3[0]
 
@@ -293,6 +338,7 @@
         upper = index_bit(bits - 3) == 1
         stacked = jnp.concatenate(ordered(a(("own", 3)), a(("sib", 3)), upper), axis=1)
         w = solve(stacked, a(("own", "c")), a(("sib", "c")), rank)
+        put("spare", jnp.zeros((PAD, rank), BF))
         w3[...] = w[:, :rank]
         w4[...] = a("w4")
         below = (2, 1)
@@ -300,40 +346,38 @@
         for i, k in enumerate(below):
             total = a(("own", k)).astype(F32) + a(("sib", k)).astype(F32)
             put(("p", k), (total - change[:, i * rank : (i + 1) * rank]).astype(BF))
-        put("h", transfer(b(("c", 2)), b(("g", 2, 1)), rank).astype(BF))
-        put(("c", 1), b(("c", 1)))
         c2[...] = b(("c", 2))
 
     by_role(lambda: run(own, got), lambda: run(got, own))
 
 
-def kernel_2(plan, bits, own, got, early, out, stacked_out, last):
-    del early
+def kernel_2(plan, bits, own, got, m0, m1, o0, o1, out, stacked_out):
     spans = plan.after_3[0]
 
     def both(key):
         lo, hi = spans[key]
         return own[lo:hi], got[lo:hi]
 
-    upper = index_bit(bits - 2) == 1
-    stacked = jnp.concatenate(ordered(*both(("p", 2)), upper), axis=1)
+    stacked = jnp.concatenate(ordered(*both(("p", 2)), index_bit(bits - 2) == 1), axis=1)
     stacked_out[...] = stacked
+    effect_1 = shared((m0, m1), (o0, o1), 1)
     a, z = both(("p", 1))
-    out[...] = (a.astype(F32) + z.astype(F32) - nn(stacked, plus(*both("h")))).astype(BF)
-    last[...] = interleave(*ordered(*both(("c", 1)), upper))
-
-
-def early_kernel(x_hbm, s4, s3, s2, s1, w4, w3, rest, s2_out, s1_out, s_v, sems):
-    rank = s4.shape[0]
-    pairs = ((x_hbm, rest), (s4, s_v.at[:rank]), (s3, s_v.at[rank:]), (s2, s2_out), (s1, s1_out))
-    copies = [pltpu.make_async_copy(a, z, sems.at[i]) for i, (a, z) in enumerate(pairs)]
+    out[...] = (a.astype(F32) + z.astype(F32) - nn(stacked, effect_1)).astype(BF)
+
+
+def fetch_kernel(after, *refs):
+    del after
+    half = len(refs) // 2
+    sems = refs[-1]
+    copies = [pltpu.make_async_copy(a, z, sems.at[i]) for i, (a, z) in enumerate(zip(refs[:half], refs[half:-1]))]
     for copy in copies:
         copy.start()
-    for copy in copies[:3]:
+    for copy in copies:
         copy.wait()
-    rest[...] -= nn(jnp.concatenate([w4[...], w3[...]], axis=1), s_v[...])
-    for copy in copies[3:]:
-        copy.wait()
+
+
+def early_kernel(rest, s4, s3, w4, w3, out):
+    out[...] = rest[...] - nn(w4[...], s4[...]) - nn(w3[...], s3[...])
 
 
 def middle_kernel(rest, s2, stacked, rows, out):
@@ -342,10 +386,11 @@
     out[...] = rest[...] - nn(weights, s2[...])
 
 
-def last_kernel(bits, chunks, own, got, coupling, rest, s1, out_hbm, out_v, sems):
+def last_kernel(bits, chunks, own, got, m0, m1, o0, o1, rest, s1, out_hbm, out_v, sems):
     upper = index_bit(bits - 1) == 1
-    rank = coupling.shape[0] // 2
-    a, z, c = own[...], got[...], coupling[...]
+    rank = m0.shape[0]
+    a, z = own[...], got[...]
+    c = shared((m0, m1), (o0, o1), 0)
     stacked = jnp.concatenate(ordered(a, z, upper), axis=1)
     weights = nt(stacked, jnp.concatenate([c[:rank], c[rank:]], axis=1)).astype(BF)
     cut = rest.shape[1] // chunks
@@ -439,55 +484,56 @@
         shares = []
         for role in (0, 1):
             share = [both[role, : device[role][1]]]
-            share += [parts[k].reshape(-1, rank) for k in ((4, 3), (2, 1))[role]]
+            share += [parts[k].reshape(-1, rank) for k in SHARES[role]]
             share = jnp.concatenate(share, axis=0)
             shares.append(jnp.pad(share, ((0, size - share.shape[0]), (0, 0))))
         buf = jnp.where(index_bit(0) == 1, shares[1], shares[0])
 
     weight = jax.ShapeDtypeStruct((width, rank), BF)
+    wide = jax.ShapeDtypeStruct((width, points), F32)
+    base = jax.ShapeDtypeStruct((rank, points), BF)
     got = swap(buf, bits - 4, bits - 3)
+    rest, s4_v, s3_v, s2_v, s1_v = pl.pallas_call(
+        fetch_kernel,
+        out_shape=[wide] + [base] * 4,
+        in_specs=[VMEM] + [HBM] * 5,
+        out_specs=[VMEM] * 5,
+        scratch_shapes=[pltpu.SemaphoreType.DMA((5,))],
+        compiler_params=params,
+        cost_estimate=cost(0, 4 * width * points + 8 * rank * points),
+        name="fetch",
+    )(buf, *[stay(x) for x in (right_solved, s4, s3, s2, s1)])
     shapes = [buffer(Plan.total(plan.after_4)), weight]
-    buf, w4 = vmem_call(functools.partial(kernel_4, plan, bits, rank), (buf, got), shapes, "level_4")
+    buf, w4 = vmem_call(functools.partial(kernel_4, plan, bits, rank), (buf, got, s1_v), shapes, "level_4")
     got = swap(buf, bits - 3, bits - 4)
-    shapes = [buffer(Plan.total(plan.before_3))]
-    (buf,) = vmem_call(functools.partial(gather_kernel, plan, bits), (buf, got, w4), shapes, "gather")
+    shapes = [buffer(Plan.total(plan.before_3)), buffer(rank)]
+    buf, gram = vmem_call(functools.partial(gather_kernel, plan, bits), (buf, got, w4), shapes, "gather")
     got = swap(buf, 0, 0)
+    (own_z,) = vmem_call(functools.partial(early_z_kernel, plan, rank), (buf, gram), [buffer(2 * rank)], "early_z")
+    got_z = swap(own_z, bits - 2, bits - 2)
     shapes = [buffer(plan.after_3[1]), weight, weight, buffer(2 * rank)]
-    buf, w4, w3, c2_v = vmem_call(functools.partial(kernel_3, plan, bits, rank), (buf, got), shapes, "level_3")
-
-    wide = jax.ShapeDtypeStruct((width, points), F32)
-    rest, s2_v, s1_v = pl.pallas_call(
-        early_kernel,
-        out_shape=[wide] + [jax.ShapeDtypeStruct((rank, points), BF)] * 2,
-        in_specs=[HBM] * 5 + [VMEM] * 2,
-        out_specs=[VMEM] * 3,
-        scratch_shapes=[pltpu.VMEM((2 * rank, points), BF), pltpu.SemaphoreType.DMA((5,))],
-        compiler_params=params,
-        cost_estimate=cost(4 * width * rank * points, 6 * width * points + 8 * rank * points),
-        name="early",
-    )(*[stay(x) for x in (right_solved, s4, s3, s2, s1)], w4, w3)
+    buf, w4, w3, c2_v = vmem_call(functools.partial(kernel_3, plan, bits, rank), (buf, got, own_z), shapes, "level_3")
 
     got = swap(buf, bits - 2, bits - 2)
-    shapes = [buffer(width), jax.ShapeDtypeStruct((width, 2 * rank), BF), buffer(2 * rank)]
-    buf, stacked, last = vmem_call(functools.partial(kernel_2, plan, bits), (buf, got, s1_v), shapes, "level_2")
-    (rest,) = vmem_call(
-        middle_kernel,
-        (rest, s2_v, stacked, c2_v),
-        [wide],
-        "middle",
-        cost_estimate=cost(2 * width * rank * points, 8 * width * points),
-    )
+    flops, moved = 2 * width * rank * points, 8 * width * points
+    (rest,) = vmem_call(early_kernel, (rest, s4_v, s3_v, w4, w3), [wide], "early", cost_estimate=cost(2 * flops, moved))
+    meet_z = functools.partial(meet_z_kernel, bits, rank)
+    met = vmem_call(meet_z, (own_z, got_z, w3), [buffer(rank)] * 2, "meet_z")
+    met = [*met, *[swap(x, 0, 0) for x in met]]
+    shapes = [buffer(width), jax.ShapeDtypeStruct((width, 2 * rank), BF)]
+    buf, stacked = vmem_call(functools.partial(kernel_2, plan, bits), (buf, got, *met), shapes, "level_2")
+    (rest,) = vmem_call(middle_kernel, (rest, s2_v, stacked, c2_v), [wide], "middle", cost_estimate=cost(flops, moved))
     got = swap(buf, bits - 1, bits - 1)
     chunks = CHUNKS_OUT
     return pl.pallas_call(
         functools.partial(last_kernel, bits, chunks),
         out_shape=wide,
-        in_specs=[VMEM] * 5,
+        in_specs=[VMEM] * 8,
         out_specs=HBM,
         scratch_shapes=[pltpu.VMEM(wide.shape, F32), pltpu.SemaphoreType.DMA((chunks,))],
         compiler_params=params,
         name="last",
-    )(buf, got, last, rest, s1_v)
+    )(buf, got, *met, rest, s1_v)
 
 
 def solution(mesh):

time: 32.2 us -> 30.9 us (0.960)
  waiting for transfers between devices: 14.4 us -> 10.6 us
  starting transfers between devices: 10.6 us -> 12.6 us
  Pallas kernels: 7.08 us -> 7.41 us
    ppermute x6 -> x9, waiting for transfers between devices: 14.4 us -> 10.6 us  [swap(): lax.ppermute(x, 'pts', [(i, i ^ 1 << (odd if i & 1 else even)) for i in r...]
    ppermute x6 -> x9, starting transfers between devices: 10.6 us -> 12.6 us  [swap(): lax.ppermute(x, 'pts', [(i, i ^ 1 << (odd if i & 1 else even)) for i in r...]
    pallas_call x6 -> x9, Pallas kernels: 1.26 us -> 1.58 us  [vmem_call(): pl.pallas_call(kernel, out_shape=shapes, in_specs=[VMEM] * len(operands),...]
  transfers between devices with their start and end apart: 6 -> 9, of which waited for: 6 -> 7; matrix products, arithmetic and copies ran while one was open for 0% -> 0% of each run, Pallas kernels for 6% -> 9%
where the time goes in v6:
time: 30.9 us; the launch traced here: 30.7 us
  starting transfers between devices  12.6 us (41%)
  waiting for transfers between devices  10.6 us (34%)
  Pallas kernels  7.41 us (24%)
    ppermute x9, starting transfers between devices, swap(): lax.ppermute(x, 'pts', [(i, i ^ 1 << (odd if i & 1 else even)) for i in r...  12.6 us
    ppermute x9, waiting for transfers between devices, swap(): lax.ppermute(x, 'pts', [(i, i ^ 1 << (odd if i & 1 else even)) for i in r...  10.6 us
    pallas_call x1, Pallas kernels, on_device(): pl.pallas_call(lambda *refs: first_kernel([t for t, _ in device], rank, w...  2.98 us
    pallas_call x1, Pallas kernels, on_device(): pl.pallas_call(fetch_kernel, out_shape=[wide] + [base] * 4, in_specs=[VME...  1.71 us
    pallas_call x9, Pallas kernels, vmem_call(): pl.pallas_call(kernel, out_shape=shapes, in_specs=[VMEM] * len(operands),...  1.58 us
    pallas_call x1, Pallas kernels, on_device(): pl.pallas_call(functools.partial(last_kernel, bits, chunks), out_shape=wi...  1.14 us
  transfers between devices with their start and end apart: 9, of which 7 were waited for; matrix products, arithmetic and copies ran while one was open for 0% of the time, Pallas kernels for 9%

profile of v6, /device:TPU:0, one launch (start us, length us, event | category | flops | bytes accessed | tf_op | source)
XLA Modules:
  0.0 30.7 jit_solution(6071318657626421960)
XLA Ops:
  0.0 3.0 %products.1 = (bf16[848,128]{1,0:T(8,128)(2,1)S(1)}, bf16[848,128]{1,0:T(8,128)(2,1)S(1)}) custom-call(f32[64,2048]{1,0:T(8,128)} %refs_0_.3, bf16[128,2048]{1,0:T(8,128)(2,1)} %refs_1_.2, bf16[128,2048]{1,0:T(8,128)(2,1)} %refs_2_.2, bf16[128,2048]{1,0:T(8,128)(2,1)} %refs_1_.3, bf16[128,2048]{1,0:T(8,128)(2,1)} %refs_2_.3, bf16[128,2048]{1,0:T(8,128)(2,1)} %refs_3_.3, ...), custom_call_target="tpu_custom_call" | custom-call | tf_op jit(solution)/shard_map/products/pallas_call | solution.py:448
  3.0 0.5 %collective-permute-start = (bf16[848,128]{1,0:T(8,128)(2,1)S(1)}, bf16[848,128]{1,0:T(8,128)(2,1)S(1)}, u32[]{:S(2)}, u32[]{:S(2)}) collective-permute-start(bf16[848,128]{1,0:T(8,128)(2,1)S(1)} %get-tuple-element.25), channel_id=1, source_target_pairs={{0,1},{1,0},{2,3},{3,2},{4,5},{5,4},{6,7},{7,6},{8,9},{9,8},{10,11... | collective-permute-start | bytes 651272 | tf_op jit(solution)/shard_map/ppermute | solution.py:92
  3.5 1.1 %collective-permute-done.got = bf16[848,128]{1,0:T(8,128)(2,1)S(1)} collective-permute-done((bf16[848,128]{1,0:T(8,128)(2,1)S(1)}, bf16[848,128]{1,0:T(8,128)(2,1)S(1)}, u32[]{:S(2)}, u32[]{:S(2)}) %collective-permute-start) | collective-permute-done | bytes 217120 | tf_op jit(solution)/shard_map/ppermute | solution.py:92
  4.7 2.9 %collective-permute-start.1 = (bf16[1056,128]{1,0:T(8,128)(2,1)S(1)}, bf16[1056,128]{1,0:T(8,128)(2,1)S(1)}, u32[]{:S(2)}, u32[]{:S(2)}) collective-permute-start(bf16[1056,128]{1,0:T(8,128)(2,1)S(1)} %merge.1.after.own), channel_id=1, source_target_pairs={{0,2},{1,5},{2,0},{3,7},{4,6},{5,1},{6,4},{7,3},{8,10},{9,13},{10,... | collective-permute-start | bytes 811016 | tf_op jit(solution)/shard_map/ppermute | solution.py:92
  7.6 1.7 %fetch.1 = (f32[64,2048]{1,0:T(8,128)S(1)}, bf16[128,2048]{1,0:T(8,128)(2,1)S(1)}, bf16[128,2048]{1,0:T(8,128)(2,1)S(1)}, bf16[128,2048]{1,0:T(8,128)(2,1)S(1)}, bf16[128,2048]{1,0:T(8,128)(2,1)S(1)}) custom-call(bf16[1056,128]{1,0:T(8,128)(2,1)S(1)} %merge.1.after.own, f32[64,2048]{1,0:T(8,128)} %refs_0_.3, bf16[128,2048]{1,0:T(8,128)(2,1)} %refs_1_.3, ...), custom_call_target="tpu_custom_call" | custom-call | bytes 2621440 | tf_op jit(solution)/shard_map/fetch/pallas_call | solution.py:496
  9.3 2.7 %collective-permute-done.1.got = bf16[1056,128]{1,0:T(8,128)(2,1)S(1)} collective-permute-done((bf16[1056,128]{1,0:T(8,128)(2,1)S(1)}, bf16[1056,128]{1,0:T(8,128)(2,1)S(1)}, u32[]{:S(2)}, u32[]{:S(2)}) %collective-permute-start.1) | collective-permute-done | bytes 270368 | tf_op jit(solution)/shard_map/ppermute | solution.py:92
  12.0 0.3 %level_4.1 = (bf16[768,128]{1,0:T(8,128)(2,1)S(1)}, bf16[64,128]{1,0:T(8,128)(2,1)S(1)}) custom-call(bf16[1056,128]{1,0:T(8,128)(2,1)S(1)} %merge.1.after.own, bf16[1056,128]{1,0:T(8,128)(2,1)S(1)} %collective-permute-done.1.got, bf16[128,2048]{1,0:T(8,128)(2,1)S(1)} %get-tuple-element.26.after.s1), custom_call_target="tpu_custom_call" | custom-call | tf_op jit(solution)/shard_map/level_4/pallas_call | solution.py:422
  12.4 2.1 %collective-permute-start.2 = (bf16[768,128]{1,0:T(8,128)(2,1)S(1)}, bf16[768,128]{1,0:T(8,128)(2,1)S(1)}, u32[]{:S(2)}, u32[]{:S(2)}) collective-permute-start(bf16[768,128]{1,0:T(8,128)(2,1)S(1)} %get-tuple-element.27.own), channel_id=1, source_target_pairs={{0,4},{1,3},{2,6},{3,1},{4,0},{5,7},{6,2},{7,5},{8,12},{9,11},{10,... | collective-permute-start | bytes 589832 | tf_op jit(solution)/shard_map/ppermute | solution.py:92
  14.5 3.6 %collective-permute-done.2.got = bf16[768,128]{1,0:T(8,128)(2,1)S(1)} collective-permute-done((bf16[768,128]{1,0:T(8,128)(2,1)S(1)}, bf16[768,128]{1,0:T(8,128)(2,1)S(1)}, u32[]{:S(2)}, u32[]{:S(2)}) %collective-permute-start.2) | collective-permute-done | bytes 196640 | tf_op jit(solution)/shard_map/ppermute | solution.py:92
  18.2 0.1 collective-permute-start.3
  18.3 2.1 %collective-permute-start.5 = (bf16[256,128]{1,0:T(8,128)(2,1)S(1)}, bf16[256,128]{1,0:T(8,128)(2,1)S(1)}, u32[]{:S(2)}, u32[]{:S(2)}) collective-permute-start(bf16[256,128]{1,0:T(8,128)(2,1)S(1)} %early_z.1.after.own), channel_id=1, source_target_pairs={{0,8},{1,9},{2,10},{3,11},{4,12},{5,13},{6,14},{7,15},{8,0},{9,1},... | collective-permute-start | bytes 196616 | tf_op jit(solution)/shard_map/ppermute | solution.py:92
  20.4 0.0 collective-permute-done.3.got
  20.4 0.3 %level_3.1 = (bf16[144,128]{1,0:T(8,128)(2,1)S(1)}, bf16[64,128]{1,0:T(8,128)(2,1)S(1)}, bf16[64,128]{1,0:T(8,128)(2,1)S(1)}, bf16[256,128]{1,0:T(8,128)(2,1)S(1)}) custom-call(bf16[960,128]{1,0:T(8,128)(2,1)S(1)} %get-tuple-element.29.own, bf16[960,128]{1,0:T(8,128)(2,1)S(1)} %collective-permute-done.3.got, bf16[256,128]{1,0:T(8,128)(2,1)S(1)} %early_z.1.after.own), custom_call_target="tpu_custom_call" | custom-call | tf_op jit(solution)/shard_map/level_3/pallas_call | solution.py:422
  20.8 1.5 %collective-permute-start.4 = (bf16[144,128]{1,0:T(8,128)(2,1)S(1)}, bf16[144,128]{1,0:T(8,128)(2,1)S(1)}, u32[]{:S(2)}, u32[]{:S(2)}) collective-permute-start(bf16[144,128]{1,0:T(8,128)(2,1)S(1)} %get-tuple-element.31.own), channel_id=1, source_target_pairs={{0,8},{1,9},{2,10},{3,11},{4,12},{5,13},{6,14},{7,15},{8,0},{9,1},... | collective-permute-start | bytes 110600 | tf_op jit(solution)/shard_map/ppermute | solution.py:92
  22.2 1.1 %collective-permute-done.5.got = bf16[256,128]{1,0:T(8,128)(2,1)S(1)} collective-permute-done((bf16[256,128]{1,0:T(8,128)(2,1)S(1)}, bf16[256,128]{1,0:T(8,128)(2,1)S(1)}, u32[]{:S(2)}, u32[]{:S(2)}) %collective-permute-start.5) | collective-permute-done | bytes 65568 | tf_op jit(solution)/shard_map/ppermute | solution.py:92
  23.4 0.1 collective-permute-start.6
  23.5 0.4 %collective-permute-start.7 = (bf16[128,128]{1,0:T(8,128)(2,1)S(1)}, bf16[128,128]{1,0:T(8,128)(2,1)S(1)}, u32[]{:S(2)}, u32[]{:S(2)}) collective-permute-start(bf16[128,128]{1,0:T(8,128)(2,1)S(1)} %get-tuple-element.34.m1), channel_id=1, source_target_pairs={{0,1},{1,0},{2,3},{3,2},{4,5},{5,4},{6,7},{7,6},{8,9},{9,8},{10,11... | collective-permute-start | bytes 98312 | tf_op jit(solution)/shard_map/ppermute | solution.py:92
  23.9 0.7 %collective-permute-done.6.o0 = bf16[128,128]{1,0:T(8,128)(2,1)S(1)} collective-permute-done((bf16[128,128]{1,0:T(8,128)(2,1)S(1)}, bf16[128,128]{1,0:T(8,128)(2,1)S(1)}, u32[]{:S(2)}, u32[]{:S(2)}) %collective-permute-start.6) | collective-permute-done | bytes 32800 | tf_op jit(solution)/shard_map/ppermute | solution.py:92
  24.6 0.2 collective-permute-done.7.o1
  24.8 0.0 collective-permute-done.4.got
  24.8 0.1 level_2.1
  24.9 2.8 %collective-permute-start.8 = (bf16[64,128]{1,0:T(8,128)(2,1)S(1)}, bf16[64,128]{1,0:T(8,128)(2,1)S(1)}, u32[]{:S(2)}, u32[]{:S(2)}) collective-permute-start(bf16[64,128]{1,0:T(8,128)(2,1)S(1)} %get-tuple-element.35.own), channel_id=1, source_target_pairs={{0,16},{1,17},{2,18},{3,19},{4,20},{5,21},{6,22},{7,23},{8,24},{9,... | collective-permute-start | bytes 49160 | tf_op jit(solution)/shard_map/ppermute | solution.py:92
  27.7 0.3 early.1.rest
  28.0 0.4 %middle.1.rest = f32[64,2048]{1,0:T(8,128)S(1)} custom-call(f32[64,2048]{1,0:T(8,128)S(1)} %early.1.rest, bf16[128,2048]{1,0:T(8,128)(2,1)S(1)} %get-tuple-element.40.s2, bf16[64,256]{1,0:T(8,128)(2,1)S(1)} %get-tuple-element.41.stacked, bf16[256,128]{1,0:T(8,128)(2,1)S(1)} %get-tuple-element.42.rows), custom_call_target="tpu_custom_call" | custom-call | flops 33554432 | bytes 1048576 | tf_op jit(solution)/shard_map/middle/pallas_call | solution.py:422
  28.4 1.2 %collective-permute-done.8.got = bf16[64,128]{1,0:T(8,128)(2,1)S(1)} collective-permute-done((bf16[64,128]{1,0:T(8,128)(2,1)S(1)}, bf16[64,128]{1,0:T(8,128)(2,1)S(1)}, u32[]{:S(2)}, u32[]{:S(2)}) %collective-permute-start.8) | collective-permute-done | bytes 16416 | tf_op jit(solution)/shard_map/ppermute | solution.py:92
  29.6 1.1 %last.1 = f32[64,2048]{1,0:T(8,128)} custom-call(bf16[64,128]{1,0:T(8,128)(2,1)S(1)} %get-tuple-element.35.own, bf16[64,128]{1,0:T(8,128)(2,1)S(1)} %collective-permute-done.8.got, bf16[128,128]{1,0:T(8,128)(2,1)S(1)} %get-tuple-element.33.m0, bf16[128,128]{1,0:T(8,128)(2,1)S(1)} %get-tuple-element.34.m1, bf16[128,128]{1,0:T(8,128)(2,1)S(1)} %collective-permute-done.6.o0, ...), custom_call_target="tpu_custom_call" | custom-call | tf_op jit(solution)/shard_map/last/pallas_call | solution.py:528
  (4 shorter events, 0.1 us)
Async XLA Ops:
  3.0 1.6 %collective-permute-start = (bf16[848,128]{1,0:T(8,128)(2,1)S(1)}, bf16[848,128]{1,0:T(8,128)(2,1)S(1)}, u32[]{:S(2)}, u32[]{:S(2)}) collective-permute-start(bf16[848,128]{1,0:T(8,128)(2,1)S(1)} %get-tuple-element.25), channel_id=1, source_target_pairs={{0,1},{1,0},{2,3},{3,2},{4,5},{5,4},{6,7},{7,6},{8,9},{9,8},{10,11... | collective-permute-start | bytes 651272 | tf_op jit(solution)/shard_map/ppermute | solution.py:92
  4.7 7.4 %collective-permute-start.1 = (bf16[1056,128]{1,0:T(8,128)(2,1)S(1)}, bf16[1056,128]{1,0:T(8,128)(2,1)S(1)}, u32[]{:S(2)}, u32[]{:S(2)}) collective-permute-start(bf16[1056,128]{1,0:T(8,128)(2,1)S(1)} %merge.1.after.own), channel_id=1, source_target_pairs={{0,2},{1,5},{2,0},{3,7},{4,6},{5,1},{6,4},{7,3},{8,10},{9,13},{10,... | collective-permute-start | bytes 811016 | tf_op jit(solution)/shard_map/ppermute | solution.py:92
  12.4 5.8 %collective-permute-start.2 = (bf16[768,128]{1,0:T(8,128)(2,1)S(1)}, bf16[768,128]{1,0:T(8,128)(2,1)S(1)}, u32[]{:S(2)}, u32[]{:S(2)}) collective-permute-start(bf16[768,128]{1,0:T(8,128)(2,1)S(1)} %get-tuple-element.27.own), channel_id=1, source_target_pairs={{0,4},{1,3},{2,6},{3,1},{4,0},{5,7},{6,2},{7,5},{8,12},{9,11},{10,... | collective-permute-start | bytes 589832 | tf_op jit(solution)/shard_map/ppermute | solution.py:92
  18.2 2.3 %collective-permute-start.3 = (bf16[960,128]{1,0:T(8,128)(2,1)S(1)}, bf16[960,128]{1,0:T(8,128)(2,1)S(1)}, u32[]{:S(2)}, u32[]{:S(2)}) collective-permute-start(bf16[960,128]{1,0:T(8,128)(2,1)S(1)} %get-tuple-element.29.own), channel_id=1, source_target_pairs={{0,1},{1,0},{2,3},{3,2},{4,5},{5,4},{6,7},{7,6},{8,9},{9,8},{10,11... | collective-permute-start | bytes 737288 | tf_op jit(solution)/shard_map/ppermute | solution.py:92
  18.3 5.1 %collective-permute-start.5 = (bf16[256,128]{1,0:T(8,128)(2,1)S(1)}, bf16[256,128]{1,0:T(8,128)(2,1)S(1)}, u32[]{:S(2)}, u32[]{:S(2)}) collective-permute-start(bf16[256,128]{1,0:T(8,128)(2,1)S(1)} %early_z.1.after.own), channel_id=1, source_target_pairs={{0,8},{1,9},{2,10},{3,11},{4,12},{5,13},{6,14},{7,15},{8,0},{9,1},... | collective-permute-start | bytes 196616 | tf_op jit(solution)/shard_map/ppermute | solution.py:92
  20.8 4.0 %collective-permute-start.4 = (bf16[144,128]{1,0:T(8,128)(2,1)S(1)}, bf16[144,128]{1,0:T(8,128)(2,1)S(1)}, u32[]{:S(2)}, u32[]{:S(2)}) collective-permute-start(bf16[144,128]{1,0:T(8,128)(2,1)S(1)} %get-tuple-element.31.own), channel_id=1, source_target_pairs={{0,8},{1,9},{2,10},{3,11},{4,12},{5,13},{6,14},{7,15},{8,0},{9,1},... | collective-permute-start | bytes 110600 | tf_op jit(solution)/shard_map/ppermute | solution.py:92
  23.4 1.3 %collective-permute-start.6 = (bf16[128,128]{1,0:T(8,128)(2,1)S(1)}, bf16[128,128]{1,0:T(8,128)(2,1)S(1)}, u32[]{:S(2)}, u32[]{:S(2)}) collective-permute-start(bf16[128,128]{1,0:T(8,128)(2,1)S(1)} %get-tuple-element.33.m0), channel_id=1, source_target_pairs={{0,1},{1,0},{2,3},{3,2},{4,5},{5,4},{6,7},{7,6},{8,9},{9,8},{10,11... | collective-permute-start | bytes 98312 | tf_op jit(solution)/shard_map/ppermute | solution.py:92
  23.5 1.3 %collective-permute-start.7 = (bf16[128,128]{1,0:T(8,128)(2,1)S(1)}, bf16[128,128]{1,0:T(8,128)(2,1)S(1)}, u32[]{:S(2)}, u32[]{:S(2)}) collective-permute-start(bf16[128,128]{1,0:T(8,128)(2,1)S(1)} %get-tuple-element.34.m1), channel_id=1, source_target_pairs={{0,1},{1,0},{2,3},{3,2},{4,5},{5,4},{6,7},{7,6},{8,9},{9,8},{10,11... | collective-permute-start | bytes 98312 | tf_op jit(solution)/shard_map/ppermute | solution.py:92
  24.9 4.6 %collective-permute-start.8 = (bf16[64,128]{1,0:T(8,128)(2,1)S(1)}, bf16[64,128]{1,0:T(8,128)(2,1)S(1)}, u32[]{:S(2)}, u32[]{:S(2)}) collective-permute-start(bf16[64,128]{1,0:T(8,128)(2,1)S(1)} %get-tuple-element.35.own), channel_id=1, source_target_pairs={{0,16},{1,17},{2,18},{3,19},{4,20},{5,21},{6,22},{7,23},{8,24},{9,... | collective-permute-start | bytes 49160 | tf_op jit(solution)/shard_map/ppermute | solution.py:92

commit v7 on v6

--- a/solution.py
+++ b/solution.py
@@ -10,6 +10,7 @@
 BF = jnp.bfloat16
 F32 = jnp.float32
 LEVELS = (4, 3, 2, 1)
+LATE = (("c", 3), ("c", 1))
 SHARES = ((4, 3, 1), (2,))
 VMEM = pl.BlockSpec(memory_space=pltpu.VMEM)
 HBM = pl.BlockSpec(memory_space=pltpu.HBM)
@@ -51,7 +52,10 @@
             return spread(first), spread(second)
 
         self.device = start(1)
-        self.child = start(2)
+        (first, _), second = start(2)
+        late = {key: z - a for key, (a, z) in first.items() if key in LATE}
+        self.aside = spread(late)
+        self.child = (spread({key: z - a for key, (a, z) in first.items() if key not in LATE}), second)
         self.after_4 = (
             spread({("p", 3): w, ("p", 2): w, ("p", 1): w, ("c", 3): 8 * rows[3], ("c", 1): 8 * rows[1]}),
             spread(
@@ -179,7 +183,7 @@
     return (a.astype(F32) + z.astype(F32)).astype(BF)
 
 
-def merge_kernel(plan, keep, got, out):
+def merge_kernel(plan, keep, got, out, aside):
     def merge(role):
         for key, (lo, hi) in plan.device[role][0].items():
             a, z = keep[lo:hi], got[lo:hi]
@@ -187,8 +191,11 @@
                 value = interleave(z, a) if role else interleave(a, z)
             else:
                 value = plus(a, z)
-            lo, hi = plan.child[role][0][key]
-            out[lo:hi] = value
+            late = role == 0 and key in LATE
+            lo, hi = (plan.aside if late else plan.child[role])[0][key]
+            (aside if late else out)[lo:hi] = value
+        if role:
+            aside[...] = jnp.zeros_like(aside)
 
     by_role(lambda: merge(0), lambda: merge(1))
 
@@ -228,9 +235,6 @@
             a, z = both(("p", k))
             lo, hi = then[("p", k)]
             out[lo:hi] = (a.astype(F32) + z.astype(F32) - change[:, i * rank : (i + 1) * rank]).astype(BF)
-        for k in (3, 1):
-            lo, hi = then[("c", k)]
-            out[lo:hi] = interleave(*ordered(*both(("c", k)), upper))
 
     def second():
         spans, then = plan.child[1][0], plan.after_4[1][0]
@@ -252,6 +256,18 @@
         w4[...] = jnp.zeros_like(w4)
 
     by_role(first, second)
+
+
+def place_kernel(plan, bits, before, own, got, out):
+    del before
+
+    def first():
+        for key, (lo, hi) in plan.aside[0].items():
+            value = interleave(*ordered(own[lo:hi], got[lo:hi], index_bit(bits - 4) == 1))
+            lo, hi = plan.after_4[0][0][key]
+            out[lo:hi] = value
+
+    pl.when(index_bit(0) == 0)(first)
 
 
 def gather_kernel(plan, bits, own, got, w4, out, gram):
@@ -386,18 +402,21 @@
     out[...] = rest[...] - nn(weights, s2[...])
 
 
-def last_kernel(bits, chunks, own, got, m0, m1, o0, o1, rest, s1, out_hbm, out_v, sems):
+def basis_kernel(m0, m1, o0, o1, s1, out):
+    rank = m0.shape[0]
+    c = shared((m0, m1), (o0, o1), 0)
+    out[:rank] = tn(c[:rank], s1[...]).astype(BF)
+    out[rank:] = tn(c[rank:], s1[...]).astype(BF)
+
+
+def last_kernel(bits, chunks, own, got, rest, basis, out_hbm, out_v, sems):
     upper = index_bit(bits - 1) == 1
-    rank = m0.shape[0]
-    a, z = own[...], got[...]
-    c = shared((m0, m1), (o0, o1), 0)
-    stacked = jnp.concatenate(ordered(a, z, upper), axis=1)
-    weights = nt(stacked, jnp.concatenate([c[:rank], c[rank:]], axis=1)).astype(BF)
+    stacked = jnp.concatenate(ordered(own[...], got[...], upper), axis=1)
     cut = rest.shape[1] // chunks
     copies = []
     for j in range(chunks):
         cols = slice(j * cut, (j + 1) * cut)
-        out_v[:, cols] = rest[:, cols] - nn(weights, s1[:, cols])
+        out_v[:, cols] = rest[:, cols] - nn(stacked, basis[:, cols])
         span = pl.ds(j * cut, cut)
         copies.append(pltpu.make_async_copy(out_v.at[:, span], out_hbm.at[:, span], sems.at[j]))
         copies[-1].start()
@@ -468,7 +487,8 @@
     size = Plan.total(plan.child)
     if in_kernel:
         got = swap(send, 0, 0)
-        (buf,) = vmem_call(functools.partial(merge_kernel, plan), (keep, got), [buffer(size)], "merge")
+        shapes = [buffer(size), buffer(plan.aside[1])]
+        buf, aside = vmem_call(functools.partial(merge_kernel, plan), (keep, got), shapes, "merge")
     else:
         both = jnp.stack([keep, send])
         parts = {k: jnp.stack([c[:, :rank], c[:, rank:]]).astype(BF) for k, c in coupling.items()}
@@ -484,15 +504,17 @@
         shares = []
         for role in (0, 1):
             share = [both[role, : device[role][1]]]
-            share += [parts[k].reshape(-1, rank) for k in SHARES[role]]
+            share += [parts[k].reshape(-1, rank) for k in SHARES[role] if ("c", k) not in LATE]
             share = jnp.concatenate(share, axis=0)
             shares.append(jnp.pad(share, ((0, size - share.shape[0]), (0, 0))))
         buf = jnp.where(index_bit(0) == 1, shares[1], shares[0])
+        aside = jnp.concatenate([parts[k].reshape(-1, rank) for _, k in LATE], axis=0)
 
     weight = jax.ShapeDtypeStruct((width, rank), BF)
     wide = jax.ShapeDtypeStruct((width, points), F32)
     base = jax.ShapeDtypeStruct((rank, points), BF)
     got = swap(buf, bits - 4, bits - 3)
+    got_aside = swap(aside, bits - 4, bits - 3)
     rest, s4_v, s3_v, s2_v, s1_v = pl.pallas_call(
         fetch_kernel,
         out_shape=[wide] + [base] * 4,
@@ -505,6 +527,8 @@
     )(buf, *[stay(x) for x in (right_solved, s4, s3, s2, s1)])
     shapes = [buffer(Plan.total(plan.after_4)), weight]
     buf, w4 = vmem_call(functools.partial(kernel_4, plan, bits, rank), (buf, got, s1_v), shapes, "level_4")
+    place = functools.partial(place_kernel, plan, bits)
+    (buf,) = vmem_call(place, (buf, aside, got_aside), [buffer(Plan.total(plan.after_4))], "place", input_output_aliases={0: 0})
     got = swap(buf, bits - 3, bits - 4)
     shapes = [buffer(Plan.total(plan.before_3)), buffer(rank)]
     buf, gram = vmem_call(functools.partial(gather_kernel, plan, bits), (buf, got, w4), shapes, "gather")
@@ -523,17 +547,19 @@
     shapes = [buffer(width), jax.ShapeDtypeStruct((width, 2 * rank), BF)]
     buf, stacked = vmem_call(functools.partial(kernel_2, plan, bits), (buf, got, *met), shapes, "level_2")
     (rest,) = vmem_call(middle_kernel, (rest, s2_v, stacked, c2_v), [wide], "middle", cost_estimate=cost(flops, moved))
+    wide_basis = jax.ShapeDtypeStruct((2 * rank, points), BF)
+    (basis_1,) = vmem_call(basis_kernel, (*met, s1_v), [wide_basis], "basis_1", cost_estimate=cost(4 * rank * rank * points, 6 * rank * points))
     got = swap(buf, bits - 1, bits - 1)
     chunks = CHUNKS_OUT
     return pl.pallas_call(
         functools.partial(last_kernel, bits, chunks),
         out_shape=wide,
-        in_specs=[VMEM] * 8,
+        in_specs=[VMEM] * 4,
         out_specs=HBM,
         scratch_shapes=[pltpu.VMEM(wide.shape, F32), pltpu.SemaphoreType.DMA((chunks,))],
         compiler_params=params,
         name="last",
-    )(buf, got, *met, rest, s1_v)
+    )(buf, got, rest, basis_1)
 
 
 def solution(mesh):

time: 30.9 us -> 30.4 us (0.984)
  waiting for transfers between devices: 10.6 us -> 9.76 us
  Pallas kernels: 7.41 us -> 7.77 us
    ppermute x9 -> x10, waiting for transfers between devices: 10.6 us -> 9.76 us  [swap(): lax.ppermute(x, 'pts', [(i, i ^ 1 << (odd if i & 1 else even)) for i in r...]
    pallas_call x9 -> x11, Pallas kernels: 1.58 us -> 2.05 us  [vmem_call(): pl.pallas_call(kernel, out_shape=shapes, in_specs=[VMEM] * len(operands),...]
    ppermute x9 -> x10, starting transfers between devices: 12.6 us -> 12.6 us  [swap(): lax.ppermute(x, 'pts', [(i, i ^ 1 << (odd if i & 1 else even)) for i in r...]
  transfers between devices with their start and end apart: 9 -> 10, of which waited for: 7 -> 8; matrix products, arithmetic and copies ran while one was open for 0% -> 0% of each run, Pallas kernels for 9% -> 12%
where the time goes in v7:
time: 30.4 us; the launch traced here: 30.3 us
  starting transfers between devices  12.6 us (41%)
  waiting for transfers between devices  9.76 us (32%)
  Pallas kernels  7.77 us (26%)
    ppermute x10, starting transfers between devices, swap(): lax.ppermute(x, 'pts', [(i, i ^ 1 << (odd if i & 1 else even)) for i in r...  12.6 us
    ppermute x10, waiting for transfers between devices, swap(): lax.ppermute(x, 'pts', [(i, i ^ 1 << (odd if i & 1 else even)) for i in r...  9.76 us
    pallas_call x1, Pallas kernels, on_device(): pl.pallas_call(lambda *refs: first_kernel([t for t, _ in device], rank, w...  2.98 us
    pallas_call x11, Pallas kernels, vmem_call(): pl.pallas_call(kernel, out_shape=shapes, in_specs=[VMEM] * len(operands),...  2.05 us
    pallas_call x1, Pallas kernels, on_device(): pl.pallas_call(fetch_kernel, out_shape=[wide] + [base] * 4, in_specs=[VME...  1.71 us
    pallas_call x1, Pallas kernels, on_device(): pl.pallas_call(functools.partial(last_kernel, bits, chunks), out_shape=wi...  1.03 us
  transfers between devices with their start and end apart: 10, of which 8 were waited for; matrix products, arithmetic and copies ran while one was open for 0% of the time, Pallas kernels for 12%

profile of v7, /device:TPU:0, one launch (start us, length us, event | category | flops | bytes accessed | tf_op | source)
XLA Modules:
  0.0 30.3 jit_solution(6550288360103825442)
XLA Ops:
  0.0 3.0 %products.1 = (bf16[848,128]{1,0:T(8,128)(2,1)S(1)}, bf16[848,128]{1,0:T(8,128)(2,1)S(1)}) custom-call(f32[64,2048]{1,0:T(8,128)} %refs_0_.3, bf16[128,2048]{1,0:T(8,128)(2,1)} %refs_1_.2, bf16[128,2048]{1,0:T(8,128)(2,1)} %refs_2_.2, bf16[128,2048]{1,0:T(8,128)(2,1)} %refs_1_.3, bf16[128,2048]{1,0:T(8,128)(2,1)} %refs_2_.3, bf16[128,2048]{1,0:T(8,128)(2,1)} %refs_3_.3, ...), custom_call_target="tpu_custom_call" | custom-call | tf_op jit(solution)/shard_map/products/pallas_call | solution.py:467
  3.0 0.5 %collective-permute-start = (bf16[848,128]{1,0:T(8,128)(2,1)S(1)}, bf16[848,128]{1,0:T(8,128)(2,1)S(1)}, u32[]{:S(2)}, u32[]{:S(2)}) collective-permute-start(bf16[848,128]{1,0:T(8,128)(2,1)S(1)} %get-tuple-element.27), channel_id=1, source_target_pairs={{0,1},{1,0},{2,3},{3,2},{4,5},{5,4},{6,7},{7,6},{8,9},{9,8},{10,11... | collective-permute-start | bytes 651272 | tf_op jit(solution)/shard_map/ppermute | solution.py:96
  3.5 1.1 %collective-permute-done.got = bf16[848,128]{1,0:T(8,128)(2,1)S(1)} collective-permute-done((bf16[848,128]{1,0:T(8,128)(2,1)S(1)}, bf16[848,128]{1,0:T(8,128)(2,1)S(1)}, u32[]{:S(2)}, u32[]{:S(2)}) %collective-permute-start) | collective-permute-done | bytes 217120 | tf_op jit(solution)/shard_map/ppermute | solution.py:96
  4.7 2.9 %collective-permute-start.1 = (bf16[896,128]{1,0:T(8,128)(2,1)S(1)}, bf16[896,128]{1,0:T(8,128)(2,1)S(1)}, u32[]{:S(2)}, u32[]{:S(2)}) collective-permute-start(bf16[896,128]{1,0:T(8,128)(2,1)S(1)} %get-tuple-element.28.after.own), channel_id=1, source_target_pairs={{0,2},{1,5},{2,0},{3,7},{4,6},{5,1},{6,4},{7,3},{8,10},{9,13},{10,... | collective-permute-start | bytes 688136 | tf_op jit(solution)/shard_map/ppermute | solution.py:96
  7.6 0.1 collective-permute-start.2
  7.7 1.7 %fetch.1 = (f32[64,2048]{1,0:T(8,128)S(1)}, bf16[128,2048]{1,0:T(8,128)(2,1)S(1)}, bf16[128,2048]{1,0:T(8,128)(2,1)S(1)}, bf16[128,2048]{1,0:T(8,128)(2,1)S(1)}, bf16[128,2048]{1,0:T(8,128)(2,1)S(1)}) custom-call(bf16[896,128]{1,0:T(8,128)(2,1)S(1)} %get-tuple-element.28.after.own, f32[64,2048]{1,0:T(8,128)} %refs_0_.3, bf16[128,2048]{1,0:T(8,128)(2,1)} %refs_1_.3, ...), custom_call_target="tpu_custom_call" | custom-call | bytes 2621440 | tf_op jit(solution)/shard_map/fetch/pallas_call | solution.py:518
  9.4 2.2 %collective-permute-done.1.got = bf16[896,128]{1,0:T(8,128)(2,1)S(1)} collective-permute-done((bf16[896,128]{1,0:T(8,128)(2,1)S(1)}, bf16[896,128]{1,0:T(8,128)(2,1)S(1)}, u32[]{:S(2)}, u32[]{:S(2)}) %collective-permute-start.1) | collective-permute-done | bytes 229408 | tf_op jit(solution)/shard_map/ppermute | solution.py:96
  11.6 0.3 %level_4.1 = (bf16[768,128]{1,0:T(8,128)(2,1)S(1)}, bf16[64,128]{1,0:T(8,128)(2,1)S(1)}) custom-call(bf16[896,128]{1,0:T(8,128)(2,1)S(1)} %get-tuple-element.28.after.own, bf16[896,128]{1,0:T(8,128)(2,1)S(1)} %collective-permute-done.1.got, bf16[128,2048]{1,0:T(8,128)(2,1)S(1)} %get-tuple-element.29.after.s1), custom_call_target="tpu_custom_call" | custom-call | tf_op jit(solution)/shard_map/level_4/pallas_call | solution.py:441
  11.9 0.1 collective-permute-done.2.got
  12.0 2.1 %collective-permute-start.3 = (bf16[768,128]{1,0:T(8,128)(2,1)S(1)}, bf16[768,128]{1,0:T(8,128)(2,1)S(1)}, u32[]{:S(2)}, u32[]{:S(2)}) collective-permute-start(bf16[768,128]{1,0:T(8,128)(2,1)S(1)} %place.1.own), channel_id=1, source_target_pairs={{0,4},{1,3},{2,6},{3,1},{4,0},{5,7},{6,2},{7,5},{8,12},{9,11},{10,... | collective-permute-start | bytes 589832 | tf_op jit(solution)/shard_map/ppermute | solution.py:96
  14.2 3.6 %collective-permute-done.3.got = bf16[768,128]{1,0:T(8,128)(2,1)S(1)} collective-permute-done((bf16[768,128]{1,0:T(8,128)(2,1)S(1)}, bf16[768,128]{1,0:T(8,128)(2,1)S(1)}, u32[]{:S(2)}, u32[]{:S(2)}) %collective-permute-start.3) | collective-permute-done | bytes 196640 | tf_op jit(solution)/shard_map/ppermute | solution.py:96
  17.8 0.1 collective-permute-start.4
  18.0 2.1 %collective-permute-start.6 = (bf16[256,128]{1,0:T(8,128)(2,1)S(1)}, bf16[256,128]{1,0:T(8,128)(2,1)S(1)}, u32[]{:S(2)}, u32[]{:S(2)}) collective-permute-start(bf16[256,128]{1,0:T(8,128)(2,1)S(1)} %early_z.1.after.own), channel_id=1, source_target_pairs={{0,8},{1,9},{2,10},{3,11},{4,12},{5,13},{6,14},{7,15},{8,0},{9,1},... | collective-permute-start | bytes 196616 | tf_op jit(solution)/shard_map/ppermute | solution.py:96
  20.1 0.0 collective-permute-done.4.got
  20.1 0.3 %level_3.1 = (bf16[144,128]{1,0:T(8,128)(2,1)S(1)}, bf16[64,128]{1,0:T(8,128)(2,1)S(1)}, bf16[64,128]{1,0:T(8,128)(2,1)S(1)}, bf16[256,128]{1,0:T(8,128)(2,1)S(1)}) custom-call(bf16[960,128]{1,0:T(8,128)(2,1)S(1)} %get-tuple-element.33.own, bf16[960,128]{1,0:T(8,128)(2,1)S(1)} %collective-permute-done.4.got, bf16[256,128]{1,0:T(8,128)(2,1)S(1)} %early_z.1.after.own), custom_call_target="tpu_custom_call" | custom-call | tf_op jit(solution)/shard_map/level_3/pallas_call | solution.py:441
  20.4 1.5 %collective-permute-start.5 = (bf16[144,128]{1,0:T(8,128)(2,1)S(1)}, bf16[144,128]{1,0:T(8,128)(2,1)S(1)}, u32[]{:S(2)}, u32[]{:S(2)}) collective-permute-start(bf16[144,128]{1,0:T(8,128)(2,1)S(1)} %get-tuple-element.35.own), channel_id=1, source_target_pairs={{0,8},{1,9},{2,10},{3,11},{4,12},{5,13},{6,14},{7,15},{8,0},{9,1},... | collective-permute-start | bytes 110600 | tf_op jit(solution)/shard_map/ppermute | solution.py:96
  21.9 1.1 %collective-permute-done.6.got = bf16[256,128]{1,0:T(8,128)(2,1)S(1)} collective-permute-done((bf16[256,128]{1,0:T(8,128)(2,1)S(1)}, bf16[256,128]{1,0:T(8,128)(2,1)S(1)}, u32[]{:S(2)}, u32[]{:S(2)}) %collective-permute-start.6) | collective-permute-done | bytes 65568 | tf_op jit(solution)/shard_map/ppermute | solution.py:96
  23.0 0.1 collective-permute-start.7
  23.2 0.4 %collective-permute-start.8 = (bf16[128,128]{1,0:T(8,128)(2,1)S(1)}, bf16[128,128]{1,0:T(8,128)(2,1)S(1)}, u32[]{:S(2)}, u32[]{:S(2)}) collective-permute-start(bf16[128,128]{1,0:T(8,128)(2,1)S(1)} %get-tuple-element.38.m1), channel_id=1, source_target_pairs={{0,1},{1,0},{2,3},{3,2},{4,5},{5,4},{6,7},{7,6},{8,9},{9,8},{10,11... | collective-permute-start | bytes 98312 | tf_op jit(solution)/shard_map/ppermute | solution.py:96
  23.6 0.7 %collective-permute-done.7.o0 = bf16[128,128]{1,0:T(8,128)(2,1)S(1)} collective-permute-done((bf16[128,128]{1,0:T(8,128)(2,1)S(1)}, bf16[128,128]{1,0:T(8,128)(2,1)S(1)}, u32[]{:S(2)}, u32[]{:S(2)}) %collective-permute-start.7) | collective-permute-done | bytes 32800 | tf_op jit(solution)/shard_map/ppermute | solution.py:96
  24.3 0.2 collective-permute-done.8.o1
  24.5 0.0 collective-permute-done.5.got
  24.5 0.1 level_2.1
  24.6 2.8 %collective-permute-start.9 = (bf16[64,128]{1,0:T(8,128)(2,1)S(1)}, bf16[64,128]{1,0:T(8,128)(2,1)S(1)}, u32[]{:S(2)}, u32[]{:S(2)}) collective-permute-start(bf16[64,128]{1,0:T(8,128)(2,1)S(1)} %get-tuple-element.39.own), channel_id=1, source_target_pairs={{0,16},{1,17},{2,18},{3,19},{4,20},{5,21},{6,22},{7,23},{8,24},{9,... | collective-permute-start | bytes 49160 | tf_op jit(solution)/shard_map/ppermute | solution.py:96
  27.4 0.3 early.1.rest
  27.7 0.5 %basis_1.1.basis = bf16[256,2048]{1,0:T(8,128)(2,1)S(1)} custom-call(bf16[128,128]{1,0:T(8,128)(2,1)S(1)} %get-tuple-element.37.m0, bf16[128,128]{1,0:T(8,128)(2,1)S(1)} %get-tuple-element.38.m1, bf16[128,128]{1,0:T(8,128)(2,1)S(1)} %collective-permute-done.7.o0, bf16[128,128]{1,0:T(8,128)(2,1)S(1)} %collective-permute-done.8.o1, ...), custom_call_target="tpu_custom_call" | custom-call | flops 134217728 | bytes 1572864 | tf_op jit(solution)/shard_map/basis_1/pallas_call | solution.py:441
  28.2 0.4 %middle.1.rest = f32[64,2048]{1,0:T(8,128)S(1)} custom-call(f32[64,2048]{1,0:T(8,128)S(1)} %early.1.rest, bf16[128,2048]{1,0:T(8,128)(2,1)S(1)} %get-tuple-element.44.s2, bf16[64,256]{1,0:T(8,128)(2,1)S(1)} %get-tuple-element.45.stacked, bf16[256,128]{1,0:T(8,128)(2,1)S(1)} %get-tuple-element.46.rows), custom_call_target="tpu_custom_call" | custom-call | flops 33554432 | bytes 1048576 | tf_op jit(solution)/shard_map/middle/pallas_call | solution.py:441
  28.5 0.7 %collective-permute-done.9.got = bf16[64,128]{1,0:T(8,128)(2,1)S(1)} collective-permute-done((bf16[64,128]{1,0:T(8,128)(2,1)S(1)}, bf16[64,128]{1,0:T(8,128)(2,1)S(1)}, u32[]{:S(2)}, u32[]{:S(2)}) %collective-permute-start.9) | collective-permute-done | bytes 16416 | tf_op jit(solution)/shard_map/ppermute | solution.py:96
  29.3 1.0 %last.1 = f32[64,2048]{1,0:T(8,128)} custom-call(bf16[64,128]{1,0:T(8,128)(2,1)S(1)} %get-tuple-element.39.own, bf16[64,128]{1,0:T(8,128)(2,1)S(1)} %collective-permute-done.9.got, f32[64,2048]{1,0:T(8,128)S(1)} %middle.1.rest, bf16[256,2048]{1,0:T(8,128)(2,1)S(1)} %basis_1.1.basis), custom_call_target="tpu_custom_call" | custom-call | tf_op jit(solution)/shard_map/last/pallas_call | solution.py:554
  (5 shorter events, 0.1 us)
Async XLA Ops:
  3.0 1.6 %collective-permute-start = (bf16[848,128]{1,0:T(8,128)(2,1)S(1)}, bf16[848,128]{1,0:T(8,128)(2,1)S(1)}, u32[]{:S(2)}, u32[]{:S(2)}) collective-permute-start(bf16[848,128]{1,0:T(8,128)(2,1)S(1)} %get-tuple-element.27), channel_id=1, source_target_pairs={{0,1},{1,0},{2,3},{3,2},{4,5},{5,4},{6,7},{7,6},{8,9},{9,8},{10,11... | collective-permute-start | bytes 651272 | tf_op jit(solution)/shard_map/ppermute | solution.py:96
  4.7 6.9 %collective-permute-start.1 = (bf16[896,128]{1,0:T(8,128)(2,1)S(1)}, bf16[896,128]{1,0:T(8,128)(2,1)S(1)}, u32[]{:S(2)}, u32[]{:S(2)}) collective-permute-start(bf16[896,128]{1,0:T(8,128)(2,1)S(1)} %get-tuple-element.28.after.own), channel_id=1, source_target_pairs={{0,2},{1,5},{2,0},{3,7},{4,6},{5,1},{6,4},{7,3},{8,10},{9,13},{10,... | collective-permute-start | bytes 688136 | tf_op jit(solution)/shard_map/ppermute | solution.py:96
  7.6 4.4 %collective-permute-start.2 = (bf16[160,128]{1,0:T(8,128)(2,1)S(1)}, bf16[160,128]{1,0:T(8,128)(2,1)S(1)}, u32[]{:S(2)}, u32[]{:S(2)}) collective-permute-start(bf16[160,128]{1,0:T(8,128)(2,1)S(1)} %get-tuple-element.31.own), channel_id=1, source_target_pairs={{0,2},{1,5},{2,0},{3,7},{4,6},{5,1},{6,4},{7,3},{8,10},{9,13},{10,... | collective-permute-start | bytes 122888 | tf_op jit(solution)/shard_map/ppermute | solution.py:96
  12.0 5.8 %collective-permute-start.3 = (bf16[768,128]{1,0:T(8,128)(2,1)S(1)}, bf16[768,128]{1,0:T(8,128)(2,1)S(1)}, u32[]{:S(2)}, u32[]{:S(2)}) collective-permute-start(bf16[768,128]{1,0:T(8,128)(2,1)S(1)} %place.1.own), channel_id=1, source_target_pairs={{0,4},{1,3},{2,6},{3,1},{4,0},{5,7},{6,2},{7,5},{8,12},{9,11},{10,... | collective-permute-start | bytes 589832 | tf_op jit(solution)/shard_map/ppermute | solution.py:96
  17.8 2.3 %collective-permute-start.4 = (bf16[960,128]{1,0:T(8,128)(2,1)S(1)}, bf16[960,128]{1,0:T(8,128)(2,1)S(1)}, u32[]{:S(2)}, u32[]{:S(2)}) collective-permute-start(bf16[960,128]{1,0:T(8,128)(2,1)S(1)} %get-tuple-element.33.own), channel_id=1, source_target_pairs={{0,1},{1,0},{2,3},{3,2},{4,5},{5,4},{6,7},{7,6},{8,9},{9,8},{10,11... | collective-permute-start | bytes 737288 | tf_op jit(solution)/shard_map/ppermute | solution.py:96
  18.0 5.1 %collective-permute-start.6 = (bf16[256,128]{1,0:T(8,128)(2,1)S(1)}, bf16[256,128]{1,0:T(8,128)(2,1)S(1)}, u32[]{:S(2)}, u32[]{:S(2)}) collective-permute-start(bf16[256,128]{1,0:T(8,128)(2,1)S(1)} %early_z.1.after.own), channel_id=1, source_target_pairs={{0,8},{1,9},{2,10},{3,11},{4,12},{5,13},{6,14},{7,15},{8,0},{9,1},... | collective-permute-start | bytes 196616 | tf_op jit(solution)/shard_map/ppermute | solution.py:96
  20.4 4.0 %collective-permute-start.5 = (bf16[144,128]{1,0:T(8,128)(2,1)S(1)}, bf16[144,128]{1,0:T(8,128)(2,1)S(1)}, u32[]{:S(2)}, u32[]{:S(2)}) collective-permute-start(bf16[144,128]{1,0:T(8,128)(2,1)S(1)} %get-tuple-element.35.own), channel_id=1, source_target_pairs={{0,8},{1,9},{2,10},{3,11},{4,12},{5,13},{6,14},{7,15},{8,0},{9,1},... | collective-permute-start | bytes 110600 | tf_op jit(solution)/shard_map/ppermute | solution.py:96
  23.0 1.3 %collective-permute-start.7 = (bf16[128,128]{1,0:T(8,128)(2,1)S(1)}, bf16[128,128]{1,0:T(8,128)(2,1)S(1)}, u32[]{:S(2)}, u32[]{:S(2)}) collective-permute-start(bf16[128,128]{1,0:T(8,128)(2,1)S(1)} %get-tuple-element.37.m0), channel_id=1, source_target_pairs={{0,1},{1,0},{2,3},{3,2},{4,5},{5,4},{6,7},{7,6},{8,9},{9,8},{10,11... | collective-permute-start | bytes 98312 | tf_op jit(solution)/shard_map/ppermute | solution.py:96
  23.2 1.3 %collective-permute-start.8 = (bf16[128,128]{1,0:T(8,128)(2,1)S(1)}, bf16[128,128]{1,0:T(8,128)(2,1)S(1)}, u32[]{:S(2)}, u32[]{:S(2)}) collective-permute-start(bf16[128,128]{1,0:T(8,128)(2,1)S(1)} %get-tuple-element.38.m1), channel_id=1, source_target_pairs={{0,1},{1,0},{2,3},{3,2},{4,5},{5,4},{6,7},{7,6},{8,9},{9,8},{10,11... | collective-permute-start | bytes 98312 | tf_op jit(solution)/shard_map/ppermute | solution.py:96
  24.6 4.6 %collective-permute-start.9 = (bf16[64,128]{1,0:T(8,128)(2,1)S(1)}, bf16[64,128]{1,0:T(8,128)(2,1)S(1)}, u32[]{:S(2)}, u32[]{:S(2)}) collective-permute-start(bf16[64,128]{1,0:T(8,128)(2,1)S(1)} %get-tuple-element.39.own), channel_id=1, source_target_pairs={{0,16},{1,17},{2,18},{3,19},{4,20},{5,21},{6,22},{7,23},{8,24},{9,... | collective-permute-start | bytes 49160 | tf_op jit(solution)/shard_map/ppermute | solution.py:96

commit v8 on v7

--- a/solution.py
+++ b/solution.py
@@ -10,7 +10,7 @@
 BF = jnp.bfloat16
 F32 = jnp.float32
 LEVELS = (4, 3, 2, 1)
-LATE = (("c", 3), ("c", 1))
+LATE = (("p", 2), ("p", 1), ("g", 4, 2), ("g", 4, 1))
 SHARES = ((4, 3, 1), (2,))
 VMEM = pl.BlockSpec(memory_space=pltpu.VMEM)
 HBM = pl.BlockSpec(memory_space=pltpu.HBM)
@@ -56,16 +56,13 @@
         late = {key: z - a for key, (a, z) in first.items() if key in LATE}
         self.aside = spread(late)
         self.child = (spread({key: z - a for key, (a, z) in first.items() if key not in LATE}), second)
-        self.after_4 = (
-            spread({("p", 3): w, ("p", 2): w, ("p", 1): w, ("c", 3): 8 * rows[3], ("c", 1): 8 * rows[1]}),
-            spread(
-                {
-                    **{("own", 3, k): r for k in (2, 1)},
-                    **{("sib", 3, k): r for k in (2, 1)},
-                    ("g", 2, 1): r,
-                    **{("c", 2, y): 4 * rows[2] for y in (0, 1)},
-                }
-            ),
+        self.near = (
+            spread({("p", 3): w, ("c", 3): 8 * rows[3]}),
+            spread({("own", 3, 2): r, ("sib", 3, 2): r, ("own", 3, 1): r, **{("c", 2, y): 4 * rows[2] for y in (0, 1)}}),
+        )
+        self.far = (
+            spread({("p", 2): w, ("p", 1): w, ("c", 1): 8 * rows[1]}),
+            spread({("sib", 3, 1): r, ("g", 2, 1): r}),
         )
         self.before_3 = (
             spread(
@@ -214,11 +211,11 @@
     return jnp.concatenate([tn(rows[:rank], gram), tn(rows[rank:], gram)], axis=0)
 
 
-def kernel_4(plan, bits, rank, own, got, after, out, w4):
+def kernel_4(plan, bits, rank, own, got, after, near, far, weights):
     del after
 
     def first():
-        spans, then = plan.child[0][0], plan.after_4[0][0]
+        spans = plan.child[0][0]
 
         def both(key):
             lo, hi = spans[key]
@@ -227,21 +224,24 @@
         upper = index_bit(bits - 4) == 1
         stacked = jnp.concatenate(ordered(*both(("p", 4)), upper), axis=1)
         w = solve(stacked, *both(("c", 4)), rank)
-        w4[...] = w[:, :rank]
-        below = (3, 2, 1)
-        pairs = [both(("g", 4, k)) for k in below]
-        change = effect(w, [p[0] for p in pairs], [p[1] for p in pairs])
-        for i, k in enumerate(below):
-            a, z = both(("p", k))
-            lo, hi = then[("p", k)]
-            out[lo:hi] = (a.astype(F32) + z.astype(F32) - change[:, i * rank : (i + 1) * rank]).astype(BF)
+        weights[...] = w
+        a, z = both(("g", 4, 3))
+        change = effect(w, [a], [z])
+        a, z = both(("p", 3))
+        lo, hi = plan.near[0][0][("p", 3)]
+        near[lo:hi] = (a.astype(F32) + z.astype(F32) - change).astype(BF)
+        for key, out, then in ((("c", 3), near, plan.near[0][0]), (("c", 1), far, plan.far[0][0])):
+            lo, hi = then[key]
+            out[lo:hi] = interleave(*ordered(*both(key), upper))
 
     def second():
-        spans, then = plan.child[1][0], plan.after_4[1][0]
+        spans = plan.child[1][0]
         upper = index_bit(bits - 3) == 1
 
         def put(key, value):
-            out[then[key][0] : then[key][1]] = value
+            for out, then in ((near, plan.near[1][0]), (far, plan.far[1][0])):
+                if key in then:
+                    out[then[key][0] : then[key][1]] = value
 
         for key, (lo, hi) in spans.items():
             a, z = own[lo:hi], got[lo:hi]
@@ -253,49 +253,65 @@
                 put(("sib", *key[1:]), z)
             else:
                 put(key, plus(a, z))
-        w4[...] = jnp.zeros_like(w4)
+        weights[...] = jnp.zeros_like(weights)
 
     by_role(first, second)
 
 
-def place_kernel(plan, bits, before, own, got, out):
+def place_kernel(plan, bits, rank, before, own, got, weights, out):
     del before
 
     def first():
-        for key, (lo, hi) in plan.aside[0].items():
-            value = interleave(*ordered(own[lo:hi], got[lo:hi], index_bit(bits - 4) == 1))
-            lo, hi = plan.after_4[0][0][key]
+        def both(key):
+            lo, hi = plan.aside[0][key]
+            return own[lo:hi], got[lo:hi]
+
+        def put(key, value):
+            lo, hi = plan.far[0][0][key]
             out[lo:hi] = value
 
+        below = (2, 1)
+        pairs = [both(("g", 4, k)) for k in below]
+        change = effect(weights[...], [p[0] for p in pairs], [p[1] for p in pairs])
+        for i, k in enumerate(below):
+            a, z = both(("p", k))
+            put(("p", k), (a.astype(F32) + z.astype(F32) - change[:, i * rank : (i + 1) * rank]).astype(BF))
+
     pl.when(index_bit(0) == 0)(first)
 
 
-def gather_kernel(plan, bits, own, got, w4, out, gram):
+def gather_kernel(plan, bits, rank, own_n, got_n, own_f, got_f, weights, out, gram):
+    def keys(role):
+        return (*plan.near[role][0], *plan.far[role][0])
+
+    def both(role, key):
+        if key in plan.near[role][0]:
+            lo, hi = plan.near[role][0][key]
+            return own_n[lo:hi], got_n[lo:hi]
+        lo, hi = plan.far[role][0][key]
+        return own_f[lo:hi], got_f[lo:hi]
+
     def first():
-        spans, then = plan.after_4[0][0], plan.before_3[0][0]
-        for key, (lo, hi) in spans.items():
+        then = plan.before_3[0][0]
+        for key in keys(0):
             if key != ("c", 1):
-                for side, ref in (("own", own), ("sib", got)):
+                for side, value in zip(("own", "sib"), both(0, key)):
                     to = then[(side, "c" if key[0] == "c" else key[1])]
-                    out[to[0] : to[1]] = ref[lo:hi]
-        out[then["w4"][0] : then["w4"][1]] = w4[...]
-        lo, hi = spans[("c", 1)]
-        gram[...] = interleave(*ordered(own[lo:hi], got[lo:hi], index_bit(bits - 3) == 1))
+                    out[to[0] : to[1]] = value
+        out[then["w4"][0] : then["w4"][1]] = weights[:, :rank]
+        gram[...] = interleave(*ordered(*both(0, ("c", 1)), index_bit(bits - 3) == 1))
 
     def second():
-        spans, then = plan.after_4[1][0], plan.before_3[1][0]
+        then = plan.before_3[1][0]
         upper = index_bit(bits - 4) == 1
-        for key, (lo, hi) in spans.items():
+        for key in keys(1):
             if key[0] != "c":
-                value = plus(own[lo:hi], got[lo:hi])
+                value = plus(*both(1, key))
                 if key in then:
                     out[then[key][0] : then[key][1]] = value
                 else:
                     gram[...] = value
-        rows = []
-        for y in (0, 1):
-            lo, hi = spans[("c", 2, y)]
-            rows.append(interleave(*ordered(own[lo:hi], got[lo:hi], upper)))
+        rows = [interleave(*ordered(*both(1, ("c", 2, y)), upper)) for y in (0, 1)]
         to = then[("c", 2)]
         out[to[0] : to[1]] = interleave(*rows)
 
@@ -501,14 +517,16 @@
             for k in LEVELS:
                 got = swap(parts[k], bit, bit)
                 parts[k] = jnp.concatenate(ordered(parts[k], got, upper), axis=1)
-        shares = []
+        pieces = [{}, {}]
         for role in (0, 1):
-            share = [both[role, : device[role][1]]]
-            share += [parts[k].reshape(-1, rank) for k in SHARES[role] if ("c", k) not in LATE]
-            share = jnp.concatenate(share, axis=0)
-            shares.append(jnp.pad(share, ((0, size - share.shape[0]), (0, 0))))
+            for key, (lo, hi) in device[role][0].items():
+                pieces[role][key] = both[role, lo:hi]
+            for k in SHARES[role]:
+                pieces[role][("c", k)] = parts[k].reshape(-1, rank)
+        shares = [jnp.concatenate([pieces[role][k] for k in plan.child[role][0]], axis=0) for role in (0, 1)]
+        shares = [jnp.pad(x, ((0, size - x.shape[0]), (0, 0))) for x in shares]
         buf = jnp.where(index_bit(0) == 1, shares[1], shares[0])
-        aside = jnp.concatenate([parts[k].reshape(-1, rank) for _, k in LATE], axis=0)
+        aside = jnp.concatenate([pieces[0][k] for k in plan.aside[0]], axis=0)
 
     weight = jax.ShapeDtypeStruct((width, rank), BF)
     wide = jax.ShapeDtypeStruct((width, points), F32)
@@ -525,13 +543,17 @@
         cost_estimate=cost(0, 4 * width * points + 8 * rank * points),
         name="fetch",
     )(buf, *[stay(x) for x in (right_solved, s4, s3, s2, s1)])
-    shapes = [buffer(Plan.total(plan.after_4)), weight]
-    buf, w4 = vmem_call(functools.partial(kernel_4, plan, bits, rank), (buf, got, s1_v), shapes, "level_4")
-    place = functools.partial(place_kernel, plan, bits)
-    (buf,) = vmem_call(place, (buf, aside, got_aside), [buffer(Plan.total(plan.after_4))], "place", input_output_aliases={0: 0})
-    got = swap(buf, bits - 3, bits - 4)
+    both_weights = jax.ShapeDtypeStruct((width, 2 * rank), BF)
+    shapes = [buffer(Plan.total(plan.near)), buffer(Plan.total(plan.far)), both_weights]
+    near, far, weights = vmem_call(functools.partial(kernel_4, plan, bits, rank), (buf, got, s1_v), shapes, "level_4")
+    got_near = swap(near, bits - 3, bits - 4)
+    place = functools.partial(place_kernel, plan, bits, rank)
+    operands = (far, aside, got_aside, weights)
+    (far,) = vmem_call(place, operands, [buffer(Plan.total(plan.far))], "place", input_output_aliases={0: 0})
+    got_far = swap(far, bits - 3, bits - 4)
     shapes = [buffer(Plan.total(plan.before_3)), buffer(rank)]
-    buf, gram = vmem_call(functools.partial(gather_kernel, plan, bits), (buf, got, w4), shapes, "gather")
+    operands = (near, got_near, far, got_far, weights)
+    buf, gram = vmem_call(functools.partial(gather_kernel, plan, bits, rank), operands, shapes, "gather")
     got = swap(buf, 0, 0)
     (own_z,) = vmem_call(functools.partial(early_z_kernel, plan, rank), (buf, gram), [buffer(2 * rank)], "early_z")
     got_z = swap(own_z, bits - 2, bits - 2)

time: 30.4 us -> 30.2 us (level)
  waiting for transfers between devices: 9.76 us -> 9.33 us
    ppermute x10 -> x11, waiting for transfers between devices: 9.76 us -> 9.33 us  [swap(): lax.ppermute(x, 'pts', [(i, i ^ 1 << (odd if i & 1 else even)) for i in r...]
    ppermute x10 -> x11, starting transfers between devices: 12.6 us -> 12.7 us  [swap(): lax.ppermute(x, 'pts', [(i, i ^ 1 << (odd if i & 1 else even)) for i in r...]
  transfers between devices with their start and end apart: 10 -> 11, of which waited for: 8 -> 7; matrix products, arithmetic and copies ran while one was open for 0% -> 0% of each run, Pallas kernels for 12% -> 12%
where the time goes in v8:
time: 30.2 us; the launch traced here: 30 us
  starting transfers between devices  12.7 us (42%)
  waiting for transfers between devices  9.33 us (31%)
  Pallas kernels  7.9 us (26%)
    ppermute x11, starting transfers between devices, swap(): lax.ppermute(x, 'pts', [(i, i ^ 1 << (odd if i & 1 else even)) for i in r...  12.7 us
    ppermute x11, waiting for transfers between devices, swap(): lax.ppermute(x, 'pts', [(i, i ^ 1 << (odd if i & 1 else even)) for i in r...  9.33 us
    pallas_call x1, Pallas kernels, on_device(): pl.pallas_call(lambda *refs: first_kernel([t for t, _ in device], rank, w...  2.98 us
    pallas_call x11, Pallas kernels, vmem_call(): pl.pallas_call(kernel, out_shape=shapes, in_specs=[VMEM] * len(operands),...  2.17 us
    pallas_call x1, Pallas kernels, on_device(): pl.pallas_call(fetch_kernel, out_shape=[wide] + [base] * 4, in_specs=[VME...  1.71 us
    pallas_call x1, Pallas kernels, on_device(): pl.pallas_call(functools.partial(last_kernel, bits, chunks), out_shape=wi...  1.03 us
  transfers between devices with their start and end apart: 11, of which 7 were waited for; matrix products, arithmetic and copies ran while one was open for 0% of the time, Pallas kernels for 12%

profile of v8, /device:TPU:0, one launch (start us, length us, event | category | flops | bytes accessed | tf_op | source)
XLA Modules:
  0.0 30.0 jit_solution(3572655481381290829)
XLA Ops:
  0.0 3.0 %products.1 = (bf16[848,128]{1,0:T(8,128)(2,1)S(1)}, bf16[848,128]{1,0:T(8,128)(2,1)S(1)}) custom-call(f32[64,2048]{1,0:T(8,128)} %refs_0_.3, bf16[128,2048]{1,0:T(8,128)(2,1)} %refs_1_.2, bf16[128,2048]{1,0:T(8,128)(2,1)} %refs_2_.2, bf16[128,2048]{1,0:T(8,128)(2,1)} %refs_1_.3, bf16[128,2048]{1,0:T(8,128)(2,1)} %refs_2_.3, bf16[128,2048]{1,0:T(8,128)(2,1)} %refs_3_.3, ...), custom_call_target="tpu_custom_call" | custom-call | tf_op jit(solution)/shard_map/products/pallas_call | solution.py:483
  3.0 0.5 %collective-permute-start = (bf16[848,128]{1,0:T(8,128)(2,1)S(1)}, bf16[848,128]{1,0:T(8,128)(2,1)S(1)}, u32[]{:S(2)}, u32[]{:S(2)}) collective-permute-start(bf16[848,128]{1,0:T(8,128)(2,1)S(1)} %get-tuple-element.28), channel_id=1, source_target_pairs={{0,1},{1,0},{2,3},{3,2},{4,5},{5,4},{6,7},{7,6},{8,9},{9,8},{10,11... | collective-permute-start | bytes 651272 | tf_op jit(solution)/shard_map/ppermute | solution.py:93
  3.5 1.1 %collective-permute-done.got = bf16[848,128]{1,0:T(8,128)(2,1)S(1)} collective-permute-done((bf16[848,128]{1,0:T(8,128)(2,1)S(1)}, bf16[848,128]{1,0:T(8,128)(2,1)S(1)}, u32[]{:S(2)}, u32[]{:S(2)}) %collective-permute-start) | collective-permute-done | bytes 217120 | tf_op jit(solution)/shard_map/ppermute | solution.py:93
  4.7 2.9 %collective-permute-start.1 = (bf16[672,128]{1,0:T(8,128)(2,1)S(1)}, bf16[672,128]{1,0:T(8,128)(2,1)S(1)}, u32[]{:S(2)}, u32[]{:S(2)}) collective-permute-start(bf16[672,128]{1,0:T(8,128)(2,1)S(1)} %get-tuple-element.29.after.own), channel_id=1, source_target_pairs={{0,2},{1,5},{2,0},{3,7},{4,6},{5,1},{6,4},{7,3},{8,10},{9,13},{10,... | collective-permute-start | bytes 516104 | tf_op jit(solution)/shard_map/ppermute | solution.py:93
  7.6 0.1 collective-permute-start.3
  7.7 1.7 %fetch.1 = (f32[64,2048]{1,0:T(8,128)S(1)}, bf16[128,2048]{1,0:T(8,128)(2,1)S(1)}, bf16[128,2048]{1,0:T(8,128)(2,1)S(1)}, bf16[128,2048]{1,0:T(8,128)(2,1)S(1)}, bf16[128,2048]{1,0:T(8,128)(2,1)S(1)}) custom-call(bf16[672,128]{1,0:T(8,128)(2,1)S(1)} %get-tuple-element.29.after.own, f32[64,2048]{1,0:T(8,128)} %refs_0_.3, bf16[128,2048]{1,0:T(8,128)(2,1)} %refs_1_.3, ...), custom_call_target="tpu_custom_call" | custom-call | bytes 2621440 | tf_op jit(solution)/shard_map/fetch/pallas_call | solution.py:536
  9.4 1.6 %collective-permute-done.1.got = bf16[672,128]{1,0:T(8,128)(2,1)S(1)} collective-permute-done((bf16[672,128]{1,0:T(8,128)(2,1)S(1)}, bf16[672,128]{1,0:T(8,128)(2,1)S(1)}, u32[]{:S(2)}, u32[]{:S(2)}) %collective-permute-start.1) | collective-permute-done | bytes 172064 | tf_op jit(solution)/shard_map/ppermute | solution.py:93
  11.0 0.3 %level_4.1 = (bf16[512,128]{1,0:T(8,128)(2,1)S(1)}, bf16[256,128]{1,0:T(8,128)(2,1)S(1)}, bf16[64,256]{1,0:T(8,128)(2,1)S(1)}) custom-call(bf16[672,128]{1,0:T(8,128)(2,1)S(1)} %get-tuple-element.29.after.own, bf16[672,128]{1,0:T(8,128)(2,1)S(1)} %collective-permute-done.1.got, bf16[128,2048]{1,0:T(8,128)(2,1)S(1)} %get-tuple-element.30.after.s1), custom_call_target="tpu_custom_call" | custom-call | tf_op jit(solution)/shard_map/level_4/pallas_call | solution.py:457
  11.3 2.1 %collective-permute-start.2 = (bf16[512,128]{1,0:T(8,128)(2,1)S(1)}, bf16[512,128]{1,0:T(8,128)(2,1)S(1)}, u32[]{:S(2)}, u32[]{:S(2)}) collective-permute-start(bf16[512,128]{1,0:T(8,128)(2,1)S(1)} %get-tuple-element.31.own_n), channel_id=1, source_target_pairs={{0,4},{1,3},{2,6},{3,1},{4,0},{5,7},{6,2},{7,5},{8,12},{9,11},{10,... | collective-permute-start | bytes 393224 | tf_op jit(solution)/shard_map/ppermute | solution.py:93
  13.4 0.0 collective-permute-done.3.got
  13.4 0.2 place.1.own_f
  13.6 0.7 %collective-permute-start.4 = (bf16[256,128]{1,0:T(8,128)(2,1)S(1)}, bf16[256,128]{1,0:T(8,128)(2,1)S(1)}, u32[]{:S(2)}, u32[]{:S(2)}) collective-permute-start(bf16[256,128]{1,0:T(8,128)(2,1)S(1)} %place.1.own_f), channel_id=1, source_target_pairs={{0,4},{1,3},{2,6},{3,1},{4,0},{5,7},{6,2},{7,5},{8,12},{9,11},{10,... | collective-permute-start | bytes 196616 | tf_op jit(solution)/shard_map/ppermute | solution.py:93
  14.3 3.6 %collective-permute-done.4.got_f = bf16[256,128]{1,0:T(8,128)(2,1)S(1)} collective-permute-done((bf16[256,128]{1,0:T(8,128)(2,1)S(1)}, bf16[256,128]{1,0:T(8,128)(2,1)S(1)}, u32[]{:S(2)}, u32[]{:S(2)}) %collective-permute-start.4) | collective-permute-done | bytes 65568 | tf_op jit(solution)/shard_map/ppermute | solution.py:93
  17.9 0.0 collective-permute-done.2.got_n
  17.9 0.1 collective-permute-start.5
  18.0 1.6 %collective-permute-start.7 = (bf16[256,128]{1,0:T(8,128)(2,1)S(1)}, bf16[256,128]{1,0:T(8,128)(2,1)S(1)}, u32[]{:S(2)}, u32[]{:S(2)}) collective-permute-start(bf16[256,128]{1,0:T(8,128)(2,1)S(1)} %early_z.1.after.own), channel_id=1, source_target_pairs={{0,8},{1,9},{2,10},{3,11},{4,12},{5,13},{6,14},{7,15},{8,0},{9,1},... | collective-permute-start | bytes 196616 | tf_op jit(solution)/shard_map/ppermute | solution.py:93
  19.7 0.0 collective-permute-done.5.got
  19.7 0.3 %level_3.1 = (bf16[144,128]{1,0:T(8,128)(2,1)S(1)}, bf16[64,128]{1,0:T(8,128)(2,1)S(1)}, bf16[64,128]{1,0:T(8,128)(2,1)S(1)}, bf16[256,128]{1,0:T(8,128)(2,1)S(1)}) custom-call(bf16[960,128]{1,0:T(8,128)(2,1)S(1)} %get-tuple-element.35.own, bf16[960,128]{1,0:T(8,128)(2,1)S(1)} %collective-permute-done.5.got, bf16[256,128]{1,0:T(8,128)(2,1)S(1)} %early_z.1.after.own), custom_call_target="tpu_custom_call" | custom-call | tf_op jit(solution)/shard_map/level_3/pallas_call | solution.py:457
  20.0 1.5 %collective-permute-start.6 = (bf16[144,128]{1,0:T(8,128)(2,1)S(1)}, bf16[144,128]{1,0:T(8,128)(2,1)S(1)}, u32[]{:S(2)}, u32[]{:S(2)}) collective-permute-start(bf16[144,128]{1,0:T(8,128)(2,1)S(1)} %get-tuple-element.37.own), channel_id=1, source_target_pairs={{0,8},{1,9},{2,10},{3,11},{4,12},{5,13},{6,14},{7,15},{8,0},{9,1},... | collective-permute-start | bytes 110600 | tf_op jit(solution)/shard_map/ppermute | solution.py:93
  21.5 1.3 %collective-permute-done.7.got = bf16[256,128]{1,0:T(8,128)(2,1)S(1)} collective-permute-done((bf16[256,128]{1,0:T(8,128)(2,1)S(1)}, bf16[256,128]{1,0:T(8,128)(2,1)S(1)}, u32[]{:S(2)}, u32[]{:S(2)}) %collective-permute-start.7) | collective-permute-done | bytes 65568 | tf_op jit(solution)/shard_map/ppermute | solution.py:93
  22.8 0.1 collective-permute-start.8
  22.8 0.5 %collective-permute-start.9 = (bf16[128,128]{1,0:T(8,128)(2,1)S(1)}, bf16[128,128]{1,0:T(8,128)(2,1)S(1)}, u32[]{:S(2)}, u32[]{:S(2)}) collective-permute-start(bf16[128,128]{1,0:T(8,128)(2,1)S(1)} %get-tuple-element.40.m1), channel_id=1, source_target_pairs={{0,1},{1,0},{2,3},{3,2},{4,5},{5,4},{6,7},{7,6},{8,9},{9,8},{10,11... | collective-permute-start | bytes 98312 | tf_op jit(solution)/shard_map/ppermute | solution.py:93
  23.3 0.7 %collective-permute-done.8.o0 = bf16[128,128]{1,0:T(8,128)(2,1)S(1)} collective-permute-done((bf16[128,128]{1,0:T(8,128)(2,1)S(1)}, bf16[128,128]{1,0:T(8,128)(2,1)S(1)}, u32[]{:S(2)}, u32[]{:S(2)}) %collective-permute-start.8) | collective-permute-done | bytes 32800 | tf_op jit(solution)/shard_map/ppermute | solution.py:93
  24.0 0.2 collective-permute-done.9.o1
  24.2 0.0 collective-permute-done.6.got
  24.2 0.1 level_2.1
  24.3 2.6 %collective-permute-start.10 = (bf16[64,128]{1,0:T(8,128)(2,1)S(1)}, bf16[64,128]{1,0:T(8,128)(2,1)S(1)}, u32[]{:S(2)}, u32[]{:S(2)}) collective-permute-start(bf16[64,128]{1,0:T(8,128)(2,1)S(1)} %get-tuple-element.41.own), channel_id=1, source_target_pairs={{0,16},{1,17},{2,18},{3,19},{4,20},{5,21},{6,22},{7,23},{8,24},{9,... | collective-permute-start | bytes 49160 | tf_op jit(solution)/shard_map/ppermute | solution.py:93
  26.9 0.3 early.1.rest
  27.2 0.5 %basis_1.1.basis = bf16[256,2048]{1,0:T(8,128)(2,1)S(1)} custom-call(bf16[128,128]{1,0:T(8,128)(2,1)S(1)} %get-tuple-element.39.m0, bf16[128,128]{1,0:T(8,128)(2,1)S(1)} %get-tuple-element.40.m1, bf16[128,128]{1,0:T(8,128)(2,1)S(1)} %collective-permute-done.8.o0, bf16[128,128]{1,0:T(8,128)(2,1)S(1)} %collective-permute-done.9.o1, ...), custom_call_target="tpu_custom_call" | custom-call | flops 134217728 | bytes 1572864 | tf_op jit(solution)/shard_map/basis_1/pallas_call | solution.py:457
  27.7 0.4 %middle.1.rest = f32[64,2048]{1,0:T(8,128)S(1)} custom-call(f32[64,2048]{1,0:T(8,128)S(1)} %early.1.rest, bf16[128,2048]{1,0:T(8,128)(2,1)S(1)} %get-tuple-element.46.s2, bf16[64,256]{1,0:T(8,128)(2,1)S(1)} %get-tuple-element.47.stacked, bf16[256,128]{1,0:T(8,128)(2,1)S(1)} %get-tuple-element.48.rows), custom_call_target="tpu_custom_call" | custom-call | flops 33554432 | bytes 1048576 | tf_op jit(solution)/shard_map/middle/pallas_call | solution.py:457
  28.1 0.9 %collective-permute-done.10.got = bf16[64,128]{1,0:T(8,128)(2,1)S(1)} collective-permute-done((bf16[64,128]{1,0:T(8,128)(2,1)S(1)}, bf16[64,128]{1,0:T(8,128)(2,1)S(1)}, u32[]{:S(2)}, u32[]{:S(2)}) %collective-permute-start.10) | collective-permute-done | bytes 16416 | tf_op jit(solution)/shard_map/ppermute | solution.py:93
  29.0 1.0 %last.1 = f32[64,2048]{1,0:T(8,128)} custom-call(bf16[64,128]{1,0:T(8,128)(2,1)S(1)} %get-tuple-element.41.own, bf16[64,128]{1,0:T(8,128)(2,1)S(1)} %collective-permute-done.10.got, f32[64,2048]{1,0:T(8,128)S(1)} %middle.1.rest, bf16[256,2048]{1,0:T(8,128)(2,1)S(1)} %basis_1.1.basis), custom_call_target="tpu_custom_call" | custom-call | tf_op jit(solution)/shard_map/last/pallas_call | solution.py:576
  (4 shorter events, 0.1 us)
Async XLA Ops:
  3.0 1.6 %collective-permute-start = (bf16[848,128]{1,0:T(8,128)(2,1)S(1)}, bf16[848,128]{1,0:T(8,128)(2,1)S(1)}, u32[]{:S(2)}, u32[]{:S(2)}) collective-permute-start(bf16[848,128]{1,0:T(8,128)(2,1)S(1)} %get-tuple-element.28), channel_id=1, source_target_pairs={{0,1},{1,0},{2,3},{3,2},{4,5},{5,4},{6,7},{7,6},{8,9},{9,8},{10,11... | collective-permute-start | bytes 651272 | tf_op jit(solution)/shard_map/ppermute | solution.py:93
  4.7 6.3 %collective-permute-start.1 = (bf16[672,128]{1,0:T(8,128)(2,1)S(1)}, bf16[672,128]{1,0:T(8,128)(2,1)S(1)}, u32[]{:S(2)}, u32[]{:S(2)}) collective-permute-start(bf16[672,128]{1,0:T(8,128)(2,1)S(1)} %get-tuple-element.29.after.own), channel_id=1, source_target_pairs={{0,2},{1,5},{2,0},{3,7},{4,6},{5,1},{6,4},{7,3},{8,10},{9,13},{10,... | collective-permute-start | bytes 516104 | tf_op jit(solution)/shard_map/ppermute | solution.py:93
  7.6 5.8 %collective-permute-start.3 = (bf16[384,128]{1,0:T(8,128)(2,1)S(1)}, bf16[384,128]{1,0:T(8,128)(2,1)S(1)}, u32[]{:S(2)}, u32[]{:S(2)}) collective-permute-start(bf16[384,128]{1,0:T(8,128)(2,1)S(1)} %get-tuple-element.33.own), channel_id=1, source_target_pairs={{0,2},{1,5},{2,0},{3,7},{4,6},{5,1},{6,4},{7,3},{8,10},{9,13},{10,... | collective-permute-start | bytes 294920 | tf_op jit(solution)/shard_map/ppermute | solution.py:93
  11.3 6.6 %collective-permute-start.2 = (bf16[512,128]{1,0:T(8,128)(2,1)S(1)}, bf16[512,128]{1,0:T(8,128)(2,1)S(1)}, u32[]{:S(2)}, u32[]{:S(2)}) collective-permute-start(bf16[512,128]{1,0:T(8,128)(2,1)S(1)} %get-tuple-element.31.own_n), channel_id=1, source_target_pairs={{0,4},{1,3},{2,6},{3,1},{4,0},{5,7},{6,2},{7,5},{8,12},{9,11},{10,... | collective-permute-start | bytes 393224 | tf_op jit(solution)/shard_map/ppermute | solution.py:93
  13.6 4.3 %collective-permute-start.4 = (bf16[256,128]{1,0:T(8,128)(2,1)S(1)}, bf16[256,128]{1,0:T(8,128)(2,1)S(1)}, u32[]{:S(2)}, u32[]{:S(2)}) collective-permute-start(bf16[256,128]{1,0:T(8,128)(2,1)S(1)} %place.1.own_f), channel_id=1, source_target_pairs={{0,4},{1,3},{2,6},{3,1},{4,0},{5,7},{6,2},{7,5},{8,12},{9,11},{10,... | collective-permute-start | bytes 196616 | tf_op jit(solution)/shard_map/ppermute | solution.py:93
  17.9 1.8 %collective-permute-start.5 = (bf16[960,128]{1,0:T(8,128)(2,1)S(1)}, bf16[960,128]{1,0:T(8,128)(2,1)S(1)}, u32[]{:S(2)}, u32[]{:S(2)}) collective-permute-start(bf16[960,128]{1,0:T(8,128)(2,1)S(1)} %get-tuple-element.35.own), channel_id=1, source_target_pairs={{0,1},{1,0},{2,3},{3,2},{4,5},{5,4},{6,7},{7,6},{8,9},{9,8},{10,11... | collective-permute-start | bytes 737288 | tf_op jit(solution)/shard_map/ppermute | solution.py:93
  18.0 4.7 %collective-permute-start.7 = (bf16[256,128]{1,0:T(8,128)(2,1)S(1)}, bf16[256,128]{1,0:T(8,128)(2,1)S(1)}, u32[]{:S(2)}, u32[]{:S(2)}) collective-permute-start(bf16[256,128]{1,0:T(8,128)(2,1)S(1)} %early_z.1.after.own), channel_id=1, source_target_pairs={{0,8},{1,9},{2,10},{3,11},{4,12},{5,13},{6,14},{7,15},{8,0},{9,1},... | collective-permute-start | bytes 196616 | tf_op jit(solution)/shard_map/ppermute | solution.py:93
  20.0 4.2 %collective-permute-start.6 = (bf16[144,128]{1,0:T(8,128)(2,1)S(1)}, bf16[144,128]{1,0:T(8,128)(2,1)S(1)}, u32[]{:S(2)}, u32[]{:S(2)}) collective-permute-start(bf16[144,128]{1,0:T(8,128)(2,1)S(1)} %get-tuple-element.37.own), channel_id=1, source_target_pairs={{0,8},{1,9},{2,10},{3,11},{4,12},{5,13},{6,14},{7,15},{8,0},{9,1},... | collective-permute-start | bytes 110600 | tf_op jit(solution)/shard_map/ppermute | solution.py:93
  22.8 1.3 %collective-permute-start.8 = (bf16[128,128]{1,0:T(8,128)(2,1)S(1)}, bf16[128,128]{1,0:T(8,128)(2,1)S(1)}, u32[]{:S(2)}, u32[]{:S(2)}) collective-permute-start(bf16[128,128]{1,0:T(8,128)(2,1)S(1)} %get-tuple-element.39.m0), channel_id=1, source_target_pairs={{0,1},{1,0},{2,3},{3,2},{4,5},{5,4},{6,7},{7,6},{8,9},{9,8},{10,11... | collective-permute-start | bytes 98312 | tf_op jit(solution)/shard_map/ppermute | solution.py:93
  22.8 1.4 %collective-permute-start.9 = (bf16[128,128]{1,0:T(8,128)(2,1)S(1)}, bf16[128,128]{1,0:T(8,128)(2,1)S(1)}, u32[]{:S(2)}, u32[]{:S(2)}) collective-permute-start(bf16[128,128]{1,0:T(8,128)(2,1)S(1)} %get-tuple-element.40.m1), channel_id=1, source_target_pairs={{0,1},{1,0},{2,3},{3,2},{4,5},{5,4},{6,7},{7,6},{8,9},{9,8},{10,11... | collective-permute-start | bytes 98312 | tf_op jit(solution)/shard_map/ppermute | solution.py:93
  24.3 4.6 %collective-permute-start.10 = (bf16[64,128]{1,0:T(8,128)(2,1)S(1)}, bf16[64,128]{1,0:T(8,128)(2,1)S(1)}, u32[]{:S(2)}, u32[]{:S(2)}) collective-permute-start(bf16[64,128]{1,0:T(8,128)(2,1)S(1)} %get-tuple-element.41.own), channel_id=1, source_target_pairs={{0,16},{1,17},{2,18},{3,19},{4,20},{5,21},{6,22},{7,23},{8,24},{9,... | collective-permute-start | bytes 49160 | tf_op jit(solution)/shard_map/ppermute | solution.py:93

commit v9 on v8

--- a/solution.py
+++ b/solution.py
@@ -10,7 +10,7 @@
 BF = jnp.bfloat16
 F32 = jnp.float32
 LEVELS = (4, 3, 2, 1)
-LATE = (("p", 2), ("p", 1), ("g", 4, 2), ("g", 4, 1))
+LATE = (("p", 2), ("p", 1), ("g", 4, 2), ("g", 4, 1), ("c", 1))
 SHARES = ((4, 3, 1), (2,))
 VMEM = pl.BlockSpec(memory_space=pltpu.VMEM)
 HBM = pl.BlockSpec(memory_space=pltpu.HBM)
@@ -230,9 +230,8 @@
         a, z = both(("p", 3))
         lo, hi = plan.near[0][0][("p", 3)]
         near[lo:hi] = (a.astype(F32) + z.astype(F32) - change).astype(BF)
-        for key, out, then in ((("c", 3), near, plan.near[0][0]), (("c", 1), far, plan.far[0][0])):
-            lo, hi = then[key]
-            out[lo:hi] = interleave(*ordered(*both(key), upper))
+        lo, hi = plan.near[0][0][("c", 3)]
+        near[lo:hi] = interleave(*ordered(*both(("c", 3)), upper))
 
     def second():
         spans = plan.child[1][0]
@@ -276,6 +275,7 @@
         for i, k in enumerate(below):
             a, z = both(("p", k))
             put(("p", k), (a.astype(F32) + z.astype(F32) - change[:, i * rank : (i + 1) * rank]).astype(BF))
+        put(("c", 1), interleave(*ordered(*both(("c", 1)), index_bit(bits - 4) == 1)))
 
     pl.when(index_bit(0) == 0)(first)
 

time: 30.2 us -> 30.1 us (level)
  no operation moved by 1% of the time
where the time goes in v9:
time: 30.1 us; the launch traced here: 29.9 us
  starting transfers between devices  12.8 us (43%)
  waiting for transfers between devices  9.15 us (30%)
  Pallas kernels  7.89 us (26%)
    ppermute x11, starting transfers between devices, swap(): lax.ppermute(x, 'pts', [(i, i ^ 1 << (odd if i & 1 else even)) for i in r...  12.8 us
    ppermute x11, waiting for transfers between devices, swap(): lax.ppermute(x, 'pts', [(i, i ^ 1 << (odd if i & 1 else even)) for i in r...  9.15 us
    pallas_call x1, Pallas kernels, on_device(): pl.pallas_call(lambda *refs: first_kernel([t for t, _ in device], rank, w...  2.98 us
    pallas_call x11, Pallas kernels, vmem_call(): pl.pallas_call(kernel, out_shape=shapes, in_specs=[VMEM] * len(operands),...  2.16 us
    pallas_call x1, Pallas kernels, on_device(): pl.pallas_call(fetch_kernel, out_shape=[wide] + [base] * 4, in_specs=[VME...  1.71 us
    pallas_call x1, Pallas kernels, on_device(): pl.pallas_call(functools.partial(last_kernel, bits, chunks), out_shape=wi...  1.03 us
  transfers between devices with their start and end apart: 11, of which 7 were waited for; matrix products, arithmetic and copies ran while one was open for 0% of the time, Pallas kernels for 12%

profile of v9, /device:TPU:0, one launch (start us, length us, event | category | flops | bytes accessed | tf_op | source)
XLA Modules:
  0.0 29.9 jit_solution(9521765956701309394)
XLA Ops:
  0.0 3.0 %products.1 = (bf16[848,128]{1,0:T(8,128)(2,1)S(1)}, bf16[848,128]{1,0:T(8,128)(2,1)S(1)}) custom-call(f32[64,2048]{1,0:T(8,128)} %refs_0_.3, bf16[128,2048]{1,0:T(8,128)(2,1)} %refs_1_.2, bf16[128,2048]{1,0:T(8,128)(2,1)} %refs_2_.2, bf16[128,2048]{1,0:T(8,128)(2,1)} %refs_1_.3, bf16[128,2048]{1,0:T(8,128)(2,1)} %refs_2_.3, bf16[128,2048]{1,0:T(8,128)(2,1)} %refs_3_.3, ...), custom_call_target="tpu_custom_call" | custom-call | tf_op jit(solution)/shard_map/products/pallas_call | solution.py:483
  3.0 0.5 %collective-permute-start = (bf16[848,128]{1,0:T(8,128)(2,1)S(1)}, bf16[848,128]{1,0:T(8,128)(2,1)S(1)}, u32[]{:S(2)}, u32[]{:S(2)}) collective-permute-start(bf16[848,128]{1,0:T(8,128)(2,1)S(1)} %get-tuple-element.28), channel_id=1, source_target_pairs={{0,1},{1,0},{2,3},{3,2},{4,5},{5,4},{6,7},{7,6},{8,9},{9,8},{10,11... | collective-permute-start | bytes 651272 | tf_op jit(solution)/shard_map/ppermute | solution.py:93
  3.5 1.1 %collective-permute-done.got = bf16[848,128]{1,0:T(8,128)(2,1)S(1)} collective-permute-done((bf16[848,128]{1,0:T(8,128)(2,1)S(1)}, bf16[848,128]{1,0:T(8,128)(2,1)S(1)}, u32[]{:S(2)}, u32[]{:S(2)}) %collective-permute-start) | collective-permute-done | bytes 217120 | tf_op jit(solution)/shard_map/ppermute | solution.py:93
  4.7 2.9 %collective-permute-start.1 = (bf16[640,128]{1,0:T(8,128)(2,1)S(1)}, bf16[640,128]{1,0:T(8,128)(2,1)S(1)}, u32[]{:S(2)}, u32[]{:S(2)}) collective-permute-start(bf16[640,128]{1,0:T(8,128)(2,1)S(1)} %get-tuple-element.29.after.own), channel_id=1, source_target_pairs={{0,2},{1,5},{2,0},{3,7},{4,6},{5,1},{6,4},{7,3},{8,10},{9,13},{10,... | collective-permute-start | bytes 491528 | tf_op jit(solution)/shard_map/ppermute | solution.py:93
  7.6 0.1 collective-permute-start.3
  7.7 1.7 %fetch.1 = (f32[64,2048]{1,0:T(8,128)S(1)}, bf16[128,2048]{1,0:T(8,128)(2,1)S(1)}, bf16[128,2048]{1,0:T(8,128)(2,1)S(1)}, bf16[128,2048]{1,0:T(8,128)(2,1)S(1)}, bf16[128,2048]{1,0:T(8,128)(2,1)S(1)}) custom-call(bf16[640,128]{1,0:T(8,128)(2,1)S(1)} %get-tuple-element.29.after.own, f32[64,2048]{1,0:T(8,128)} %refs_0_.3, bf16[128,2048]{1,0:T(8,128)(2,1)} %refs_1_.3, ...), custom_call_target="tpu_custom_call" | custom-call | bytes 2621440 | tf_op jit(solution)/shard_map/fetch/pallas_call | solution.py:536
  9.4 1.5 %collective-permute-done.1.got = bf16[640,128]{1,0:T(8,128)(2,1)S(1)} collective-permute-done((bf16[640,128]{1,0:T(8,128)(2,1)S(1)}, bf16[640,128]{1,0:T(8,128)(2,1)S(1)}, u32[]{:S(2)}, u32[]{:S(2)}) %collective-permute-start.1) | collective-permute-done | bytes 163872 | tf_op jit(solution)/shard_map/ppermute | solution.py:93
  10.9 0.3 %level_4.1 = (bf16[512,128]{1,0:T(8,128)(2,1)S(1)}, bf16[256,128]{1,0:T(8,128)(2,1)S(1)}, bf16[64,256]{1,0:T(8,128)(2,1)S(1)}) custom-call(bf16[640,128]{1,0:T(8,128)(2,1)S(1)} %get-tuple-element.29.after.own, bf16[640,128]{1,0:T(8,128)(2,1)S(1)} %collective-permute-done.1.got, bf16[128,2048]{1,0:T(8,128)(2,1)S(1)} %get-tuple-element.30.after.s1), custom_call_target="tpu_custom_call" | custom-call | tf_op jit(solution)/shard_map/level_4/pallas_call | solution.py:457
  11.2 2.1 %collective-permute-start.2 = (bf16[512,128]{1,0:T(8,128)(2,1)S(1)}, bf16[512,128]{1,0:T(8,128)(2,1)S(1)}, u32[]{:S(2)}, u32[]{:S(2)}) collective-permute-start(bf16[512,128]{1,0:T(8,128)(2,1)S(1)} %get-tuple-element.31.own_n), channel_id=1, source_target_pairs={{0,4},{1,3},{2,6},{3,1},{4,0},{5,7},{6,2},{7,5},{8,12},{9,11},{10,... | collective-permute-start | bytes 393224 | tf_op jit(solution)/shard_map/ppermute | solution.py:93
  13.3 0.0 collective-permute-done.3.got
  13.3 0.1 place.1.own_f
  13.5 0.8 %collective-permute-start.4 = (bf16[256,128]{1,0:T(8,128)(2,1)S(1)}, bf16[256,128]{1,0:T(8,128)(2,1)S(1)}, u32[]{:S(2)}, u32[]{:S(2)}) collective-permute-start(bf16[256,128]{1,0:T(8,128)(2,1)S(1)} %place.1.own_f), channel_id=1, source_target_pairs={{0,4},{1,3},{2,6},{3,1},{4,0},{5,7},{6,2},{7,5},{8,12},{9,11},{10,... | collective-permute-start | bytes 196616 | tf_op jit(solution)/shard_map/ppermute | solution.py:93
  14.3 3.5 %collective-permute-done.4.got_f = bf16[256,128]{1,0:T(8,128)(2,1)S(1)} collective-permute-done((bf16[256,128]{1,0:T(8,128)(2,1)S(1)}, bf16[256,128]{1,0:T(8,128)(2,1)S(1)}, u32[]{:S(2)}, u32[]{:S(2)}) %collective-permute-start.4) | collective-permute-done | bytes 65568 | tf_op jit(solution)/shard_map/ppermute | solution.py:93
  17.8 0.0 collective-permute-done.2.got_n
  17.8 0.1 collective-permute-start.5
  17.9 1.6 %collective-permute-start.7 = (bf16[256,128]{1,0:T(8,128)(2,1)S(1)}, bf16[256,128]{1,0:T(8,128)(2,1)S(1)}, u32[]{:S(2)}, u32[]{:S(2)}) collective-permute-start(bf16[256,128]{1,0:T(8,128)(2,1)S(1)} %early_z.1.after.own), channel_id=1, source_target_pairs={{0,8},{1,9},{2,10},{3,11},{4,12},{5,13},{6,14},{7,15},{8,0},{9,1},... | collective-permute-start | bytes 196616 | tf_op jit(solution)/shard_map/ppermute | solution.py:93
  19.6 0.0 collective-permute-done.5.got
  19.6 0.3 %level_3.1 = (bf16[144,128]{1,0:T(8,128)(2,1)S(1)}, bf16[64,128]{1,0:T(8,128)(2,1)S(1)}, bf16[64,128]{1,0:T(8,128)(2,1)S(1)}, bf16[256,128]{1,0:T(8,128)(2,1)S(1)}) custom-call(bf16[960,128]{1,0:T(8,128)(2,1)S(1)} %get-tuple-element.35.own, bf16[960,128]{1,0:T(8,128)(2,1)S(1)} %collective-permute-done.5.got, bf16[256,128]{1,0:T(8,128)(2,1)S(1)} %early_z.1.after.own), custom_call_target="tpu_custom_call" | custom-call | tf_op jit(solution)/shard_map/level_3/pallas_call | solution.py:457
  19.9 1.5 %collective-permute-start.6 = (bf16[144,128]{1,0:T(8,128)(2,1)S(1)}, bf16[144,128]{1,0:T(8,128)(2,1)S(1)}, u32[]{:S(2)}, u32[]{:S(2)}) collective-permute-start(bf16[144,128]{1,0:T(8,128)(2,1)S(1)} %get-tuple-element.37.own), channel_id=1, source_target_pairs={{0,8},{1,9},{2,10},{3,11},{4,12},{5,13},{6,14},{7,15},{8,0},{9,1},... | collective-permute-start | bytes 110600 | tf_op jit(solution)/shard_map/ppermute | solution.py:93
  21.4 1.3 %collective-permute-done.7.got = bf16[256,128]{1,0:T(8,128)(2,1)S(1)} collective-permute-done((bf16[256,128]{1,0:T(8,128)(2,1)S(1)}, bf16[256,128]{1,0:T(8,128)(2,1)S(1)}, u32[]{:S(2)}, u32[]{:S(2)}) %collective-permute-start.7) | collective-permute-done | bytes 65568 | tf_op jit(solution)/shard_map/ppermute | solution.py:93
  22.7 0.1 collective-permute-start.8
  22.7 0.5 %collective-permute-start.9 = (bf16[128,128]{1,0:T(8,128)(2,1)S(1)}, bf16[128,128]{1,0:T(8,128)(2,1)S(1)}, u32[]{:S(2)}, u32[]{:S(2)}) collective-permute-start(bf16[128,128]{1,0:T(8,128)(2,1)S(1)} %get-tuple-element.40.m1), channel_id=1, source_target_pairs={{0,1},{1,0},{2,3},{3,2},{4,5},{5,4},{6,7},{7,6},{8,9},{9,8},{10,11... | collective-permute-start | bytes 98312 | tf_op jit(solution)/shard_map/ppermute | solution.py:93
  23.2 0.7 %collective-permute-done.8.o0 = bf16[128,128]{1,0:T(8,128)(2,1)S(1)} collective-permute-done((bf16[128,128]{1,0:T(8,128)(2,1)S(1)}, bf16[128,128]{1,0:T(8,128)(2,1)S(1)}, u32[]{:S(2)}, u32[]{:S(2)}) %collective-permute-start.8) | collective-permute-done | bytes 32800 | tf_op jit(solution)/shard_map/ppermute | solution.py:93
  23.9 0.2 collective-permute-done.9.o1
  24.1 0.0 collective-permute-done.6.got
  24.1 0.1 level_2.1
  24.2 2.6 %collective-permute-start.10 = (bf16[64,128]{1,0:T(8,128)(2,1)S(1)}, bf16[64,128]{1,0:T(8,128)(2,1)S(1)}, u32[]{:S(2)}, u32[]{:S(2)}) collective-permute-start(bf16[64,128]{1,0:T(8,128)(2,1)S(1)} %get-tuple-element.41.own), channel_id=1, source_target_pairs={{0,16},{1,17},{2,18},{3,19},{4,20},{5,21},{6,22},{7,23},{8,24},{9,... | collective-permute-start | bytes 49160 | tf_op jit(solution)/shard_map/ppermute | solution.py:93
  26.8 0.3 early.1.rest
  27.1 0.5 %basis_1.1.basis = bf16[256,2048]{1,0:T(8,128)(2,1)S(1)} custom-call(bf16[128,128]{1,0:T(8,128)(2,1)S(1)} %get-tuple-element.39.m0, bf16[128,128]{1,0:T(8,128)(2,1)S(1)} %get-tuple-element.40.m1, bf16[128,128]{1,0:T(8,128)(2,1)S(1)} %collective-permute-done.8.o0, bf16[128,128]{1,0:T(8,128)(2,1)S(1)} %collective-permute-done.9.o1, ...), custom_call_target="tpu_custom_call" | custom-call | flops 134217728 | bytes 1572864 | tf_op jit(solution)/shard_map/basis_1/pallas_call | solution.py:457
  27.6 0.4 %middle.1.rest = f32[64,2048]{1,0:T(8,128)S(1)} custom-call(f32[64,2048]{1,0:T(8,128)S(1)} %early.1.rest, bf16[128,2048]{1,0:T(8,128)(2,1)S(1)} %get-tuple-element.46.s2, bf16[64,256]{1,0:T(8,128)(2,1)S(1)} %get-tuple-element.47.stacked, bf16[256,128]{1,0:T(8,128)(2,1)S(1)} %get-tuple-element.48.rows), custom_call_target="tpu_custom_call" | custom-call | flops 33554432 | bytes 1048576 | tf_op jit(solution)/shard_map/middle/pallas_call | solution.py:457
  28.0 0.9 %collective-permute-done.10.got = bf16[64,128]{1,0:T(8,128)(2,1)S(1)} collective-permute-done((bf16[64,128]{1,0:T(8,128)(2,1)S(1)}, bf16[64,128]{1,0:T(8,128)(2,1)S(1)}, u32[]{:S(2)}, u32[]{:S(2)}) %collective-permute-start.10) | collective-permute-done | bytes 16416 | tf_op jit(solution)/shard_map/ppermute | solution.py:93
  28.9 1.0 %last.1 = f32[64,2048]{1,0:T(8,128)} custom-call(bf16[64,128]{1,0:T(8,128)(2,1)S(1)} %get-tuple-element.41.own, bf16[64,128]{1,0:T(8,128)(2,1)S(1)} %collective-permute-done.10.got, f32[64,2048]{1,0:T(8,128)S(1)} %middle.1.rest, bf16[256,2048]{1,0:T(8,128)(2,1)S(1)} %basis_1.1.basis), custom_call_target="tpu_custom_call" | custom-call | tf_op jit(solution)/shard_map/last/pallas_call | solution.py:576
  (4 shorter events, 0.1 us)
Async XLA Ops:
  3.0 1.6 %collective-permute-start = (bf16[848,128]{1,0:T(8,128)(2,1)S(1)}, bf16[848,128]{1,0:T(8,128)(2,1)S(1)}, u32[]{:S(2)}, u32[]{:S(2)}) collective-permute-start(bf16[848,128]{1,0:T(8,128)(2,1)S(1)} %get-tuple-element.28), channel_id=1, source_target_pairs={{0,1},{1,0},{2,3},{3,2},{4,5},{5,4},{6,7},{7,6},{8,9},{9,8},{10,11... | collective-permute-start | bytes 651272 | tf_op jit(solution)/shard_map/ppermute | solution.py:93
  4.7 6.2 %collective-permute-start.1 = (bf16[640,128]{1,0:T(8,128)(2,1)S(1)}, bf16[640,128]{1,0:T(8,128)(2,1)S(1)}, u32[]{:S(2)}, u32[]{:S(2)}) collective-permute-start(bf16[640,128]{1,0:T(8,128)(2,1)S(1)} %get-tuple-element.29.after.own), channel_id=1, source_target_pairs={{0,2},{1,5},{2,0},{3,7},{4,6},{5,1},{6,4},{7,3},{8,10},{9,13},{10,... | collective-permute-start | bytes 491528 | tf_op jit(solution)/shard_map/ppermute | solution.py:93
  7.6 5.7 %collective-permute-start.3 = (bf16[416,128]{1,0:T(8,128)(2,1)S(1)}, bf16[416,128]{1,0:T(8,128)(2,1)S(1)}, u32[]{:S(2)}, u32[]{:S(2)}) collective-permute-start(bf16[416,128]{1,0:T(8,128)(2,1)S(1)} %get-tuple-element.33.own), channel_id=1, source_target_pairs={{0,2},{1,5},{2,0},{3,7},{4,6},{5,1},{6,4},{7,3},{8,10},{9,13},{10,... | collective-permute-start | bytes 319496 | tf_op jit(solution)/shard_map/ppermute | solution.py:93
  11.2 6.6 %collective-permute-start.2 = (bf16[512,128]{1,0:T(8,128)(2,1)S(1)}, bf16[512,128]{1,0:T(8,128)(2,1)S(1)}, u32[]{:S(2)}, u32[]{:S(2)}) collective-permute-start(bf16[512,128]{1,0:T(8,128)(2,1)S(1)} %get-tuple-element.31.own_n), channel_id=1, source_target_pairs={{0,4},{1,3},{2,6},{3,1},{4,0},{5,7},{6,2},{7,5},{8,12},{9,11},{10,... | collective-permute-start | bytes 393224 | tf_op jit(solution)/shard_map/ppermute | solution.py:93
  13.5 4.3 %collective-permute-start.4 = (bf16[256,128]{1,0:T(8,128)(2,1)S(1)}, bf16[256,128]{1,0:T(8,128)(2,1)S(1)}, u32[]{:S(2)}, u32[]{:S(2)}) collective-permute-start(bf16[256,128]{1,0:T(8,128)(2,1)S(1)} %place.1.own_f), channel_id=1, source_target_pairs={{0,4},{1,3},{2,6},{3,1},{4,0},{5,7},{6,2},{7,5},{8,12},{9,11},{10,... | collective-permute-start | bytes 196616 | tf_op jit(solution)/shard_map/ppermute | solution.py:93
  17.8 1.8 %collective-permute-start.5 = (bf16[960,128]{1,0:T(8,128)(2,1)S(1)}, bf16[960,128]{1,0:T(8,128)(2,1)S(1)}, u32[]{:S(2)}, u32[]{:S(2)}) collective-permute-start(bf16[960,128]{1,0:T(8,128)(2,1)S(1)} %get-tuple-element.35.own), channel_id=1, source_target_pairs={{0,1},{1,0},{2,3},{3,2},{4,5},{5,4},{6,7},{7,6},{8,9},{9,8},{10,11... | collective-permute-start | bytes 737288 | tf_op jit(solution)/shard_map/ppermute | solution.py:93
  17.9 4.7 %collective-permute-start.7 = (bf16[256,128]{1,0:T(8,128)(2,1)S(1)}, bf16[256,128]{1,0:T(8,128)(2,1)S(1)}, u32[]{:S(2)}, u32[]{:S(2)}) collective-permute-start(bf16[256,128]{1,0:T(8,128)(2,1)S(1)} %early_z.1.after.own), channel_id=1, source_target_pairs={{0,8},{1,9},{2,10},{3,11},{4,12},{5,13},{6,14},{7,15},{8,0},{9,1},... | collective-permute-start | bytes 196616 | tf_op jit(solution)/shard_map/ppermute | solution.py:93
  19.9 4.2 %collective-permute-start.6 = (bf16[144,128]{1,0:T(8,128)(2,1)S(1)}, bf16[144,128]{1,0:T(8,128)(2,1)S(1)}, u32[]{:S(2)}, u32[]{:S(2)}) collective-permute-start(bf16[144,128]{1,0:T(8,128)(2,1)S(1)} %get-tuple-element.37.own), channel_id=1, source_target_pairs={{0,8},{1,9},{2,10},{3,11},{4,12},{5,13},{6,14},{7,15},{8,0},{9,1},... | collective-permute-start | bytes 110600 | tf_op jit(solution)/shard_map/ppermute | solution.py:93
  22.7 1.3 %collective-permute-start.8 = (bf16[128,128]{1,0:T(8,128)(2,1)S(1)}, bf16[128,128]{1,0:T(8,128)(2,1)S(1)}, u32[]{:S(2)}, u32[]{:S(2)}) collective-permute-start(bf16[128,128]{1,0:T(8,128)(2,1)S(1)} %get-tuple-element.39.m0), channel_id=1, source_target_pairs={{0,1},{1,0},{2,3},{3,2},{4,5},{5,4},{6,7},{7,6},{8,9},{9,8},{10,11... | collective-permute-start | bytes 98312 | tf_op jit(solution)/shard_map/ppermute | solution.py:93
  22.7 1.4 %collective-permute-start.9 = (bf16[128,128]{1,0:T(8,128)(2,1)S(1)}, bf16[128,128]{1,0:T(8,128)(2,1)S(1)}, u32[]{:S(2)}, u32[]{:S(2)}) collective-permute-start(bf16[128,128]{1,0:T(8,128)(2,1)S(1)} %get-tuple-element.40.m1), channel_id=1, source_target_pairs={{0,1},{1,0},{2,3},{3,2},{4,5},{5,4},{6,7},{7,6},{8,9},{9,8},{10,11... | collective-permute-start | bytes 98312 | tf_op jit(solution)/shard_map/ppermute | solution.py:93
  24.2 4.6 %collective-permute-start.10 = (bf16[64,128]{1,0:T(8,128)(2,1)S(1)}, bf16[64,128]{1,0:T(8,128)(2,1)S(1)}, u32[]{:S(2)}, u32[]{:S(2)}) collective-permute-start(bf16[64,128]{1,0:T(8,128)(2,1)S(1)} %get-tuple-element.41.own), channel_id=1, source_target_pairs={{0,16},{1,17},{2,18},{3,19},{4,20},{5,21},{6,22},{7,23},{8,24},{9,... | collective-permute-start | bytes 49160 | tf_op jit(solution)/shard_map/ppermute | solution.py:93
